TPU v7x, 32 devices: a whole 2x2x4 slice. The times are simulated.
32 devices in a mesh: gx: 2 (over y), gy: 4 (over x, core), gz: 4 (over z).
Axes of the slice: x: 2, y: 2, z: 4, core: 2. Of those that a mesh axis runs over, the one named last changes fastest.
Arguments:
- initial_warmth: float32 [128, 512, 1024], P('gx', 'gy', 'gz'), may hold values from -6 to 6
- heat_supply: float32 [128, 512, 1024], P('gx', 'gy', 'gz'), may hold values from -82944 to 82946
Outputs:
- updated: float32 [128, 512, 1024], P('gx', 'gy', 'gz')
All inputs are finite; a program needn't handle non-finite values.
Results may differ from a plain program's by a relative error of at most 0.0009.
Values sent between devices are 32-bit elements; how exact they have to be, the bound alone decides.
No kernel may reach another device: no remote copies, remote signals or barrier semaphores. Data moves between devices by JAX's collectives and lax.ppermute only.
A program may use at most 128 MiB of HBM per device.

v0:
```python
import jax
import jax.numpy as jnp
from jax import lax
from jax.sharding import PartitionSpec as P


def padded(cells, sides, width):
    for axis, dim in sides:
        count = lax.axis_size(axis)
        ends = count - 1
        head = lax.slice_in_dim(cells, 0, width, axis=dim)
        tail = lax.slice_in_dim(cells, cells.shape[dim] - width, cells.shape[dim], axis=dim)
        cells = jnp.concatenate(
            [
                lax.ppermute(tail, axis, [(i, (i + 1) % count) for i in range(ends)]),
                cells,
                lax.ppermute(head, axis, [((i + 1) % count, i) for i in range(ends)]),
            ],
            axis=dim,
        )
    return cells


def spike_tables(length, factor):
    identity_matrix = jnp.eye(length, dtype=jnp.float32)
    diagonal = jnp.full((length,), 1.0 + factor, jnp.float32)
    sideband = jnp.full((length,), -0.5 * factor, jnp.float32)
    lower_band = sideband.at[0].set(0.0)
    upper_band = sideband.at[length - 1].set(0.0)
    inverse = lax.linalg.tridiagonal_solve(lower_band, diagonal, upper_band, identity_matrix)
    right_spike = inverse[:, length - 1] * (-0.5 * factor)
    left_spike = inverse[:, 0] * (-0.5 * factor)
    return (inverse, right_spike, left_spike)


def chain_tables(right_spike, left_spike, members):
    right_head = right_spike[0]
    right_tail = right_spike[-1]
    left_head = left_spike[0]
    left_tail = left_spike[-1]
    gamma_now = jnp.zeros((), jnp.float32)
    denoms = []
    priors = []
    for member in range(members):
        denominator = 1.0 - left_head * gamma_now
        priors.append(gamma_now)
        denoms.append(denominator)
        gamma_now = right_tail + left_tail * gamma_now * right_head / denominator
    denoms = jnp.stack(denoms)
    priors = jnp.stack(priors)
    slopes = -left_tail / denoms
    thetas = right_head / denoms
    return (denoms, priors, slopes, thetas, left_head, left_tail)


def pick_own(table, selector):
    return jnp.sum(table * selector)


def finish_pair(beta_own, tau_own, following, prior_own, theta_own):
    preceding = beta_own - prior_own * (tau_own - theta_own * following)
    return (preceding, following)


def reduced_rows(chain_data, selector, members):
    denoms, priors, slopes, thetas, left_head, left_tail = chain_data
    basis = jnp.reshape(jnp.eye(2 * members, dtype=jnp.float32), (members, 2, 2 * members))
    incoming = jnp.zeros((2 * members,), jnp.float32)
    before_list = []
    for member in range(members):
        before_list.append(incoming)
        carry_term = (
            basis[member, 1] + left_tail * priors[member] * basis[member, 0] / denoms[member]
        )
        incoming = slopes[member] * incoming + carry_term
    tau_list = [
        (basis[member, 0] - left_head * before_list[member]) / denoms[member]
        for member in range(members)
    ]
    outgoing = jnp.zeros((2 * members,), jnp.float32)
    after_list = [outgoing] * members
    for member in reversed(range(members)):
        after_list[member] = outgoing
        outgoing = tau_list[member] - thetas[member] * outgoing
    beta_own = sum((selector[member] * before_list[member] for member in range(members)))
    tau_own = sum((selector[member] * tau_list[member] for member in range(members)))
    following = sum((selector[member] * after_list[member] for member in range(members)))
    return finish_pair(
        beta_own, tau_own, following, pick_own(priors, selector), pick_own(thetas, selector)
    )


def settle_gathered(gathered, chain_data, selector):
    members = gathered.shape[0]
    row_before, row_after = reduced_rows(chain_data, selector, members)
    flat_ends = jnp.reshape(gathered, (2 * members, -1))
    both_rows = jnp.stack([row_before, row_after])
    applied = jnp.dot(
        both_rows, flat_ends, precision=lax.Precision.HIGHEST, preferred_element_type=jnp.float32
    )
    shape_out = gathered.shape[2:]
    return (jnp.reshape(applied[0], shape_out), jnp.reshape(applied[1], shape_out))


def sweep_axis(values, tables, dimension, settle):
    inverse, right_spike, left_spike = tables
    if dimension == 0:
        partial_value = jnp.einsum(
            "ik,kbc->ibc",
            inverse,
            values,
            precision=lax.Precision.HIGHEST,
            preferred_element_type=jnp.float32,
        )
        endpoints = jnp.stack([partial_value[0], partial_value[-1]])
        preceding, following = settle(endpoints)
        return (
            partial_value
            - right_spike[:, None, None] * following[None]
            - left_spike[:, None, None] * preceding[None]
        )
    if dimension == 1:
        partial_value = jnp.einsum(
            "jk,akc->ajc",
            inverse,
            values,
            precision=lax.Precision.HIGHEST,
            preferred_element_type=jnp.float32,
        )
        endpoints = jnp.stack([partial_value[:, 0, :], partial_value[:, -1, :]])
        preceding, following = settle(endpoints)
        return (
            partial_value
            - right_spike[None, :, None] * following[:, None, :]
            - left_spike[None, :, None] * preceding[:, None, :]
        )
    partial_value = jnp.einsum(
        "abk,jk->abj",
        values,
        inverse,
        precision=lax.Precision.HIGHEST,
        preferred_element_type=jnp.float32,
    )
    endpoints = jnp.stack([partial_value[:, :, 0], partial_value[:, :, -1]])
    preceding, following = settle(endpoints)
    return (
        partial_value
        - right_spike[None, None, :] * following[:, :, None]
        - left_spike[None, None, :] * preceding[:, :, None]
    )


def selector_for(members, position):
    return (jnp.arange(members) == position).astype(jnp.float32)


def local(initial_warmth, heat_supply):
    extent_east, extent_north, extent_upward = initial_warmth.shape
    members_first = lax.axis_size("gx")
    members_second = lax.axis_size("gy")
    members_third = lax.axis_size("gz")
    whole_east = extent_east * members_first
    whole_north = extent_north * members_second
    whole_upward = extent_upward * members_third
    leading_factor = float(whole_east * whole_east // 4)
    factor_second = float(whole_north * whole_north // 4)
    factor_third = float(whole_upward * whole_upward // 4)
    bordered_grid = padded(initial_warmth, (("gx", 0), ("gy", 1), ("gz", 2)), 1)
    forward_increment = leading_factor * (
        bordered_grid[2:, 1:-1, 1:-1] - 2.0 * initial_warmth + bordered_grid[:-2, 1:-1, 1:-1]
    )
    forward_increment = forward_increment + factor_second * (
        bordered_grid[1:-1, 2:, 1:-1] - 2.0 * initial_warmth + bordered_grid[1:-1, :-2, 1:-1]
    )
    forward_increment = forward_increment + factor_third * (
        bordered_grid[1:-1, 1:-1, 2:] - 2.0 * initial_warmth + bordered_grid[1:-1, 1:-1, :-2]
    )
    forward_increment = forward_increment + heat_supply
    select_first = selector_for(members_first, lax.axis_index("gx"))
    select_second = selector_for(members_second, lax.axis_index("gy"))
    select_third = selector_for(members_third, lax.axis_index("gz"))
    tables_first = spike_tables(extent_east, leading_factor)
    tables_second = spike_tables(extent_north, factor_second)
    tables_third = spike_tables(extent_upward, factor_third)
    chain_first = chain_tables(tables_first[1], tables_first[2], members_first)
    chain_second = chain_tables(tables_second[1], tables_second[2], members_second)
    chain_third = chain_tables(tables_third[1], tables_third[2], members_third)

    def settle_first(endpoints):
        return settle_gathered(
            lax.all_gather(endpoints[None], "gx", axis=0, tiled=True), chain_first, select_first
        )

    def settle_second(endpoints):
        return settle_gathered(
            lax.all_gather(endpoints[None], "gy", axis=0, tiled=True), chain_second, select_second
        )

    def settle_third(endpoints):
        return settle_gathered(
            lax.all_gather(endpoints[None], "gz", axis=0, tiled=True), chain_third, select_third
        )

    section_one = sweep_axis(forward_increment, tables_first, 0, settle_first)
    section_two = sweep_axis(section_one, tables_second, 1, settle_second)
    upward_portion = sweep_axis(section_two, tables_third, 2, settle_third)
    return initial_warmth + upward_portion


def solution(mesh):
    return jax.shard_map(
        local,
        mesh=mesh,
        in_specs=(P("gx", "gy", "gz"), P("gx", "gy", "gz")),
        out_specs=P("gx", "gy", "gz"),
        check_vma=False,
    )
```

profile of v0, /device:TPU:0, one launch (start us, length us, event | category | flops | bytes accessed | tf_op | source)
XLA Modules:
  0.0 540.7 jit_solution(1028930175370737629)
XLA Ops:
  0.0 1.0 fusion.600
  1.0 1.3 collective-permute-start
  2.3 4.9 collective-permute-start.1
  7.3 5.8 %while.86 = (s32[]{:T(128)}, f32[]{:T(128)}, f32[128]{0:T(128)S(1)}, f32[3,32]{1,0:T(4,128)S(1)}, f32[3,32,128]{2,1,0:T(8,128)S(1)}, /*index=5*/f32[3,32,128]{2,...) while((s32[]{:T(128)}, f32[]{:T(128)}, ...), condition=%wide.region_3.4_spmd, body=%wide.region_2.3_spmd.sunk | while | flops 12417 | bytes 102505 | solution.py:30
  16.5 65.3 %while.87 = (s32[]{:T(128)}, f32[128]{0:T(128)S(1)}, f32[3,32,128]{2,1,0:T(8,128)S(1)}, f32[3,32,128]{2,1,0:T(8,128)S(1)}, f32[3,32]{1,0:T(4,128)S(1)}, /*index=...) while((s32[]{:T(128)}, f32[128]{0:T(128)S(1)}, ...), condition=%wide.region_5.6_spmd, body=%wide.region_4.5_spmd.sunk | while | flops 8226 | bytes 101341 | solution.py:30
  17.9 20.2 %fusion.634 = (f32[128]{0:T(128)S(1)}, f32[128]{0:T(128)S(1)}, f32[128]{0:T(128)S(1)}, f32[128]{0:T(128)S(1)}, f32[128]{0:T(128)S(1)}, /*index=5*/f32[128]{0:T(1...) fusion(f32[3,32,128]{2,1,0:T(8,128)S(1)} %get-tuple-element.208, ...), kind=kLoop, calls=%fused_computation.166.clone.1 | loop fusion | flops 8192 | bytes 33536 | tf_op jit(solution)/shard_map/while/body/eval_jaxpr/sub | solution.py:30
  39.7 20.2 %fusion.634 = (f32[128]{0:T(128)S(1)}, f32[128]{0:T(128)S(1)}, f32[128]{0:T(128)S(1)}, f32[128]{0:T(128)S(1)}, f32[128]{0:T(128)S(1)}, /*index=5*/f32[128]{0:T(1...) fusion(f32[3,32,128]{2,1,0:T(8,128)S(1)} %get-tuple-element.208, ...), kind=kLoop, calls=%fused_computation.166.clone.1 | loop fusion | flops 8192 | bytes 33536 | tf_op jit(solution)/shard_map/while/body/eval_jaxpr/sub | solution.py:30
  61.5 20.2 %fusion.634 = (f32[128]{0:T(128)S(1)}, f32[128]{0:T(128)S(1)}, f32[128]{0:T(128)S(1)}, f32[128]{0:T(128)S(1)}, f32[128]{0:T(128)S(1)}, /*index=5*/f32[128]{0:T(1...) fusion(f32[3,32,128]{2,1,0:T(8,128)S(1)} %get-tuple-element.208, ...), kind=kLoop, calls=%fused_computation.166.clone.1 | loop fusion | flops 8192 | bytes 33536 | tf_op jit(solution)/shard_map/while/body/eval_jaxpr/sub | solution.py:30
  81.8 1.3 fusion.454
  83.1 2.7 fusion.453
  85.8 2.6 fusion.452
  88.4 2.7 fusion.451
  91.1 2.7 fusion.450
  93.8 2.6 fusion.449
  96.4 2.7 fusion.448
  99.1 2.6 fusion.447
  101.7 2.6 fusion.446
  104.4 2.6 fusion.445
  107.0 2.7 fusion.444
  109.7 2.6 fusion.443
  112.3 2.7 fusion.442
  115.0 2.7 fusion.441
  117.6 2.7 fusion.440
  120.3 2.0 fusion.324
  130.8 14.9 %while.88 = (s32[]{:T(128)}, f32[]{:T(128)}, f32[256]{0:T(256)S(1)}, f32[7,32]{1,0:T(8,128)S(1)}, f32[7,32,256]{2,1,0:T(8,128)S(1)}, /*index=5*/f32[7,32,256]{2,...) while((s32[]{:T(128)}, f32[]{:T(128)}, ...), condition=%wide.region_9.10_spmd, body=%wide.region_8.9_spmd.sunk | while | flops 24705 | bytes 267885 | solution.py:30
  149.2 152.3 %while.89 = (s32[]{:T(128)}, f32[256]{0:T(256)S(1)}, f32[7,32,256]{2,1,0:T(8,128)S(1)}, f32[7,32,256]{2,1,0:T(8,128)S(1)}, f32[7,32]{1,0:T(8,128)S(1)}, /*index=...) while((s32[]{:T(128)}, f32[256]{0:T(256)S(1)}, ...), condition=%wide.region_11.12_spmd, body=%wide.region_10.11_spmd.sunk | while | flops 16418 | bytes 266721 | solution.py:30
  150.9 19.9 %multiply_subtract_fusion.240 = (f32[256]{0:T(256)S(1)}, f32[256]{0:T(256)S(1)}, f32[256]{0:T(256)S(1)}, f32[256]{0:T(256)S(1)}, f32[256]{0:T(256)S(1)}, /*index...) fusion(f32[256]{0:T(256)S(1)} %bitcast.3041, ...), kind=kLoop, calls=%fused_computation.326.clone.1 | loop fusion | flops 16384 | bytes 66688 | tf_op jit(solution)/shard_map/while/body/eval_jaxpr/sub | solution.py:30
  172.6 19.9 %multiply_subtract_fusion.240 = (f32[256]{0:T(256)S(1)}, f32[256]{0:T(256)S(1)}, f32[256]{0:T(256)S(1)}, f32[256]{0:T(256)S(1)}, f32[256]{0:T(256)S(1)}, /*index...) fusion(f32[256]{0:T(256)S(1)} %bitcast.3041, ...), kind=kLoop, calls=%fused_computation.326.clone.1 | loop fusion | flops 16384 | bytes 66688 | tf_op jit(solution)/shard_map/while/body/eval_jaxpr/sub | solution.py:30
  194.3 19.9 %multiply_subtract_fusion.240 = (f32[256]{0:T(256)S(1)}, f32[256]{0:T(256)S(1)}, f32[256]{0:T(256)S(1)}, f32[256]{0:T(256)S(1)}, f32[256]{0:T(256)S(1)}, /*index...) fusion(f32[256]{0:T(256)S(1)} %bitcast.3041, ...), kind=kLoop, calls=%fused_computation.326.clone.1 | loop fusion | flops 16384 | bytes 66688 | tf_op jit(solution)/shard_map/while/body/eval_jaxpr/sub | solution.py:30
  216.1 19.9 %multiply_subtract_fusion.240 = (f32[256]{0:T(256)S(1)}, f32[256]{0:T(256)S(1)}, f32[256]{0:T(256)S(1)}, f32[256]{0:T(256)S(1)}, f32[256]{0:T(256)S(1)}, /*index...) fusion(f32[256]{0:T(256)S(1)} %bitcast.3041, ...), kind=kLoop, calls=%fused_computation.326.clone.1 | loop fusion | flops 16384 | bytes 66688 | tf_op jit(solution)/shard_map/while/body/eval_jaxpr/sub | solution.py:30
  237.8 19.9 %multiply_subtract_fusion.240 = (f32[256]{0:T(256)S(1)}, f32[256]{0:T(256)S(1)}, f32[256]{0:T(256)S(1)}, f32[256]{0:T(256)S(1)}, f32[256]{0:T(256)S(1)}, /*index...) fusion(f32[256]{0:T(256)S(1)} %bitcast.3041, ...), kind=kLoop, calls=%fused_computation.326.clone.1 | loop fusion | flops 16384 | bytes 66688 | tf_op jit(solution)/shard_map/while/body/eval_jaxpr/sub | solution.py:30
  259.5 19.9 %multiply_subtract_fusion.240 = (f32[256]{0:T(256)S(1)}, f32[256]{0:T(256)S(1)}, f32[256]{0:T(256)S(1)}, f32[256]{0:T(256)S(1)}, f32[256]{0:T(256)S(1)}, /*index...) fusion(f32[256]{0:T(256)S(1)} %bitcast.3041, ...), kind=kLoop, calls=%fused_computation.326.clone.1 | loop fusion | flops 16384 | bytes 66688 | tf_op jit(solution)/shard_map/while/body/eval_jaxpr/sub | solution.py:30
  281.2 19.9 %multiply_subtract_fusion.240 = (f32[256]{0:T(256)S(1)}, f32[256]{0:T(256)S(1)}, f32[256]{0:T(256)S(1)}, f32[256]{0:T(256)S(1)}, f32[256]{0:T(256)S(1)}, /*index...) fusion(f32[256]{0:T(256)S(1)} %bitcast.3041, ...), kind=kLoop, calls=%fused_computation.326.clone.1 | loop fusion | flops 16384 | bytes 66688 | tf_op jit(solution)/shard_map/while/body/eval_jaxpr/sub | solution.py:30
  301.5 19.5 %multiply_subtract_fusion.34 = (f32[256]{0:T(256)S(1)}, f32[256]{0:T(256)S(1)}, f32[256]{0:T(256)S(1)}, f32[256]{0:T(256)S(1)}, f32[256]{0:T(256)S(1)}, /*index=...) fusion(f32[256]{0:T(256)S(1)} %bitcast.3252, ...), kind=kLoop, calls=%fused_computation.463 | loop fusion | flops 15872 | bytes 64636 | tf_op jit(solution)/shard_map/eval_jaxpr/sub | solution.py:30
  336.3 1.3 select_reduce_fusion.4
  341.5 1.4 select_reduce_fusion.2
  347.5 1.3 select_reduce_fusion
  352.5 2.5 fusion.345
  355.1 6.8 %bitcast_subtract_fusion.5 = (f32[1,8]{1,0:T(1,128)S(1)}, f32[1,8]{1,0:T(1,128)S(1)}) fusion(f32[]{:T(128)} %bitcast.700, f32[]{:T(128)} %bitcast.698, f32[]{:T(128)S(6)} %mul.24058, f32[]{:T(128)} %bitcast.688, f32[]{:T(128)} %get-tuple-element.747, f32[]{:T(128)S(6)} %mul.24062, f32[]{:T(128)} %bitcast.687, f32[]{:T(128)} %get-tuple-element.1228, ...), kind=kLoop, calls=%fused_computation.737 | loop fusion | flops 424 | bytes 11064 | tf_op jit(solution)/shard_map/sub | solution.py:61
  362.6 8.2 %copy.24 = f32[64,128,256]{2,0,1:T(8,128)S(1)} copy(f32[64,128,256]{2,1,0:T(8,128)} %param.22) | data formatting | bytes 16777216 | tf_op args[0]
  372.3 1.8 copy-done
  374.2 1.3 collective-permute-start.2
  375.5 3.0 collective-permute-start.3
  380.4 4.1 pad_maximum_fusion
  384.5 5.2 fusion.598
  389.7 3.6 copy.34
  393.3 4.6 collective-permute-start.5
  397.9 3.6 copy.32
  401.5 1.3 collective-permute-start.4
  402.8 6.8 %bitcast_subtract_fusion.2 = (f32[1,8]{1,0:T(1,128)S(1)}, f32[1,8]{1,0:T(1,128)S(1)}) fusion(f32[]{:T(128)} %bitcast.921, f32[]{:T(128)} %bitcast.919, f32[]{:T(128)S(6)} %mul.24253, f32[]{:T(128)} %bitcast.909, f32[]{:T(128)} %get-tuple-element.680, f32[]{:T(128)S(6)} %mul.24256, f32[]{:T(128)} %bitcast.908, f32[]{:T(128)} %get-tuple-element.1229, ...), kind=kLoop, calls=%fused_computation.724 | loop fusion | flops 424 | bytes 11064 | tf_op jit(solution)/shard_map/sub | solution.py:61
  409.7 3.7 copy.35
  413.3 3.3 copy.33
  416.6 43.2 %fusion.164 = f32[64,128,256]{2,0,1:T(8,128)} fusion(f32[66,130,1]{2,0,1:T(8,128)} %copy.35, f32[66,1,256]{2,0,1:T(8,128)S(1)} %collective-permute-done.2, f32[66,1,256]{2,0,1:T(8,128)S(1)} %collective-permute-done.3, f32[1,128,256]{2,0,1:T(1,128)S(1)} %copy.25, f32[64,128,256]{2,0,1:T(8,128)} %copy-done, f32[1,128,256]{2,0,1:T(1,128)S(1)} %copy.27, ...), kind=kOutput, calls=%fused_computation.364 | convolution fusion | flops 1675624448 | bytes 25648160 | tf_op jit(solution)/shard_map/ik,kbc->ibc/dot_general | solution.py:108
  459.8 1.7 fusion.599
  461.8 10.2 %all-gather = f32[4,128,256]{2,1,0:T(8,128)S(1)} all-gather(f32[2,128,256]{2,1,0:T(8,128)S(1)} %copy.37), channel_id=2, replica_groups=mesh['gx'=2,'gy'=4,'gz'=4] {'gx'}, dimensions={0}, use_global_device_ids=true | all-gather | bytes 786432 | tf_op jit(solution)/shard_map/all_gather | solution.py:191
  472.3 1.0 fusion.212
  474.1 5.0 multiply_subtract_fusion.33
  479.1 13.3 %fusion.200 = f32[64,128,256]{2,1,0:T(8,128)S(1)} fusion(f32[64,128,256]{2,0,1:T(8,128)S(1)} %multiply_subtract_fusion.33, f32[128,128]{1,0:T(8,128)S(1)} %concatenate.126), kind=kOutput, calls=%fused_computation.417 | convolution fusion | flops 3221225472 | bytes 16842752 | tf_op jit(solution)/shard_map/jk,akc->ajc/dot_general | solution.py:123
  492.4 3.4 copy-done.1
  496.1 6.9 %all-gather.1 = f32[8,64,256]{2,1,0:T(8,128)S(1)} all-gather(f32[2,64,256]{2,1,0:T(8,128)S(1)} %copy.39), channel_id=3, replica_groups=mesh['gx'=2,'gy'=4,'gz'=4] {'gy'}, dimensions={0}, use_global_device_ids=true | all-gather | bytes 655360 | tf_op jit(solution)/shard_map/all_gather | solution.py:196
  504.3 9.6 %fusion.187 = f32[64,128,256]{2,1,0:T(8,128)S(1)} fusion(f32[64,128,256]{2,1,0:T(8,128)} %copy-done.1, f32[64,256]{1,0:T(8,128)S(1)} %mul.24121, f32[128]{0:T(128)S(1)} %get-tuple-element.503, f32[64,256]{1,0:T(8,128)S(1)} %mul.24116, f32[128]{0:T(128)S(1)} %get-tuple-element.502, f32[256,256]{1,0:T(8,128)S(1)} %concatenate.129), kind=kOutput, calls=%fused_computation.401 | convolution fusion | flops 6450839552 | bytes 17171456 | tf_op jit(solution)/shard_map/abk,jk->abj/dot_general | solution.py:137
  513.9 3.3 slice_reduce_fusion.1
  517.3 14.7 %all-gather.2 = f32[8,64,128]{2,1,0:T(8,128)S(1)} all-gather(f32[2,64,128]{2,1,0:T(8,128)S(1)} %pad_maximum_fusion.38), channel_id=4, replica_groups=mesh['gx'=2,'gy'=4,'gz'=4] {'gz'}, dimensions={0}, use_global_device_ids=true | all-gather | bytes 327680 | tf_op jit(solution)/shard_map/all_gather | solution.py:201
  532.5 8.0 %subtract_add_fusion = f32[64,128,256]{2,1,0:T(8,128)} fusion(f32[64,128,256]{2,1,0:T(8,128)} %param.22, f32[64,128,256]{2,1,0:T(8,128)S(1)} %fusion.187, f32[64,128]{1,0:T(8,128)S(1)} %bitcast.2959, f32[256]{0:T(256)S(1)} %get-tuple-element.497, f32[64,128]{1,0:T(8,128)S(1)} %bitcast.2958, f32[256]{0:T(256)S(1)} %get-tuple-element.496), kind=kLoop, calls=%fused_computation.400 | loop fusion | flops 10485760 | bytes 25233408 | tf_op jit(solution)/shard_map/add | solution.py:207
  (256 shorter events, 42.2 us)
Async XLA Ops:
  1.0 371.1 %collective-permute-start = (f32[1,128,256]{2,1,0:T(8,128)S(1)}, f32[1,128,256]{2,1,0:T(8,128)S(1)}, u32[]{:S(2)}, u32[]{:S(2)}) collective-permute-start(f32[1,128,256]{2,1,0:T(8,128)S(1)} %get-tuple-element.1058), channel_id=1, source_target_pairs={{16,0},{17,1},{18,2},{19,3},{20,4},{21,5},{22,6},{23,7},{24,8},{25... | collective-permute-start | bytes 393224 | tf_op jit(solution)/shard_map/ppermute | solution.py:17
  2.3 369.9 %collective-permute-start.1 = (f32[1,128,256]{2,1,0:T(8,128)S(1)}, f32[1,128,256]{2,1,0:T(8,128)S(1)}, u32[]{:S(2)}, u32[]{:S(2)}) collective-permute-start(f32[1,128,256]{2,1,0:T(8,128)S(1)} %get-tuple-element.1057), channel_id=1, source_target_pairs={{0,16},{1,17},{2,18},{3,19},{4,20},{5,21},{6,22},{7,23},{8,24},{9,... | collective-permute-start | bytes 393224 | tf_op jit(solution)/shard_map/ppermute | solution.py:15
  13.1 69.9 %copy-start.2 = (f32[3,32,128]{2,1,0:T(8,128)}, f32[3,32,128]{2,1,0:T(8,128)S(1)}, u32[]{:S(2)}) copy-start(f32[3,32,128]{2,1,0:T(8,128)S(1)} %get-tuple-element.482) | copy-start | bytes 147460
  370.8 3.4 copy-start
  374.2 6.2 %collective-permute-start.2 = (f32[66,1,256]{2,0,1:T(8,128)S(1)}, f32[66,1,256]{2,0,1:T(8,128)S(1)}, u32[]{:S(2)}, u32[]{:S(2)}) collective-permute-start(f32[66,1,256]{2,0,1:T(8,128)S(1)} %get-tuple-element.1052), channel_id=1, source_target_pairs={{4,0},{8,4},{12,8},{5,1},{9,5},{13,9},{6,2},{10,6},{14,10},{7,3},{... | collective-permute-start | bytes 202760 | tf_op jit(solution)/shard_map/ppermute | solution.py:17
  375.5 4.9 collective-permute-start.3
  393.3 16.3 %collective-permute-start.5 = (f32[66,130,1]{0,1,2:T(8,128)S(1)}, f32[66,130,1]{0,1,2:T(8,128)S(1)}, u32[]{:S(2)}, u32[]{:S(2)}) collective-permute-start(f32[66,130,1]{0,1,2:T(8,128)S(1)} %copy.34), channel_id=1, source_target_pairs={{0,1},{1,2},{2,3},{4,5},{5,6},{6,7},{8,9},{9,10},{10,11},{12,13},{... | collective-permute-start | bytes 102968 | tf_op jit(solution)/shard_map/ppermute | solution.py:15
  401.5 11.8 %collective-permute-start.4 = (f32[66,130,1]{0,1,2:T(8,128)S(1)}, f32[66,130,1]{0,1,2:T(8,128)S(1)}, u32[]{:S(2)}, u32[]{:S(2)}) collective-permute-start(f32[66,130,1]{0,1,2:T(8,128)S(1)} %copy.32), channel_id=1, source_target_pairs={{1,0},{2,1},{3,2},{5,4},{6,5},{7,6},{9,8},{10,9},{11,10},{13,12},{... | collective-permute-start | bytes 102968 | tf_op jit(solution)/shard_map/ppermute | solution.py:17
  492.4 3.4 copy-start.1
where the time goes:
time: 550 us; the launch traced here: 541 us
  other arithmetic  302 us (55%)
  local copies, waits for them, and re-layouts  74.8 us (14%)
  matrix products  68.2 us (12%)
  between operations  31.9 us (6%)
  blocking collectives  31.8 us (6%)
  starting transfers between devices  16.4 us (3%)
  loops' own time  15.2 us (3%)
    sub x12, other arithmetic, spike_tables(): lax.linalg.tridiagonal_solve(lower_band, diagonal, upper_band, identity_m...  220 us
    dot_general x1, matrix products, sweep_axis(): jnp.einsum('ik,kbc->ibc', inverse, values, precision=lax.Precision.HIGHES...  43.2 us
    broadcast_in_dim x29, other arithmetic, spike_tables(): lax.linalg.tridiagonal_solve(lower_band, diagonal, upper_band, identity_m...  40.9 us
    slice x61, local copies, waits for them, and re-layouts, spike_tables(): lax.linalg.tridiagonal_solve(lower_band, diagonal, upper_band, identity_m...  20.3 us
    sub x3, other arithmetic, finish_pair(): preceding = beta_own - prior_own * (tau_own - theta_own * following)  16.2 us
    another operation x4, loops' own time, spike_tables(): lax.linalg.tridiagonal_solve(lower_band, diagonal, upper_band, identity_m...  15.2 us
    all_gather x1, blocking collectives, settle_third(): lax.all_gather(endpoints[None], 'gz', axis=0, tiled=True)  14.7 us
    unnamed x9, local copies, waits for them, and re-layouts  14.1 us
  transfers between devices with their start and end apart: 6, of which 0 were waited for; matrix products, arithmetic and copies ran while one was open for 62% of the time, Pallas kernels for 0%

commit v1 on v0

v1 whole, which is shorter than its diff:
```python
import functools

import jax
import jax.numpy as jnp
import numpy as np
from jax import lax
from jax.experimental import pallas as pl
from jax.experimental.pallas import tpu as pltpu
from jax.sharding import PartitionSpec as P

F32 = jnp.float32
BF16 = jnp.bfloat16
MIB = 1 << 20


def line_tables(length, factor):
    matrix = (1.0 + factor) * np.eye(length)
    matrix -= 0.5 * factor * (np.eye(length, k=1) + np.eye(length, k=-1))
    inverse = np.linalg.inv(matrix)
    inverse = 0.5 * (inverse + inverse.T)
    return inverse, 0.5 * factor * inverse[:, 0], 0.5 * factor * inverse[:, -1]


def interface_table(before, after, members):
    near, far = before[0], before[-1]
    system = np.eye(2 * members)
    for m in range(members):
        if m > 0:
            system[2 * m, 2 * m - 1] -= near
            system[2 * m + 1, 2 * m - 1] -= far
        if m < members - 1:
            system[2 * m, 2 * m + 2] -= far
            system[2 * m + 1, 2 * m + 2] -= near
    solved = np.linalg.inv(system)
    rows = np.zeros((members, 2, 2 * members))
    for m in range(members):
        if m > 0:
            rows[m, 0] = solved[2 * m - 1]
        if m < members - 1:
            rows[m, 1] = solved[2 * m + 2]
    return rows


def sweep_table(length, factor):
    half = 0.5 * factor
    ratio = np.zeros(length)
    scale = np.zeros(length)
    last = 0.0
    for i in range(length):
        scale[i] = 1.0 / (1.0 + factor - half * last)
        ratio[i] = last = half * scale[i]
    head = np.concatenate([[1.0], np.cumprod(ratio)[:-1]])
    return np.stack([scale, ratio, head, np.cumprod(ratio)])


def split(table):
    high = np.asarray(table, np.float32).astype(BF16)
    low = (np.asarray(table, np.float64) - high.astype(np.float64)).astype(BF16)
    return high, low


def parts(values):
    high = values.astype(BF16)
    return high, (values - high.astype(F32)).astype(BF16)


def dot(a, b):
    return jnp.dot(a, b, preferred_element_type=F32)


def exact_dot(a, b):
    return jnp.dot(a, b, precision=lax.Precision.HIGHEST, preferred_element_type=F32)


def local_kernel(
    group,
    sweep_ref, upward_high_ref, upward_low_ref, north_ref, warmth_hbm, supply_hbm,
    swept_ref, rest_ref, upward_ends_ref, north_ends_ref, east_ends_ref,
    warmth_ref, supply_ref, sems,
):
    east, north, upward = warmth_ref.shape
    groups = east // group
    copies = []
    for g in range(groups):
        block = pl.ds(g * group, group)
        copies.append((
            pltpu.make_async_copy(warmth_hbm.at[block], warmth_ref.at[block], sems.at[0, g]),
            pltpu.make_async_copy(supply_hbm.at[block], supply_ref.at[block], sems.at[1, g]),
        ))
    for pair in copies:
        for copy in pair:
            copy.start()
    upward_ends_ref[...] = jnp.zeros_like(upward_ends_ref)
    east_ends_ref[...] = jnp.zeros_like(east_ends_ref)
    lane = lax.broadcasted_iota(jnp.int32, (1, 2 * east), 1)

    def body(g, _):
        block = pl.ds(pl.multiple_of(g * group, group), group)
        for which, (hbm, ref) in enumerate(((warmth_hbm, warmth_ref), (supply_hbm, supply_ref))):
            pltpu.make_async_copy(hbm.at[block], ref.at[block], sems.at[which, g]).wait()
        warmth = warmth_ref[block]
        flat = (group * north, upward)
        heat = jnp.reshape(supply_ref[block] + 6.0 * warmth, flat)
        heat_high, heat_low = parts(heat)
        warm_high, warm_low = parts(jnp.reshape(warmth, flat))
        upward_high, upward_low = upward_high_ref[...], upward_low_ref[...]
        heat_up = dot(heat_high, upward_high) + dot(heat_low, upward_high) + dot(heat_high, upward_low)
        warm_up = dot(warm_high, upward_high) + dot(warm_low, upward_high)
        for k in range(group):
            i = g * group + k
            rows = slice(k * north, (k + 1) * north)
            first, second = heat_up[rows], warm_up[rows]
            warm = warmth[k]
            for field, value in enumerate((first, second)):
                half = upward // 2
                both = jnp.where(lane < east, value[:, : 2 * east], value[:, upward - 2 * east :])
                turned = pltpu.roll(both, 2 * i + 1, 1)
                own = (lane == 2 * i) | (lane == 2 * i + 1)
                upward_ends_ref[field] = jnp.where(own, turned, upward_ends_ref[field])
            first_high, first_low = parts(first - 2.0 * warm)
            second_high, second_low = parts(second)
            north_one = dot(north_ref[...], jnp.concatenate([first_high, first_low], axis=0))
            north_one = north_one[:north] + north_one[north:]
            north_two = dot(north_ref[:north], jnp.concatenate([second_high, second_low], axis=0))
            for field, value in enumerate((north_one, north_two)):
                north_ends_ref[field, 0, pl.ds(i, 1), :] = value[:1]
                north_ends_ref[field, 1, pl.ds(i, 1), :] = value[north - 1 :]
            rest_ref[i] = warm - 2.0 * north_two
            source = sweep_ref[0, i] * (north_one - 2.0 * second)
            swept = source + sweep_ref[1, i] * east_ends_ref[1]
            swept_ref[i] = swept
            east_ends_ref[1] = swept
            east_ends_ref[0] += sweep_ref[2, i] * swept
        return 0

    lax.fori_loop(0, groups, body, 0)


def upward_kernel(
    axis, members,
    table_ref, gathered_ref, north_ends_ref, east_ends_ref, north_inverse_ref, east_twice_ref, spikes_ref, spread_ref,
    columns_ref, north_out_ref, east_out_ref,
):
    me = lax.axis_index(axis)
    north, lanes = columns_ref.shape
    east = lanes // 2
    even = lax.broadcasted_iota(jnp.int32, (1, lanes), 1) % 2 == 0
    fields = []
    for field in range(2):
        same = jnp.zeros((north, lanes), F32)
        cross = jnp.zeros((north, lanes), F32)
        for m in range(members):
            ends = gathered_ref[m, field]
            before_head, before_tail = table_ref[me, 2 * m], table_ref[me, 2 * m + 1]
            after_head = table_ref[me, 2 * members + 2 * m]
            after_tail = table_ref[me, 2 * members + 2 * m + 1]
            same += ends * jnp.where(even, before_tail, after_head)
            cross += ends * jnp.where(even, after_tail, before_head)
        fields.append(same + jnp.where(even, pltpu.roll(cross, lanes - 1, 1), pltpu.roll(cross, 1, 1)))
    heat_side, warm_side = fields
    solved = exact_dot(north_inverse_ref[...], jnp.concatenate(fields, axis=1))
    heat_solved, warm_solved = solved[:, :lanes], solved[:, lanes:]
    swept = exact_dot(heat_solved - 2.0 * warm_side, east_twice_ref[...])
    columns_ref[...] = swept - 2.0 * warm_solved
    place = lax.broadcasted_iota(jnp.int32, (east, lanes), 1) // 2
    own = place == lax.broadcasted_iota(jnp.int32, (east, lanes), 0)
    picked = []
    for value in (heat_solved, warm_solved):
        for row in (value[:1], value[north - 1 :]):
            picked.append(jnp.where(own, row, 0.0))
    added = exact_dot(jnp.concatenate(picked, axis=0), spread_ref[...])
    for k in range(4):
        north_out_ref[k // 2, k % 2] = north_ends_ref[k // 2, k % 2] + added[k * east : (k + 1) * east]
    for end, start in ((0, 0), (1, lanes - 2)):
        east_out_ref[end] = (
            east_ends_ref[end]
            + swept[:, start : start + 1] * spikes_ref[0:1, :]
            + swept[:, start + 1 : start + 2] * spikes_ref[1:2, :]
        )


def north_kernel(
    axis, members, east_axis, pair,
    table_ref, gathered_ref, east_ends_ref, east_inverse_ref, spikes_ref,
    rows_ref, east_out_ref,
):
    me = lax.axis_index(axis)
    east = rows_ref.shape[1]
    sides = []
    for field in range(2):
        for side in range(2):
            total = jnp.zeros(rows_ref.shape[1:], F32)
            for m in range(members):
                for end in range(2):
                    total += gathered_ref[m, field, end] * table_ref[me, side * 2 * members + 2 * m + end]
            sides.append(total)
    swept = [exact_dot(east_inverse_ref[...], sides[0]), exact_dot(east_inverse_ref[...], sides[1])]
    for side in range(2):
        rows_ref[side] = swept[side] - 2.0 * sides[2 + side]
    ends = []
    for end, row in ((0, 0), (1, east - 1)):
        ends.append(
            east_ends_ref[end]
            + spikes_ref[0] * swept[0][row : row + 1]
            + spikes_ref[1] * swept[1][row : row + 1]
        )
    if pair:
        east_out_ref[...] = jnp.where(lax.axis_index(east_axis) == 0, ends[1], ends[0])
    else:
        for end in range(2):
            east_out_ref[end] = ends[end]


def final_kernel(
    axis, members, pair, tile,
    table_ref, sweep_ref, own_ref, other_ref, swept_ref, rest_ref, columns_ref, rows_ref, upward_spikes_ref, north_spikes_ref,
    out_hbm,
    out_ref, sides_ref, sems,
):
    me = lax.axis_index(axis)
    east, north, upward = out_ref.shape
    if pair:
        value = table_ref[0, 0] * other_ref[...] + table_ref[0, 1] * own_ref[...]
        sides_ref[0] = jnp.where(me == 0, 0.0, value)
        sides_ref[1] = jnp.where(me == 0, value, 0.0)
    else:
        for side in range(2):
            total = jnp.zeros(sides_ref.shape[1:], F32)
            for m in range(members):
                for end in range(2):
                    total += other_ref[m, end] * table_ref[me, side * 2 * members + 2 * m + end]
            sides_ref[side] = total

    def send(t):
        block = pl.ds(pl.multiple_of(t * tile, tile), tile)
        return pltpu.make_async_copy(out_ref.at[:, block], out_hbm.at[:, block], sems.at[t])

    def body(t, _):
        block = pl.ds(pl.multiple_of(t * tile, tile), tile)
        before = sides_ref[0, block]
        value = sides_ref[1, block]
        columns = columns_ref[block]
        first_spike, last_spike = north_spikes_ref[0, block], north_spikes_ref[1, block]
        for i in reversed(range(east)):
            value = swept_ref[i, block] + sweep_ref[3, i] * before + sweep_ref[1, i] * value
            added = (
                columns[:, 2 * i : 2 * i + 1] * upward_spikes_ref[0:1, :]
                + columns[:, 2 * i + 1 : 2 * i + 2] * upward_spikes_ref[1:2, :]
            )
            added += first_spike * rows_ref[0, i : i + 1, :] + last_spike * rows_ref[1, i : i + 1, :]
            out_ref[i, block] = rest_ref[i, block] + value + added
        send(t).start()
        return 0

    lax.fori_loop(0, north // tile, body, 0)
    for t in range(north // tile):
        send(t).wait()


def local(initial_warmth, heat_supply):
    shape = east, north, upward = initial_warmth.shape
    members = [lax.axis_size(axis) for axis in ("gx", "gy", "gz")]
    factors = [float((n * m) ** 2 // 4) for n, m in zip(shape, members)]
    lines = [line_tables(n, factor) for n, factor in zip(shape, factors)]
    faces = [interface_table(line[1], line[2], m) for line, m in zip(lines, members)]
    faces = [table.reshape(m, 4 * m).astype(np.float32) for table, m in zip(faces, members)]
    sweep = sweep_table(east, factors[0]).astype(np.float32)
    upward_high, upward_low = split(lines[2][0])
    north_high, north_low = split(lines[1][0])
    north_stack = np.block([[north_high, north_high], [north_low, np.zeros_like(north_low)]])
    east_inverse = lines[0][0].astype(np.float32)
    north_inverse = lines[1][0].astype(np.float32)
    east_twice = np.kron(lines[0][0], np.eye(2)).astype(np.float32)
    upward_spikes = np.stack(lines[2][1:]).astype(np.float32)
    spread = np.tile(upward_spikes, (east, 1))
    north_spikes = np.broadcast_to(np.stack(lines[1][1:])[:, :, None], (2, north, upward)).astype(np.float32)

    vmem = pl.BlockSpec(memory_space=pltpu.VMEM)
    smem = pl.BlockSpec(memory_space=pltpu.SMEM)
    hbm = pl.BlockSpec(memory_space=pl.ANY)
    params = pltpu.CompilerParams(vmem_limit_bytes=40 * MIB)
    small = pltpu.CompilerParams(vmem_limit_bytes=16 * MIB)
    group = 4
    swept, rest, upward_ends, north_ends, east_ends = pl.pallas_call(
        functools.partial(local_kernel, group),
        in_specs=[smem, vmem, vmem, vmem, hbm, hbm],
        out_specs=[vmem] * 5,
        out_shape=[
            pltpu.VMEM(shape, F32),
            pltpu.VMEM(shape, F32),
            jax.ShapeDtypeStruct((2, north, 2 * east), F32),
            jax.ShapeDtypeStruct((2, 2, east, upward), F32),
            jax.ShapeDtypeStruct((2, north, upward), F32),
        ],
        scratch_shapes=[
            pltpu.VMEM(shape, F32),
            pltpu.VMEM(shape, F32),
            pltpu.SemaphoreType.DMA((2, east // group)),
        ],
        compiler_params=params,
    )(sweep, upward_high, upward_low, north_stack, initial_warmth, heat_supply)

    gathered = lax.all_gather(upward_ends, "gz")
    columns, north_ends, east_ends = pl.pallas_call(
        functools.partial(upward_kernel, "gz", members[2]),
        in_specs=[smem] + [vmem] * 7,
        out_specs=[vmem] * 3,
        out_shape=[
            jax.ShapeDtypeStruct((north, 2 * east), F32),
            jax.ShapeDtypeStruct(north_ends.shape, F32),
            jax.ShapeDtypeStruct(east_ends.shape, F32),
        ],
        compiler_params=small,
    )(faces[2], gathered, north_ends, east_ends, north_inverse, east_twice, upward_spikes, spread)

    pair = members[0] == 2
    gathered = lax.all_gather(north_ends, "gy")
    rows, own = pl.pallas_call(
        functools.partial(north_kernel, "gy", members[1], "gx", pair),
        in_specs=[smem] + [vmem] * 4,
        out_specs=[vmem] * 2,
        out_shape=[
            jax.ShapeDtypeStruct((2, east, upward), F32),
            jax.ShapeDtypeStruct((north, upward) if pair else east_ends.shape, F32),
        ],
        compiler_params=small,
    )(faces[1], gathered, east_ends, east_inverse, north_spikes)

    if pair:
        other = lax.ppermute(own, "gx", [(0, 1), (1, 0)])
        near = lines[0][1][0]
        table = np.array([[1.0 / (1.0 - near**2), near / (1.0 - near**2)]], np.float32)
    else:
        other = lax.all_gather(own, "gx")
        table = faces[0]
    tile = 32
    return pl.pallas_call(
        functools.partial(final_kernel, "gx", members[0], pair, tile),
        in_specs=[smem, smem] + [vmem] * 8,
        out_specs=hbm,
        out_shape=jax.ShapeDtypeStruct(shape, F32),
        scratch_shapes=[
            pltpu.VMEM(shape, F32),
            pltpu.VMEM((2, north, upward), F32),
            pltpu.SemaphoreType.DMA((north // tile,)),
        ],
        compiler_params=params,
    )(table, sweep, own, other, swept, rest, columns, rows, upward_spikes, north_spikes)


def solution(mesh):
    return jax.shard_map(
        local,
        mesh=mesh,
        in_specs=(P("gx", "gy", "gz"), P("gx", "gy", "gz")),
        out_specs=P("gx", "gy", "gz"),
        check_vma=False,
    )
```

time: 550 us -> 99.2 us (0.18); the launches traced: 541 us -> 98.9 us
  other arithmetic: 302 us -> 0 us
  matrix products: 68.2 us -> 0 us
  local copies, waits for them, and re-layouts: 74.8 us -> 13.2 us
  Pallas kernels: 0 us -> 30.2 us
  waiting for transfers between devices: 0.02 us -> 22.8 us
  between operations: 31.9 us -> 13.5 us
  loops' own time: 15.2 us -> 0 us
  starting transfers between devices: 16.4 us -> 1.58 us
  blocking collectives: 31.8 us -> 17.6 us
    sub x16 -> x0, other arithmetic: 241 us -> none  [the longest x12 220 us: spike_tables(): lax.linalg.tridiagonal_solve(lower_band, diagonal, upper_band, identity_m...]
    dot_general x6 -> x0, matrix products: 68.2 us -> none  [the longest x1 43.2 us: sweep_axis(): jnp.einsum('ik,kbc->ibc', inverse, values, precision=lax.Precision.HIGHES...]
    slice x84 -> x0, local copies, waits for them, and re-layouts: 48.1 us -> none  [the longest x61 20.3 us: spike_tables(): lax.linalg.tridiagonal_solve(lower_band, diagonal, upper_band, identity_m...]
    broadcast_in_dim x29 -> x0, other arithmetic: 40.9 us -> none  [spike_tables(): lax.linalg.tridiagonal_solve(lower_band, diagonal, upper_band, identity_m...]
    pallas_call x0 -> x4, Pallas kernels: none -> 30.2 us  [the longest x1 18.1 us: local(): pl.pallas_call(functools.partial(local_kernel, group), in_specs=[smem, vm...]
    all_gather x0 -> x1, waiting for transfers between devices: none -> 18.7 us  [local(): gathered = lax.all_gather(north_ends, 'gy')]
    another operation x4 -> x0, loops' own time: 15.2 us -> none  [spike_tables(): lax.linalg.tridiagonal_solve(lower_band, diagonal, upper_band, identity_m...]
    ppermute x6 -> x1, starting transfers between devices: 16.4 us -> 1.54 us  [local(): other = lax.ppermute(own, 'gx', [(0, 1), (1, 0)])]
  transfers between devices with their start and end apart: 6 -> 2, of which waited for: 0 -> 2; matrix products, arithmetic and copies ran while one was open for 62% -> 0% of each run, Pallas kernels for 0% -> 0%
where the time goes in v1:
time: 99.2 us; the launch traced here: 98.9 us
  Pallas kernels  30.2 us (30%)
  waiting for transfers between devices  22.8 us (23%)
  blocking collectives  17.6 us (18%)
  between operations  13.5 us (14%)
  local copies, waits for them, and re-layouts  13.2 us (13%)
  starting transfers between devices  1.58 us (2%)
    all_gather x1, waiting for transfers between devices, local(): gathered = lax.all_gather(north_ends, 'gy')  18.7 us
    pallas_call x1, Pallas kernels, local(): pl.pallas_call(functools.partial(local_kernel, group), in_specs=[smem, vm...  18.1 us
    all_gather x1, blocking collectives, local(): gathered = lax.all_gather(upward_ends, 'gz')  17.6 us
    unnamed x32, local copies, waits for them, and re-layouts  13.2 us
    pallas_call x1, Pallas kernels, local(): pl.pallas_call(functools.partial(final_kernel, 'gx', members[0], pair, ti...  8.99 us
    ppermute x1, waiting for transfers between devices, local(): other = lax.ppermute(own, 'gx', [(0, 1), (1, 0)])  4.15 us
    pallas_call x1, Pallas kernels, local(): pl.pallas_call(functools.partial(upward_kernel, 'gz', members[2]), in_spe...  2.2 us
  transfers between devices with their start and end apart: 2, of which 2 were waited for; matrix products, arithmetic and copies ran while one was open for 0% of the time, Pallas kernels for 0%

profile of v1, /device:TPU:0, one launch (start us, length us, event | category | flops | bytes accessed | tf_op | source)
XLA Modules:
  0.0 98.9 jit_solution(8768531655792139912)
XLA Ops:
  6.5 0.0 copy-start.7
  6.5 0.0 copy-start.8
  6.5 0.0 copy-start.9
  6.5 0.0 copy-start.12
  6.5 0.0 copy-start.14
  6.6 0.0 copy-start.3
  6.6 0.0 copy-start.10
  6.6 0.0 copy-start.13
  6.6 0.0 copy-start.11
  6.6 0.0 copy-start.15
  6.6 0.0 all-gather.4.cloned.1.call-start
  6.7 18.1 %shard_map.145 = (f32[64,128,256]{2,1,0:T(8,128)S(1)}, f32[64,128,256]{2,1,0:T(8,128)S(1)}, f32[2,128,128]{2,1,0:T(8,128)}, f32[2,2,64,256]{3,2,1,0:T(8,128)}, f32[2,128,256]{2,1,0:T(8,128)}) custom-call(f32[4,64]{1,0:T(4,128)} %constant.26.clone.sweep_ref, bf16[256,256]{1,0:T(8,128)(2,1)} %constant.27.clone.upward_high_ref, ...), custom_call_target="tpu_custom_call" | custom-call | tf_op jit(solution)/shard_map/pallas_call | solution.py:284
  24.8 0.0 copy-start
  24.8 3.4 %copy-done = f32[64,128,256]{2,1,0:T(8,128)} copy-done((f32[64,128,256]{2,1,0:T(8,128)}, f32[64,128,256]{2,1,0:T(8,128)S(1)}, u32[]{:S(2)}) %copy-start) | copy-done | bytes 8388632
  28.2 0.0 copy-start.2
  28.2 3.3 %copy-done.2 = f32[64,128,256]{2,1,0:T(8,128)} copy-done((f32[64,128,256]{2,1,0:T(8,128)}, f32[64,128,256]{2,1,0:T(8,128)S(1)}, u32[]{:S(2)}) %copy-start.2) | copy-done | bytes 8388632
  31.4 17.6 %all-gather = f32[8,128,128]{2,1,0:T(8,128)S(1)} all-gather(f32[2,128,128]{2,1,0:T(8,128)} %get-tuple-element.15), channel_id=2, replica_groups=mesh['gx'=2,'gy'=4,'gz'=4] {'gz'}, dimensions={0}, use_global_device_ids=true | all-gather | bytes 655360 | tf_op jit(solution)/shard_map/all_gather | solution.py:303
  49.0 0.0 copy-done.7
  49.0 0.0 copy-done.8
  49.0 0.0 copy-done.9
  49.0 0.0 copy-done.12
  49.0 0.0 copy-done.14
  49.0 0.0 copy-start.5
  49.0 0.9 copy-done.5
  49.9 0.0 copy-start.6
  49.9 0.9 copy-done.6
  50.9 2.2 %shard_map.146 = (f32[128,128]{1,0:T(8,128)S(1)}, f32[2,2,64,256]{3,2,1,0:T(8,128)}, f32[2,128,256]{2,1,0:T(8,128)S(1)}) custom-call(f32[4,16]{1,0:T(4,128)S(1)} %copy-done.14, f32[4,2,128,128]{3,2,1,0:T(8,128)S(1)} %bitcast.2, f32[2,2,64,256]{3,2,1,0:T(8,128)S(1)} %copy-done.5, f32[2,128,256]{2,1,0:T(8,128)S(1)} %copy-done.6, f32[128,128]{1,0:T(8,128)S(1)} %copy-done.9, ...), custom_call_target="tpu_custom_call" | custom-call | tf_op jit(solution)/shard_map/pallas_call | solution.py:304
  53.1 0.0 all-gather.4.cloned.1.call-update
  53.1 18.7 %all-gather.4.cloned.1.call-done = f32[8,2,64,256]{3,2,1,0:T(8,128)} async-done(((f32[2,2,64,256]{3,2,1,0:T(8,128)}), f32[8,2,64,256]{3,2,1,0:T(8,128)}) %all-gather.4.cloned.1.call-update) | async-done | bytes 1048592 | tf_op jit(solution)/shard_map/all_gather | solution.py:317
  71.8 0.0 copy-done.3
  71.8 0.0 copy-done.10
  71.8 0.0 copy-done.13
  71.8 0.0 copy-start.4
  71.8 1.2 %copy-done.4 = f32[8,2,64,256]{3,2,1,0:T(8,128)S(1)} copy-done((f32[8,2,64,256]{3,2,1,0:T(8,128)S(1)}, f32[8,2,64,256]{3,2,1,0:T(8,128)}, u32[]{:S(2)}) %copy-start.4) | copy-done | bytes 1048600
  73.0 1.0 shard_map.147
  74.0 1.5 %collective-permute-start = (f32[128,256]{1,0:T(8,128)S(1)}, f32[128,256]{1,0:T(8,128)S(1)}, u32[]{:S(2)}, u32[]{:S(2)}) collective-permute-start(f32[128,256]{1,0:T(8,128)S(1)} %get-tuple-element.20.own_ref), channel_id=1, source_target_pairs={{0,16},{16,0},{1,17},{17,1},{2,18},{18,2},{3,19},{19,3},{4,20},{20... | collective-permute-start | bytes 393224 | tf_op jit(solution)/shard_map/ppermute | solution.py:330
  75.5 4.2 %collective-permute-done.other_ref = f32[128,256]{1,0:T(8,128)S(1)} collective-permute-done((f32[128,256]{1,0:T(8,128)S(1)}, f32[128,256]{1,0:T(8,128)S(1)}, u32[]{:S(2)}, u32[]{:S(2)}) %collective-permute-start) | collective-permute-done | bytes 131104 | tf_op jit(solution)/shard_map/ppermute | solution.py:330
  79.7 0.0 copy-done.11
  79.7 0.0 copy-done.15
  79.7 0.0 copy-start.1
  79.7 3.4 %copy-done.1 = f32[64,128,256]{2,1,0:T(8,128)S(1)} copy-done((f32[64,128,256]{2,1,0:T(8,128)S(1)}, f32[64,128,256]{2,1,0:T(8,128)}, u32[]{:S(2)}) %copy-start.1) | copy-done | bytes 8388632
  83.0 9.0 %shard_map.148 = f32[64,128,256]{2,1,0:T(8,128)} custom-call(f32[1,2]{1,0:T(1,128)S(1)} %copy-done.15, f32[4,64]{1,0:T(4,128)S(1)} %copy-done.11, f32[128,256]{1,0:T(8,128)S(1)} %get-tuple-element.20.own_ref, f32[128,256]{1,0:T(8,128)S(1)} %collective-permute-done.other_ref, f32[64,128,256]{2,1,0:T(8,128)S(1)} %copy-done.1, f32[64,128,256]{2,1,0:T(8,128)} %copy-done.2, ...), custom_call_target="tpu_custom_call" | custom-call | tf_op jit(solution)/shard_map/pallas_call | solution.py:337
Async XLA Ops:
  6.5 42.4 %copy-start.7 = (f32[128,256]{1,0:T(8,128)S(1)}, f32[128,256]{1,0:T(8,128)}, u32[]{:S(2)}) copy-start(f32[128,256]{1,0:T(8,128)} %constant.34.clone.spread_ref) | copy-start | bytes 393220
  6.5 42.4 %copy-start.8 = (f32[128,128]{1,0:T(8,128)S(1)}, f32[128,128]{1,0:T(8,128)}, u32[]{:S(2)}) copy-start(f32[128,128]{1,0:T(8,128)} %constant.32.clone.east_twice_ref) | copy-start | bytes 196612
  6.5 42.4 %copy-start.9 = (f32[128,128]{1,0:T(8,128)S(1)}, f32[128,128]{1,0:T(8,128)}, u32[]{:S(2)}) copy-start(f32[128,128]{1,0:T(8,128)} %constant.31.clone.north_inverse_ref) | copy-start | bytes 196612
  6.5 42.4 %copy-start.12 = (f32[2,256]{1,0:T(2,128)S(1)}, f32[2,256]{1,0:T(2,128)}, u32[]{:S(2)}) copy-start(f32[2,256]{1,0:T(2,128)} %constant.33.clone.spikes_ref.upward_spikes_ref) | copy-start | bytes 6148
  6.5 42.4 %copy-start.14 = (f32[4,16]{1,0:T(4,128)S(1)}, f32[4,16]{1,0:T(4,128)}, u32[]{:S(2)}) copy-start(f32[4,16]{1,0:T(4,128)} %constant.30.clone.table_ref) | copy-start | bytes 772
  6.6 65.2 %copy-start.3 = (f32[2,128,256]{2,1,0:T(8,128)S(1)}, f32[2,128,256]{2,1,0:T(8,128)}, u32[]{:S(2)}) copy-start(f32[2,128,256]{2,1,0:T(8,128)} %constant.37.clone.spikes_ref.north_spikes_ref) | copy-start | bytes 786436
  6.6 65.2 %copy-start.10 = (f32[64,64]{1,0:T(8,128)S(1)}, f32[64,64]{1,0:T(8,128)}, u32[]{:S(2)}) copy-start(f32[64,64]{1,0:T(8,128)} %constant.36.clone.east_inverse_ref) | copy-start | bytes 49156
  6.6 65.2 %copy-start.13 = (f32[4,16]{1,0:T(4,128)S(1)}, f32[4,16]{1,0:T(4,128)}, u32[]{:S(2)}) copy-start(f32[4,16]{1,0:T(4,128)} %constant.35.clone.table_ref) | copy-start | bytes 772
  6.6 73.1 %copy-start.11 = (f32[4,64]{1,0:T(4,128)S(1)}, f32[4,64]{1,0:T(4,128)}, u32[]{:S(2)}) copy-start(f32[4,64]{1,0:T(4,128)} %constant.26.clone.sweep_ref) | copy-start | bytes 3076
  6.6 73.1 %copy-start.15 = (f32[1,2]{1,0:T(1,128)S(1)}, f32[1,2]{1,0:T(1,128)}, u32[]{:S(2)}) copy-start(f32[1,2]{1,0:T(1,128)} %constant.38.clone.table_ref) | copy-start | bytes 28
  6.6 65.2 %all-gather.4.cloned.1.call-start = ((), (), s32[]{:S(2)}) async-start(), calls=%async_computation | async-start | bytes 1310720 | tf_op jit(solution)/shard_map/all_gather | solution.py:317
  24.8 3.4 %copy-start = (f32[64,128,256]{2,1,0:T(8,128)}, f32[64,128,256]{2,1,0:T(8,128)S(1)}, u32[]{:S(2)}) copy-start(f32[64,128,256]{2,1,0:T(8,128)S(1)} %get-tuple-element.21.swept_ref) | copy-start | bytes 25165828
  28.2 3.3 %copy-start.2 = (f32[64,128,256]{2,1,0:T(8,128)}, f32[64,128,256]{2,1,0:T(8,128)S(1)}, u32[]{:S(2)}) copy-start(f32[64,128,256]{2,1,0:T(8,128)S(1)} %get-tuple-element.22.rest_ref) | copy-start | bytes 25165828
  49.0 1.0 copy-start.5
  49.9 0.9 copy-start.6
  71.8 1.2 %copy-start.4 = (f32[8,2,64,256]{3,2,1,0:T(8,128)S(1)}, f32[8,2,64,256]{3,2,1,0:T(8,128)}, u32[]{:S(2)}) copy-start(f32[8,2,64,256]{3,2,1,0:T(8,128)} %all-gather.4.cloned.1.call-done) | copy-start | bytes 3145732
  74.0 5.7 %collective-permute-start = (f32[128,256]{1,0:T(8,128)S(1)}, f32[128,256]{1,0:T(8,128)S(1)}, u32[]{:S(2)}, u32[]{:S(2)}) collective-permute-start(f32[128,256]{1,0:T(8,128)S(1)} %get-tuple-element.20.own_ref), channel_id=1, source_target_pairs={{0,16},{16,0},{1,17},{17,1},{2,18},{18,2},{3,19},{19,3},{4,20},{20... | collective-permute-start | bytes 393224 | tf_op jit(solution)/shard_map/ppermute | solution.py:330
  79.7 3.4 %copy-start.1 = (f32[64,128,256]{2,1,0:T(8,128)S(1)}, f32[64,128,256]{2,1,0:T(8,128)}, u32[]{:S(2)}) copy-start(f32[64,128,256]{2,1,0:T(8,128)} %copy-done) | copy-start | bytes 25165828
Sparse Core Ops, SparseCore 0:
  53.2 18.4 all-gather.3

commit v2 on v1

v2 whole, which is shorter than its diff:
```python
import functools

import jax
import jax.numpy as jnp
import numpy as np
from jax import lax
from jax.experimental import pallas as pl
from jax.experimental.pallas import tpu as pltpu
from jax.sharding import PartitionSpec as P

F32 = jnp.float32
BF16 = jnp.bfloat16
MIB = 1 << 20


def line_tables(length, factor):
    matrix = (1.0 + factor) * np.eye(length)
    matrix -= 0.5 * factor * (np.eye(length, k=1) + np.eye(length, k=-1))
    inverse = np.linalg.inv(matrix)
    inverse = 0.5 * (inverse + inverse.T)
    return inverse, 0.5 * factor * inverse[:, 0], 0.5 * factor * inverse[:, -1]


def chain_system(near, far, members):
    system = np.eye(2 * members)
    for m in range(members):
        if m > 0:
            system[2 * m, 2 * m - 1] -= near
            system[2 * m + 1, 2 * m - 1] -= far
        if m < members - 1:
            system[2 * m, 2 * m + 2] -= far
            system[2 * m + 1, 2 * m + 2] -= near
    return np.linalg.inv(system)


def interface_table(before, after, members):
    solved = chain_system(before[0], before[-1], members)
    rows = np.zeros((members, 2, 2 * members))
    for m in range(members):
        if m > 0:
            rows[m, 0] = solved[2 * m - 1]
        if m < members - 1:
            rows[m, 1] = solved[2 * m + 2]
    return rows


def peers(member, members, distance):
    if members & (members - 1) == 0:
        return member ^ distance, member ^ distance
    return (member + distance) % members, (member - distance) % members


def exchange_tables(before, after, members):
    near, far = before[0], before[-1]
    sending = np.zeros((members, 2 * (members - 1)))
    taking = np.zeros((members, 8 + 2 * (members - 1)))
    for m in range(members):
        right = chain_system(near, far, members - 1 - m)
        left = chain_system(near, far, m)
        for d in range(1, members):
            k = peers(m, members, d)[1]
            if k > m:
                sending[k, 2 * d - 2 : 2 * d] = right[0, 2 * (k - m - 1) : 2 * (k - m)]
                taking[m, 8 + 2 * d - 1] = 1.0
            else:
                sending[k, 2 * d - 2 : 2 * d] = left[-1, 2 * k : 2 * k + 2]
                taking[m, 8 + 2 * d - 2] = 1.0
        pull_left = answer(near, far, m)
        pull_right = answer(near, far, members - 1 - m)
        system = np.array([
            [1.0, 0.0, -pull_left, 0.0],
            [0.0, 1.0, 0.0, -pull_right],
            [-near, -far, 1.0, 0.0],
            [-far, -near, 0.0, 1.0],
        ])
        taking[m, :8] = np.linalg.inv(system)[:2].reshape(8)
    return sending, taking


def answer(near, far, members):
    if members == 0:
        return 0.0
    push = np.zeros(2 * members)
    push[0], push[1] = near, far
    return chain_system(near, far, members)[0] @ push


def sweep_table(length, factor):
    half = 0.5 * factor
    ratio = np.zeros(length)
    scale = np.zeros(length)
    last = 0.0
    for i in range(length):
        scale[i] = 1.0 / (1.0 + factor - half * last)
        ratio[i] = last = half * scale[i]
    head = np.concatenate([[1.0], np.cumprod(ratio)[:-1]])
    return np.stack([scale, ratio, head, np.cumprod(ratio)])


def split(table, axis):
    rows = np.moveaxis(np.asarray(table, np.float64), axis, 0)
    high = np.zeros(rows.shape, BF16)
    carried = np.zeros(rows.shape[1:])
    for k, row in enumerate(rows):
        high[k] = (row + carried).astype(np.float32).astype(BF16)
        carried = carried + row - high[k].astype(np.float64)
    low = (rows - high.astype(np.float64)).astype(np.float32).astype(BF16)
    return np.moveaxis(high, 0, axis), np.moveaxis(low, 0, axis)


def parts(values):
    high = values.astype(BF16)
    return high, (values - high.astype(F32)).astype(BF16)


def dot(a, b):
    return jnp.dot(a, b, preferred_element_type=F32)


def exact_dot(a, b):
    return jnp.dot(a, b, precision=lax.Precision.HIGHEST, preferred_element_type=F32)


def send_all(ends, table_ref, me, out_refs):
    for d, out_ref in enumerate(out_refs):
        out_ref[...] = table_ref[me, 2 * d] * ends[0] + table_ref[me, 2 * d + 1] * ends[1]


def take_all(ends, table_ref, me, message_refs):
    left = right = 0.0
    for d, message_ref in enumerate(message_refs):
        left += table_ref[me, 8 + 2 * d] * message_ref[...]
        right += table_ref[me, 9 + 2 * d] * message_ref[...]
    known = (left, right) + tuple(ends)
    return [sum(table_ref[me, 4 * side + k] * known[k] for k in range(4)) for side in range(2)]


def ordered(pair, east):
    if not pair:
        return lambda i: i
    flip = lax.axis_index("gx")
    return lambda i: jnp.where(flip == 0, i, east - 1 - i)


def local_kernel(
    pair, group, factor,
    sweep_ref, sending_ref, upward_high_ref, upward_low_ref, north_ref, warmth_hbm, supply_hbm,
    swept_ref, warmth_ref, upward_ends_ref, north_ends_ref, east_ends_ref, *rest,
):
    *message_refs, supply_ref, both_ref, planes_ref, sems = rest
    east, north, upward = warmth_ref.shape
    groups = east // group
    last = east_ends_ref.shape[0] - 1
    place = ordered(pair, east)
    me_up = lax.axis_index("gz")

    def fetch(which, g):
        start = jnp.minimum(place(g * group), place(g * group + group - 1))
        block = pl.ds(start, group)
        source, target = ((warmth_hbm, warmth_ref), (supply_hbm, supply_ref))[which]
        return pltpu.make_async_copy(source.at[block], target.at[block], sems.at[which, g])

    for g in range(groups):
        for which in range(2):
            fetch(which, g).start()
    both_ref[...] = jnp.zeros_like(both_ref)
    east_ends_ref[...] = jnp.zeros_like(east_ends_ref)
    north_ends_ref[:, east:] = jnp.zeros_like(north_ends_ref[:, east:])
    lane = lax.broadcasted_iota(jnp.int32, (1, 2 * east), 1)
    fetch(0, 0).wait()

    def body(g, _):
        fetch(1, g).wait()

        @pl.when(g + 1 < groups)
        def _():
            fetch(0, g + 1).wait()

        flat = (group * north, upward)
        warm_list, heat_list = [], []
        for k in range(group):
            i = g * group + k
            warm = warmth_ref[place(i)]
            low = warmth_ref[place(jnp.maximum(i - 1, 0))]
            high = warmth_ref[place(jnp.minimum(i + 1, east - 1))]
            low_factor = jnp.where(i == 0, 0.0, factor)
            high_factor = jnp.where(i == east - 1, 0.0, factor)
            heat = supply_ref[place(i)] + (4.0 - 2.0 * factor) * warm
            heat_list.append(heat + (low_factor * low + high_factor * high))
            warm_list.append(warm)
        heat_high, heat_low = parts(jnp.reshape(jnp.stack(heat_list), flat))
        warm_high, warm_low = parts(jnp.reshape(jnp.stack(warm_list), flat))
        upward_high, upward_low = upward_high_ref[...], upward_low_ref[...]
        heat_up = dot(heat_high, upward_high) + dot(heat_low, upward_high) + dot(heat_high, upward_low)
        warm_up = dot(warm_high, upward_high) + dot(warm_low, upward_high)
        for k in range(group):
            i = g * group + k
            rows = slice(k * north, (k + 1) * north)
            first, second = heat_up[rows], warm_up[rows]
            for field, value in enumerate((first, second)):
                both = jnp.where(lane < east, value[:, : 2 * east], value[:, upward - 2 * east :])
                turned = pltpu.roll(both, 2 * i + 1, 1)
                own = (lane == 2 * i) | (lane == 2 * i + 1)
                both_ref[field] = jnp.where(own, turned, both_ref[field])
            first_high, first_low = parts(first - 2.0 * warm_list[k])
            solved = dot(north_ref[...], jnp.concatenate([first_high, first_low], axis=0))
            solved = solved[:north] + solved[north:]
            north_ends_ref[0, pl.ds(i, 1), :] = solved[:1]
            north_ends_ref[1, pl.ds(i, 1), :] = solved[north - 1 :]
            source = sweep_ref[0, i] * (solved - 2.0 * second)
            swept = source + sweep_ref[1, i] * east_ends_ref[last]
            swept_ref[i] = swept
            east_ends_ref[last] = swept
            if not pair:
                east_ends_ref[0] += sweep_ref[2, i] * swept

                @pl.when(i == 0)
                def _():
                    planes_ref[0] = second

            if k == group - 1:

                @pl.when(i == east - 1)
                def _():
                    planes_ref[last] = second

        return 0

    lax.fori_loop(0, groups, body, 0)

    count = east_ends_ref.shape[0]
    for p in range(count):
        high, low = parts(planes_ref[p])
        solved = dot(north_ref[...], jnp.concatenate([high, low], axis=0))
        solved = solved[:north] + solved[north:]
        row = east + count - 1 - p
        north_ends_ref[0, row : row + 1] = solved[:1]
        north_ends_ref[1, row : row + 1] = solved[north - 1 :]
        east_ends_ref[p] += 2.0 * solved
    even = lane % 2 == 0
    heat, warm = both_ref[0], both_ref[1]
    heads = jnp.where(even, pltpu.roll(heat, 2 * east - 1, 1), warm)
    tails = jnp.where(even, heat, pltpu.roll(warm, 1, 1))
    upward_ends_ref[0] = heads
    upward_ends_ref[1] = tails
    send_all((heads, tails), sending_ref, me_up, message_refs)


def upward_kernel(
    count, taken, sent,
    taking_ref, sending_ref, ends_ref, north_ends_ref, east_ends_ref, north_inverse_ref, fold_ref, spikes_ref, spread_ref, *rest,
):
    message_refs = rest[:taken]
    columns_ref, north_out_ref, east_out_ref = rest[taken : taken + 3]
    out_refs = rest[taken + 3 :]
    assert len(out_refs) == sent
    north, lanes = columns_ref.shape
    east = lanes // 2
    sides = take_all((ends_ref[0], ends_ref[1]), taking_ref, lax.axis_index("gz"), message_refs)
    sides = jnp.concatenate(sides, axis=1)
    lane = lax.broadcasted_iota(jnp.int32, (1, 2 * lanes), 1) % lanes
    solved = exact_dot(north_inverse_ref[...], sides)
    mixed = jnp.where(lane % 2 == 0, solved, sides)
    swept = [exact_dot(mixed[:, side * lanes : (side + 1) * lanes], fold_ref[...]) for side in range(2)]
    columns_ref[...] = jnp.concatenate(swept, axis=1)
    padded = north_ends_ref.shape[1]
    row = lax.broadcasted_iota(jnp.int32, (padded, 2 * lanes), 0)
    target = jnp.where(row < east, 2 * row, jnp.where(row == east, lanes - 1, jnp.where(row < east + count, 1, -1)))
    own = lax.broadcasted_iota(jnp.int32, (padded, 2 * lanes), 1) % lanes == target
    picked = [jnp.where(own, solved[y : y + 1], 0.0) for y in (0, north - 1)]
    added = exact_dot(jnp.concatenate(picked, axis=0), spread_ref[...])
    ends = [north_ends_ref[0] + added[:padded], north_ends_ref[1] + added[padded:]]
    north_out_ref[0] = ends[0]
    north_out_ref[1] = ends[1]
    send_all(ends, sending_ref, lax.axis_index("gy"), out_refs)
    for p in range(count):
        i = east - 1 if p == count - 1 else 0
        total = east_ends_ref[p]
        for side in range(2):
            odd = side * lanes + 2 * i + 1
            column = swept[side][:, i : i + 1] + 2.0 * solved[:, odd : odd + 1]
            total += column * spikes_ref[side : side + 1, :]
        east_out_ref[p] = total


def north_kernel(
    count, taken,
    taking_ref, ends_ref, east_ends_ref, east_inverse_ref, spikes_ref, *rest,
):
    message_refs = rest[:taken]
    rows_ref, east_out_ref = rest[taken:]
    east = rows_ref.shape[1]
    sides = take_all((ends_ref[0], ends_ref[1]), taking_ref, lax.axis_index("gy"), message_refs)
    swept = [exact_dot(east_inverse_ref[...], side[:east]) for side in sides]
    for side in range(2):
        rows_ref[side] = swept[side]
    for p in range(count):
        i = east - 1 if p == count - 1 else 0
        extra = east + count - 1 - p
        total = east_ends_ref[p]
        for side in range(2):
            total += spikes_ref[side] * (swept[side][i : i + 1] + 2.0 * sides[side][extra : extra + 1])
        east_out_ref[p] = total


def final_kernel(
    pair, members, tile,
    table_ref, sweep_ref, own_ref, other_ref, swept_ref, warmth_ref, columns_ref, rows_ref, upward_spikes_ref, north_spikes_ref,
    out_hbm,
    out_ref, sides_ref, sems,
):
    east, north, upward = out_ref.shape
    place = ordered(pair, east)
    if pair:
        sides_ref[0] = table_ref[0, 0] * other_ref[0] + table_ref[0, 1] * own_ref[0]
    else:
        me = lax.axis_index("gx")
        for side in range(2):
            total = jnp.zeros(sides_ref.shape[1:], F32)
            for m in range(members):
                for end in range(2):
                    total += other_ref[m, end] * table_ref[me, side * 2 * members + 2 * m + end]
            sides_ref[side] = total

    def send(t):
        block = pl.ds(pl.multiple_of(t * tile, tile), tile)
        return pltpu.make_async_copy(out_ref.at[:, block], out_hbm.at[:, block], sems.at[t])

    def body(t, _):
        block = pl.ds(pl.multiple_of(t * tile, tile), tile)
        value = sides_ref[sides_ref.shape[0] - 1, block]
        columns = columns_ref[block]
        first_spike, last_spike = north_spikes_ref[0, block], north_spikes_ref[1, block]
        for i in reversed(range(east)):
            value = swept_ref[i, block] + sweep_ref[1, i] * value
            if not pair:
                value += sweep_ref[3, i] * sides_ref[0, block]
            added = (
                columns[:, i : i + 1] * upward_spikes_ref[0:1, :]
                + columns[:, east + i : east + i + 1] * upward_spikes_ref[1:2, :]
            )
            added += first_spike * rows_ref[0, i : i + 1, :] + last_spike * rows_ref[1, i : i + 1, :]
            x = place(i)
            out_ref[x, block] = warmth_ref[x, block] + value + added
        send(t).start()
        return 0

    lax.fori_loop(0, north // tile, body, 0)
    for t in range(north // tile):
        send(t).wait()


def spread_out(messages, axis):
    members = lax.axis_size(axis)
    return [
        lax.ppermute(message, axis, [(k, peers(k, members, d + 1)[0]) for k in range(members)])
        for d, message in enumerate(messages)
    ]


def local(initial_warmth, heat_supply):
    shape = east, north, upward = initial_warmth.shape
    members = [lax.axis_size(axis) for axis in ("gx", "gy", "gz")]
    factors = [float((n * m) ** 2 // 4) for n, m in zip(shape, members)]
    lines = [line_tables(n, factor) for n, factor in zip(shape, factors)]
    sweep = sweep_table(east, factors[0]).astype(np.float32)
    exchanges = [exchange_tables(line[1], line[2], m) for line, m in zip(lines, members)]
    exchanges = [tuple(table.astype(np.float32) for table in pair_of) for pair_of in exchanges]
    upward_high, upward_low = split(lines[2][0], 0)
    north_high, north_low = split(lines[1][0], 1)
    north_stack = np.block([[north_high, north_high], [north_low, np.zeros_like(north_low)]])
    east_inverse = lines[0][0].astype(np.float32)
    north_inverse = lines[1][0].astype(np.float32)
    fold = np.kron(lines[0][0], np.array([[1.0], [-2.0]])).astype(np.float32)
    upward_spikes = np.stack(lines[2][1:]).astype(np.float32)
    spread = np.repeat(upward_spikes, 2 * east, axis=0)
    north_spikes = np.broadcast_to(np.stack(lines[1][1:])[:, :, None], (2, north, upward)).astype(np.float32)

    pair = members[0] == 2
    count = 1 if pair else 2
    padded = east + 8
    to_up, to_north = members[2] - 1, members[1] - 1
    vmem = pl.BlockSpec(memory_space=pltpu.VMEM)
    smem = pl.BlockSpec(memory_space=pltpu.SMEM)
    hbm = pl.BlockSpec(memory_space=pl.ANY)

    def kept(*sizes):
        return jax.ShapeDtypeStruct(sizes, F32)

    group = 4
    swept, warmth, upward_ends, north_ends, east_ends, *messages = pl.pallas_call(
        functools.partial(local_kernel, pair, group, factors[0]),
        in_specs=[smem, smem, vmem, vmem, vmem, hbm, hbm],
        out_specs=[vmem] * (5 + to_up),
        out_shape=[
            pltpu.VMEM(shape, F32),
            pltpu.VMEM(shape, F32),
            kept(2, north, 2 * east),
            kept(2, padded, upward),
            kept(count, north, upward),
        ]
        + [kept(north, 2 * east)] * to_up,
        scratch_shapes=[
            pltpu.VMEM(shape, F32),
            pltpu.VMEM((2, north, 2 * east), F32),
            pltpu.VMEM((count, north, upward), F32),
            pltpu.SemaphoreType.DMA((2, east // group)),
        ],
        compiler_params=pltpu.CompilerParams(vmem_limit_bytes=32 * MIB),
    )(sweep, exchanges[2][0], upward_high, upward_low, north_stack, initial_warmth, heat_supply)

    messages = spread_out(messages, "gz")
    columns, north_ends, east_ends, *messages = pl.pallas_call(
        functools.partial(upward_kernel, count, to_up, to_north),
        in_specs=[smem, smem] + [vmem] * (7 + to_up),
        out_specs=[vmem] * (3 + to_north),
        out_shape=[kept(north, 2 * east), kept(2, padded, upward), kept(count, north, upward)]
        + [kept(padded, upward)] * to_north,
        compiler_params=pltpu.CompilerParams(vmem_limit_bytes=6 * MIB),
    )(
        exchanges[2][1], exchanges[1][0], upward_ends, north_ends, east_ends, north_inverse, fold, upward_spikes, spread,
        *messages,
    )

    messages = spread_out(messages, "gy")
    rows, own = pl.pallas_call(
        functools.partial(north_kernel, count, to_north),
        in_specs=[smem] + [vmem] * (4 + to_north),
        out_specs=[vmem] * 2,
        out_shape=[kept(2, east, upward), kept(count, north, upward)],
        compiler_params=pltpu.CompilerParams(vmem_limit_bytes=6 * MIB),
    )(exchanges[1][1], north_ends, east_ends, east_inverse, north_spikes, *messages)

    if pair:
        other = lax.ppermute(own, "gx", [(0, 1), (1, 0)])
        near = lines[0][1][0]
        table = np.array([[1.0 / (1.0 - near**2), near / (1.0 - near**2)]], np.float32)
    else:
        other = lax.all_gather(own, "gx")
        table = interface_table(lines[0][1], lines[0][2], members[0]).reshape(members[0], -1).astype(np.float32)
    swept = pltpu.with_memory_space_constraint(swept, pltpu.VMEM)
    warmth = pltpu.with_memory_space_constraint(warmth, pltpu.VMEM)
    tile = 32
    return pl.pallas_call(
        functools.partial(final_kernel, pair, members[0], tile),
        in_specs=[smem, smem] + [vmem] * 8,
        out_specs=hbm,
        out_shape=kept(*shape),
        scratch_shapes=[
            pltpu.VMEM(shape, F32),
            pltpu.VMEM((count, north, upward), F32),
            pltpu.SemaphoreType.DMA((north // tile,)),
        ],
        compiler_params=pltpu.CompilerParams(vmem_limit_bytes=16 * MIB),
    )(table, sweep, own, other, swept, warmth, columns, rows, upward_spikes, north_spikes)


def solution(mesh):
    return jax.shard_map(
        local,
        mesh=mesh,
        in_specs=(P("gx", "gy", "gz"), P("gx", "gy", "gz")),
        out_specs=P("gx", "gy", "gz"),
        check_vma=False,
    )
```

time: 99.2 us -> 53.3 us (0.54)
  blocking collectives: 17.6 us -> 0 us
  between operations: 13.5 us -> 0.11 us
  local copies, waits for them, and re-layouts: 13.2 us -> 4.18 us
  waiting for transfers between devices: 22.8 us -> 14.2 us
  starting transfers between devices: 1.58 us -> 9.21 us
  Pallas kernels: 30.2 us -> 25.4 us
    all_gather x1 -> x0, waiting for transfers between devices: 18.7 us -> none  [local(): gathered = lax.all_gather(north_ends, 'gy')]
    all_gather x1 -> x0, blocking collectives: 17.6 us -> none  [local(): gathered = lax.all_gather(upward_ends, 'gz')]
    ppermute x0 -> x6, waiting for transfers between devices: none -> 10.3 us  [spread_out(): lax.ppermute(message, axis, [(k, peers(k, members, d + 1)[0]) for k in ra...]
    unnamed x32 -> x30, local copies, waits for them, and re-layouts: 13.2 us -> 4.18 us
    ppermute x0 -> x6, starting transfers between devices: none -> 7.61 us  [spread_out(): lax.ppermute(message, axis, [(k, peers(k, members, d + 1)[0]) for k in ra...]
    pallas_call x4, Pallas kernels: 30.2 us -> 25.4 us  [the longest x1 16.9 us: local(): pl.pallas_call(functools.partial(local_kernel, pair, group, factors[0]),...]
  transfers between devices with their start and end apart: 2 -> 7, of which waited for: 2 -> 5; matrix products, arithmetic and copies ran while one was open for 0% -> 0% of each run, Pallas kernels for 0% -> 0%
where the time goes in v2:
time: 53.3 us; the launch traced here: 53.1 us
  Pallas kernels  25.4 us (48%)
  waiting for transfers between devices  14.2 us (27%)
  starting transfers between devices  9.21 us (17%)
  local copies, waits for them, and re-layouts  4.18 us (8%)
    pallas_call x1, Pallas kernels, local(): pl.pallas_call(functools.partial(local_kernel, pair, group, factors[0]),...  16.9 us
    ppermute x6, waiting for transfers between devices, spread_out(): lax.ppermute(message, axis, [(k, peers(k, members, d + 1)[0]) for k in ra...  10.3 us
    ppermute x6, starting transfers between devices, spread_out(): lax.ppermute(message, axis, [(k, peers(k, members, d + 1)[0]) for k in ra...  7.61 us
    pallas_call x1, Pallas kernels, local(): pl.pallas_call(functools.partial(final_kernel, pair, members[0], tile), i...  6.06 us
    unnamed x30, local copies, waits for them, and re-layouts  4.18 us
    ppermute x1, waiting for transfers between devices, local(): other = lax.ppermute(own, 'gx', [(0, 1), (1, 0)])  3.99 us
    ppermute x1, starting transfers between devices, local(): other = lax.ppermute(own, 'gx', [(0, 1), (1, 0)])  1.6 us
    pallas_call x1, Pallas kernels, local(): pl.pallas_call(functools.partial(upward_kernel, count, to_up, to_north),...  1.46 us
  transfers between devices with their start and end apart: 7, of which 5 were waited for; matrix products, arithmetic and copies ran while one was open for 0% of the time, Pallas kernels for 0%

profile of v2, /device:TPU:0, one launch (start us, length us, event | category | flops | bytes accessed | tf_op | source)
XLA Modules:
  0.0 53.1 jit_solution(15822451785362721175)
XLA Ops:
  0.0 0.0 copy-start.1
  0.0 0.0 copy-start
  0.0 0.0 copy-start.2
  0.0 1.0 %copy-done.2 = bf16[256,256]{1,0:T(8,128)(2,1)S(1)} copy-done((bf16[256,256]{1,0:T(8,128)(2,1)S(1)}, bf16[256,256]{1,0:T(8,128)(2,1)}, u32[]{:S(2)}) %copy-start.2) | copy-done | bytes 131096
  1.0 0.0 copy-start.3
  1.0 0.9 %copy-done.3 = bf16[256,256]{1,0:T(8,128)(2,1)S(1)} copy-done((bf16[256,256]{1,0:T(8,128)(2,1)S(1)}, bf16[256,256]{1,0:T(8,128)(2,1)}, u32[]{:S(2)}) %copy-start.3) | copy-done | bytes 131096
  1.9 0.0 copy-start.4
  1.9 0.9 %copy-done.4 = bf16[256,256]{1,0:T(8,128)(2,1)S(1)} copy-done((bf16[256,256]{1,0:T(8,128)(2,1)S(1)}, bf16[256,256]{1,0:T(8,128)(2,1)}, u32[]{:S(2)}) %copy-start.4) | copy-done | bytes 131096
  2.8 0.0 copy-start.8
  2.8 0.7 %copy-done.8 = f32[4,64]{1,0:T(4,128)S(1)} copy-done((f32[4,64]{1,0:T(4,128)S(1)}, f32[4,64]{1,0:T(4,128)}, u32[]{:S(2)}) %copy-start.8) | copy-done | bytes 1048
  3.5 0.0 copy-start.13
  3.5 0.7 %copy-done.13 = f32[4,6]{1,0:T(4,128)S(1)} copy-done((f32[4,6]{1,0:T(4,128)S(1)}, f32[4,6]{1,0:T(4,128)}, u32[]{:S(2)}) %copy-start.13) | copy-done | bytes 120
  4.1 0.0 copy-start.5
  4.1 0.0 copy-start.6
  4.1 0.0 copy-start.9
  4.1 0.0 copy-start.11
  4.2 0.0 copy-start.12
  4.2 0.0 copy-start.7
  4.2 0.0 copy-start.10
  4.2 0.0 copy-start.14
  4.2 16.9 %shard_map.163 = (f32[64,128,256]{2,1,0:T(8,128)S(1)}, f32[64,128,256]{2,1,0:T(8,128)S(1)}, f32[2,128,128]{2,1,0:T(8,128)S(1)}, f32[2,72,256]{2,1,0:T(8,128)S(1)...) custom-call(f32[4,64]{1,0:T(4,128)S(1)} %copy-done.8, ...), custom_call_target="tpu_custom_call" | custom-call | tf_op jit(solution)/shard_map/pallas_call | solution.py:391
  21.1 3.1 %collective-permute-start = (f32[128,128]{1,0:T(8,128)S(1)}, f32[128,128]{1,0:T(8,128)S(1)}, u32[]{:S(2)}, u32[]{:S(2)}) collective-permute-start(f32[128,128]{1,0:T(8,128)S(1)} %get-tuple-element.24), channel_id=1, source_target_pairs={{0,1},{1,0},{2,3},{3,2},{4,5},{5,4},{6,7},{7,6},{8,9},{9,8},{10,11... | collective-permute-start | bytes 196616 | tf_op jit(solution)/shard_map/ppermute | solution.py:356
  24.2 2.6 %collective-permute-start.1 = (f32[128,128]{1,0:T(8,128)S(1)}, f32[128,128]{1,0:T(8,128)S(1)}, u32[]{:S(2)}, u32[]{:S(2)}) collective-permute-start(f32[128,128]{1,0:T(8,128)S(1)} %get-tuple-element.25), channel_id=1, source_target_pairs={{0,2},{1,3},{2,0},{3,1},{4,6},{5,7},{6,4},{7,5},{8,10},{9,11},{10,... | collective-permute-start | bytes 196616 | tf_op jit(solution)/shard_map/ppermute | solution.py:356
  26.8 0.0 collective-permute-start.2
  26.8 0.0 collective-permute-done.rest_0_
  26.8 4.7 %collective-permute-done.1.rest_1_ = f32[128,128]{1,0:T(8,128)S(1)} collective-permute-done((f32[128,128]{1,0:T(8,128)S(1)}, f32[128,128]{1,0:T(8,128)S(1)}, u32[]{:S(2)}, u32[]{:S(2)}) %collective-permute-start.1) | collective-permute-done | bytes 65568 | tf_op jit(solution)/shard_map/ppermute | solution.py:356
  31.5 1.4 %collective-permute-done.2.rest_2_ = f32[128,128]{1,0:T(8,128)S(1)} collective-permute-done((f32[128,128]{1,0:T(8,128)S(1)}, f32[128,128]{1,0:T(8,128)S(1)}, u32[]{:S(2)}, u32[]{:S(2)}) %collective-permute-start.2) | collective-permute-done | bytes 65568 | tf_op jit(solution)/shard_map/ppermute | solution.py:356
  32.9 0.0 copy-done.1
  32.9 0.0 copy-done.5
  32.9 0.0 copy-done.6
  32.9 0.0 copy-done.9
  32.9 0.0 copy-done.11
  32.9 0.0 copy-done.12
  32.9 1.5 %shard_map.164 = (f32[128,128]{1,0:T(8,128)S(1)}, f32[2,72,256]{2,1,0:T(8,128)S(1)}, f32[1,128,256]{2,1,0:T(8,128)S(1)}, f32[72,256]{1,0:T(8,128)S(1)}, f32[72,256]{1,0:T(8,128)S(1)}, /*index=5*/f32[72,256]{1,0:T(8,128)S(1)}) custom-call(f32[4,14]{1,0:T(4,128)S(1)} %copy-done.12, f32[4,6]{1,0:T(4,128)S(1)} %copy-done.11, ...), custom_call_target="tpu_custom_call" | custom-call | tf_op jit(solution)/shard_map/pallas_call | solution.py:413
  34.4 0.1 collective-permute-start.3
  34.5 1.6 %collective-permute-start.4 = (f32[72,256]{1,0:T(8,128)S(1)}, f32[72,256]{1,0:T(8,128)S(1)}, u32[]{:S(2)}, u32[]{:S(2)}) collective-permute-start(f32[72,256]{1,0:T(8,128)S(1)} %get-tuple-element.30), channel_id=1, source_target_pairs={{0,8},{4,12},{8,0},{12,4},{1,9},{5,13},{9,1},{13,5},{2,10},{6,14},... | collective-permute-start | bytes 221192 | tf_op jit(solution)/shard_map/ppermute | solution.py:356
  36.0 0.3 collective-permute-start.5
  36.3 0.0 collective-permute-done.3.rest_0_
  36.3 3.0 %collective-permute-done.4.rest_1_ = f32[72,256]{1,0:T(8,128)S(1)} collective-permute-done((f32[72,256]{1,0:T(8,128)S(1)}, f32[72,256]{1,0:T(8,128)S(1)}, u32[]{:S(2)}, u32[]{:S(2)}) %collective-permute-start.4) | collective-permute-done | bytes 73760 | tf_op jit(solution)/shard_map/ppermute | solution.py:356
  39.3 1.2 %collective-permute-done.5.rest_2_ = f32[72,256]{1,0:T(8,128)S(1)} collective-permute-done((f32[72,256]{1,0:T(8,128)S(1)}, f32[72,256]{1,0:T(8,128)S(1)}, u32[]{:S(2)}, u32[]{:S(2)}) %collective-permute-start.5) | collective-permute-done | bytes 73760 | tf_op jit(solution)/shard_map/ppermute | solution.py:356
  40.5 0.0 copy-done
  40.5 0.0 copy-done.7
  40.5 0.0 copy-done.10
  40.5 0.9 %shard_map.165 = (f32[2,64,256]{2,1,0:T(8,128)S(1)}, f32[1,128,256]{2,1,0:T(8,128)S(1)}) custom-call(f32[4,14]{1,0:T(4,128)S(1)} %copy-done.10, f32[2,72,256]{2,1,0:T(8,128)S(1)} %get-tuple-element.27.ends_ref, f32[1,128,256]{2,1,0:T(8,128)S(1)} %get-tuple-element.28.east_ends_ref, f32[64,64]{1,0:T(8,128)S(1)} %copy-done.7, f32[2,128,256]{2,1,0:T(8,128)S(1)} %copy-done, ...), custom_call_target="tpu_custom_call" | custom-call | tf_op jit(solution)/shard_map/pallas_call | solution.py:426
  41.5 1.6 %collective-permute-start.6 = (f32[1,128,256]{2,1,0:T(8,128)S(1)}, f32[1,128,256]{2,1,0:T(8,128)S(1)}, u32[]{:S(2)}, u32[]{:S(2)}) collective-permute-start(f32[1,128,256]{2,1,0:T(8,128)S(1)} %get-tuple-element.32.own_ref), channel_id=1, source_target_pairs={{0,16},{16,0},{1,17},{17,1},{2,18},{18,2},{3,19},{19,3},{4,20},{20... | collective-permute-start | bytes 393224 | tf_op jit(solution)/shard_map/ppermute | solution.py:435
  43.1 4.0 %collective-permute-done.6.other_ref = f32[1,128,256]{2,1,0:T(8,128)S(1)} collective-permute-done((f32[1,128,256]{2,1,0:T(8,128)S(1)}, f32[1,128,256]{2,1,0:T(8,128)S(1)}, u32[]{:S(2)}, u32[]{:S(2)}) %collective-permute-start.6) | collective-permute-done | bytes 131104 | tf_op jit(solution)/shard_map/ppermute | solution.py:435
  47.0 0.0 copy-done.14
  47.0 6.1 %shard_map.166 = f32[64,128,256]{2,1,0:T(8,128)} custom-call(f32[1,2]{1,0:T(1,128)S(1)} %copy-done.14, f32[4,64]{1,0:T(4,128)S(1)} %copy-done.8, f32[1,128,256]{2,1,0:T(8,128)S(1)} %get-tuple-element.32.own_ref, f32[1,128,256]{2,1,0:T(8,128)S(1)} %collective-permute-done.6.other_ref, f32[64,128,256]{2,1,0:T(8,128)S(1)} %get-tuple-element.33.swept_ref, ...), custom_call_target="tpu_custom_call" | custom-call | tf_op jit(solution)/shard_map/pallas_call | solution.py:444
Async XLA Ops:
  0.0 32.9 %copy-start.1 = (f32[256,256]{1,0:T(8,128)S(1)}, f32[256,256]{1,0:T(8,128)}, u32[]{:S(2)}) copy-start(f32[256,256]{1,0:T(8,128)} %constant.40.clone.spread_ref) | copy-start | bytes 786436
  0.0 40.5 %copy-start = (f32[2,128,256]{2,1,0:T(8,128)S(1)}, f32[2,128,256]{2,1,0:T(8,128)}, u32[]{:S(2)}) copy-start(f32[2,128,256]{2,1,0:T(8,128)} %constant.43.clone.spikes_ref.north_spikes_ref) | copy-start | bytes 786436
  0.0 1.0 %copy-start.2 = (bf16[256,256]{1,0:T(8,128)(2,1)S(1)}, bf16[256,256]{1,0:T(8,128)(2,1)}, u32[]{:S(2)}) copy-start(bf16[256,256]{1,0:T(8,128)(2,1)} %constant.34.clone.north_ref) | copy-start | bytes 393220
  1.0 0.9 %copy-start.3 = (bf16[256,256]{1,0:T(8,128)(2,1)S(1)}, bf16[256,256]{1,0:T(8,128)(2,1)}, u32[]{:S(2)}) copy-start(bf16[256,256]{1,0:T(8,128)(2,1)} %constant.33.clone.upward_low_ref) | copy-start | bytes 393220
  1.9 0.9 %copy-start.4 = (bf16[256,256]{1,0:T(8,128)(2,1)S(1)}, bf16[256,256]{1,0:T(8,128)(2,1)}, u32[]{:S(2)}) copy-start(bf16[256,256]{1,0:T(8,128)(2,1)} %constant.32.clone.upward_high_ref) | copy-start | bytes 393220
  2.8 0.7 %copy-start.8 = (f32[4,64]{1,0:T(4,128)S(1)}, f32[4,64]{1,0:T(4,128)}, u32[]{:S(2)}) copy-start(f32[4,64]{1,0:T(4,128)} %constant.30.clone.sweep_ref) | copy-start | bytes 3076
  3.5 0.7 %copy-start.13 = (f32[4,6]{1,0:T(4,128)S(1)}, f32[4,6]{1,0:T(4,128)}, u32[]{:S(2)}) copy-start(f32[4,6]{1,0:T(4,128)} %constant.31.clone.sending_ref) | copy-start | bytes 292
  4.1 28.7 %copy-start.5 = (f32[128,64]{1,0:T(8,128)S(1)}, f32[128,64]{1,0:T(8,128)}, u32[]{:S(2)}) copy-start(f32[128,64]{1,0:T(8,128)} %constant.38.clone.fold_ref) | copy-start | bytes 98308
  4.1 28.7 %copy-start.6 = (f32[128,128]{1,0:T(8,128)S(1)}, f32[128,128]{1,0:T(8,128)}, u32[]{:S(2)}) copy-start(f32[128,128]{1,0:T(8,128)} %constant.37.clone.north_inverse_ref) | copy-start | bytes 196612
  4.1 28.7 %copy-start.9 = (f32[2,256]{1,0:T(2,128)S(1)}, f32[2,256]{1,0:T(2,128)}, u32[]{:S(2)}) copy-start(f32[2,256]{1,0:T(2,128)} %constant.39.clone.spikes_ref.upward_spikes_ref) | copy-start | bytes 6148
  4.1 28.8 %copy-start.11 = (f32[4,6]{1,0:T(4,128)S(1)}, f32[4,6]{1,0:T(4,128)}, u32[]{:S(2)}) copy-start(f32[4,6]{1,0:T(4,128)} %constant.36.clone.sending_ref) | copy-start | bytes 292
  4.2 28.8 %copy-start.12 = (f32[4,14]{1,0:T(4,128)S(1)}, f32[4,14]{1,0:T(4,128)}, u32[]{:S(2)}) copy-start(f32[4,14]{1,0:T(4,128)} %constant.35.clone.taking_ref) | copy-start | bytes 676
  4.2 36.4 %copy-start.7 = (f32[64,64]{1,0:T(8,128)S(1)}, f32[64,64]{1,0:T(8,128)}, u32[]{:S(2)}) copy-start(f32[64,64]{1,0:T(8,128)} %constant.42.clone.east_inverse_ref) | copy-start | bytes 49156
  4.2 36.3 %copy-start.10 = (f32[4,14]{1,0:T(4,128)S(1)}, f32[4,14]{1,0:T(4,128)}, u32[]{:S(2)}) copy-start(f32[4,14]{1,0:T(4,128)} %constant.41.clone.taking_ref) | copy-start | bytes 676
  4.2 42.9 %copy-start.14 = (f32[1,2]{1,0:T(1,128)S(1)}, f32[1,2]{1,0:T(1,128)}, u32[]{:S(2)}) copy-start(f32[1,2]{1,0:T(1,128)} %constant.44.clone.table_ref) | copy-start | bytes 28
  21.1 5.7 %collective-permute-start = (f32[128,128]{1,0:T(8,128)S(1)}, f32[128,128]{1,0:T(8,128)S(1)}, u32[]{:S(2)}, u32[]{:S(2)}) collective-permute-start(f32[128,128]{1,0:T(8,128)S(1)} %get-tuple-element.24), channel_id=1, source_target_pairs={{0,1},{1,0},{2,3},{3,2},{4,5},{5,4},{6,7},{7,6},{8,9},{9,8},{10,11... | collective-permute-start | bytes 196616 | tf_op jit(solution)/shard_map/ppermute | solution.py:356
  24.2 7.3 %collective-permute-start.1 = (f32[128,128]{1,0:T(8,128)S(1)}, f32[128,128]{1,0:T(8,128)S(1)}, u32[]{:S(2)}, u32[]{:S(2)}) collective-permute-start(f32[128,128]{1,0:T(8,128)S(1)} %get-tuple-element.25), channel_id=1, source_target_pairs={{0,2},{1,3},{2,0},{3,1},{4,6},{5,7},{6,4},{7,5},{8,10},{9,11},{10,... | collective-permute-start | bytes 196616 | tf_op jit(solution)/shard_map/ppermute | solution.py:356
  26.8 6.1 %collective-permute-start.2 = (f32[128,128]{1,0:T(8,128)S(1)}, f32[128,128]{1,0:T(8,128)S(1)}, u32[]{:S(2)}, u32[]{:S(2)}) collective-permute-start(f32[128,128]{1,0:T(8,128)S(1)} %get-tuple-element.26), channel_id=1, source_target_pairs={{0,3},{1,2},{2,1},{3,0},{4,7},{5,6},{6,5},{7,4},{8,11},{9,10},{10,... | collective-permute-start | bytes 196616 | tf_op jit(solution)/shard_map/ppermute | solution.py:356
  34.4 1.9 %collective-permute-start.3 = (f32[72,256]{1,0:T(8,128)S(1)}, f32[72,256]{1,0:T(8,128)S(1)}, u32[]{:S(2)}, u32[]{:S(2)}) collective-permute-start(f32[72,256]{1,0:T(8,128)S(1)} %get-tuple-element.29), channel_id=1, source_target_pairs={{0,4},{4,0},{8,12},{12,8},{1,5},{5,1},{9,13},{13,9},{2,6},{6,2},{1... | collective-permute-start | bytes 221192 | tf_op jit(solution)/shard_map/ppermute | solution.py:356
  34.5 4.8 %collective-permute-start.4 = (f32[72,256]{1,0:T(8,128)S(1)}, f32[72,256]{1,0:T(8,128)S(1)}, u32[]{:S(2)}, u32[]{:S(2)}) collective-permute-start(f32[72,256]{1,0:T(8,128)S(1)} %get-tuple-element.30), channel_id=1, source_target_pairs={{0,8},{4,12},{8,0},{12,4},{1,9},{5,13},{9,1},{13,5},{2,10},{6,14},... | collective-permute-start | bytes 221192 | tf_op jit(solution)/shard_map/ppermute | solution.py:356
  36.0 4.5 %collective-permute-start.5 = (f32[72,256]{1,0:T(8,128)S(1)}, f32[72,256]{1,0:T(8,128)S(1)}, u32[]{:S(2)}, u32[]{:S(2)}) collective-permute-start(f32[72,256]{1,0:T(8,128)S(1)} %get-tuple-element.31), channel_id=1, source_target_pairs={{0,12},{4,8},{8,4},{12,0},{1,13},{5,9},{9,5},{13,1},{2,14},{6,10},... | collective-permute-start | bytes 221192 | tf_op jit(solution)/shard_map/ppermute | solution.py:356
  41.5 5.6 %collective-permute-start.6 = (f32[1,128,256]{2,1,0:T(8,128)S(1)}, f32[1,128,256]{2,1,0:T(8,128)S(1)}, u32[]{:S(2)}, u32[]{:S(2)}) collective-permute-start(f32[1,128,256]{2,1,0:T(8,128)S(1)} %get-tuple-element.32.own_ref), channel_id=1, source_target_pairs={{0,16},{16,0},{1,17},{17,1},{2,18},{18,2},{3,19},{19,3},{4,20},{20... | collective-permute-start | bytes 393224 | tf_op jit(solution)/shard_map/ppermute | solution.py:435

commit v3 on v2

v3 whole, which is shorter than its diff:
```python
import functools

import jax
import jax.numpy as jnp
import numpy as np
from jax import lax
from jax.experimental import pallas as pl
from jax.experimental.pallas import tpu as pltpu
from jax.sharding import PartitionSpec as P

F32 = jnp.float32
BF16 = jnp.bfloat16
MIB = 1 << 20


def line_tables(length, factor):
    matrix = (1.0 + factor) * np.eye(length)
    matrix -= 0.5 * factor * (np.eye(length, k=1) + np.eye(length, k=-1))
    inverse = np.linalg.inv(matrix)
    inverse = 0.5 * (inverse + inverse.T)
    return inverse, 0.5 * factor * inverse[:, 0], 0.5 * factor * inverse[:, -1]


def chain_system(near, far, members):
    system = np.eye(2 * members)
    for m in range(members):
        if m > 0:
            system[2 * m, 2 * m - 1] -= near
            system[2 * m + 1, 2 * m - 1] -= far
        if m < members - 1:
            system[2 * m, 2 * m + 2] -= far
            system[2 * m + 1, 2 * m + 2] -= near
    return np.linalg.inv(system)


def interface_table(before, after, members):
    solved = chain_system(before[0], before[-1], members)
    rows = np.zeros((members, 2, 2 * members))
    for m in range(members):
        if m > 0:
            rows[m, 0] = solved[2 * m - 1]
        if m < members - 1:
            rows[m, 1] = solved[2 * m + 2]
    return rows


def peers(member, members, distance):
    if members & (members - 1) == 0:
        return member ^ distance, member ^ distance
    return (member + distance) % members, (member - distance) % members


def exchange_tables(before, after, members):
    near, far = before[0], before[-1]
    sending = np.zeros((members, 2 * (members - 1)))
    taking = np.zeros((members, 8 + 2 * (members - 1)))
    for m in range(members):
        right = chain_system(near, far, members - 1 - m)
        left = chain_system(near, far, m)
        for d in range(1, members):
            k = peers(m, members, d)[1]
            if k > m:
                sending[k, 2 * d - 2 : 2 * d] = right[0, 2 * (k - m - 1) : 2 * (k - m)]
                taking[m, 8 + 2 * d - 1] = 1.0
            else:
                sending[k, 2 * d - 2 : 2 * d] = left[-1, 2 * k : 2 * k + 2]
                taking[m, 8 + 2 * d - 2] = 1.0
        pull_left = answer(near, far, m)
        pull_right = answer(near, far, members - 1 - m)
        system = np.array([
            [1.0, 0.0, -pull_left, 0.0],
            [0.0, 1.0, 0.0, -pull_right],
            [-near, -far, 1.0, 0.0],
            [-far, -near, 0.0, 1.0],
        ])
        taking[m, :8] = np.linalg.inv(system)[:2].reshape(8)
    return sending, taking


def answer(near, far, members):
    if members == 0:
        return 0.0
    push = np.zeros(2 * members)
    push[0], push[1] = near, far
    return chain_system(near, far, members)[0] @ push


def sweep_table(length, factor):
    half = 0.5 * factor
    ratio = np.zeros(length)
    scale = np.zeros(length)
    last = 0.0
    for i in range(length):
        scale[i] = 1.0 / (1.0 + factor - half * last)
        ratio[i] = last = half * scale[i]
    head = np.concatenate([[1.0], np.cumprod(ratio)[:-1]])
    return np.stack([scale, ratio, head, np.cumprod(ratio)])


def split(table, axis):
    rows = np.moveaxis(np.asarray(table, np.float64), axis, 0)
    high = np.zeros(rows.shape, BF16)
    carried = np.zeros(rows.shape[1:])
    for k, row in enumerate(rows):
        high[k] = (row + carried).astype(np.float32).astype(BF16)
        carried = carried + row - high[k].astype(np.float64)
    low = (rows - high.astype(np.float64)).astype(np.float32).astype(BF16)
    return np.moveaxis(high, 0, axis), np.moveaxis(low, 0, axis)


def parts(values):
    high = values.astype(BF16)
    return high, (values - high.astype(F32)).astype(BF16)


def dot(a, b):
    return jnp.dot(a, b, preferred_element_type=F32)


def exact_dot(a, b):
    return jnp.dot(a, b, precision=lax.Precision.HIGHEST, preferred_element_type=F32)


def upward_dot(values, table_ref):
    high, low = parts(values)
    return dot(jnp.concatenate([high, low, high], axis=1), table_ref[...])


def north_dot(table_ref, values):
    north = values.shape[0]
    solved = dot(table_ref[...], jnp.concatenate(parts(values), axis=0))
    return solved[:north] + solved[north:]


def pick(column, me):
    value = float(column[0])
    for k in range(1, len(column)):
        value = jnp.where(me == k, float(column[k]), value)
    return value


def send_all(ends, table, me, out_refs):
    for d, out_ref in enumerate(out_refs):
        out_ref[...] = pick(table[:, 2 * d], me) * ends[0] + pick(table[:, 2 * d + 1], me) * ends[1]


def take_all(ends, table, me, messages):
    left = right = 0.0
    for d, message in enumerate(messages):
        left += pick(table[:, 8 + 2 * d], me) * message
        right += pick(table[:, 9 + 2 * d], me) * message
    known = (left, right) + tuple(ends)
    return [sum(pick(table[:, 4 * side + k], me) * known[k] for k in range(4)) for side in range(2)]


def diagonal(size):
    return lax.broadcasted_iota(jnp.int32, (size, size), 0) == lax.broadcasted_iota(jnp.int32, (size, size), 1)


def as_row(column):
    return jnp.sum(jnp.where(diagonal(column.shape[0]), column, 0.0), axis=0, keepdims=True)


def as_column(row):
    return jnp.sum(jnp.where(diagonal(row.shape[1]), row, 0.0), axis=1, keepdims=True)


def stacked(rows, height):
    filler = jnp.zeros((height - sum(row.shape[0] for row in rows), rows[0].shape[1]), F32)
    return jnp.concatenate(list(rows) + [filler], axis=0)


def ordered(pair, east):
    if not pair:
        return lambda i: i
    flip = lax.axis_index("gx")
    return lambda i: jnp.where(flip == 0, i, east - 1 - i)


def end_places(count, east):
    if count == 1:
        return [(east - 1, 0)]
    return [(0, 0), (east - 1, 1)]


def local_kernel(
    pair, group, factors, sending,
    tables_hbm, warmth_hbm, supply_hbm,
    swept_ref, warmth_ref, upward_ends_ref, north_ends_ref, east_ends_ref, *rest,
):
    to_up, to_north = (table.shape[1] // 2 for table in sending)
    up_refs, north_refs = rest[:to_up], rest[to_up : to_up + to_north]
    supply_ref, both_ref, edges_ref, tables_ref, up_ref, north_ref, sems = rest[to_up + to_north :]
    east, north, upward = supply_ref.shape
    groups = east // group
    count = east_ends_ref.shape[0]
    place = ordered(pair, east)

    def fetch(which, g):
        start = jnp.minimum(place(g * group), place(g * group + group - 1))
        block = pl.ds(start, group)
        if which == 0:
            return pltpu.make_async_copy(warmth_hbm.at[block], warmth_ref.at[pl.ds(start + 1, group)], sems.at[0, g])
        return pltpu.make_async_copy(supply_hbm.at[block], supply_ref.at[block], sems.at[1, g])

    tables = pltpu.make_async_copy(tables_hbm, tables_ref, sems.at[0, groups])
    tables.start()
    for g in range(groups):
        for which in range(2):
            fetch(which, g).start()
    warmth_ref[0] = jnp.zeros((north, upward), F32)
    warmth_ref[east + 1] = jnp.zeros((north, upward), F32)
    both_ref[...] = jnp.zeros_like(both_ref)
    east_ends_ref[...] = jnp.zeros_like(east_ends_ref)
    lane = lax.broadcasted_iota(jnp.int32, (1, 2 * east), 1)
    line = lax.broadcasted_iota(jnp.int32, (north, 1), 0)
    tables.wait()
    up_ref[...] = tables_ref[: 3 * upward].astype(BF16)
    north_ref[...] = tables_ref[3 * upward : 3 * upward + 2 * north, : 2 * north].astype(BF16)
    sweep = 3 * upward + 2 * north
    fetch(0, 0).wait()

    def body(g, _):
        fetch(1, g).wait()

        @pl.when(g + 1 < groups)
        def _():
            fetch(0, g + 1).wait()

        warm_list, heat_list = [], []
        for k in range(group):
            i = g * group + k
            x = place(i)
            warm = warmth_ref[x + 1]
            bent = (warmth_ref[x] - warm) + (warmth_ref[x + 2] - warm)
            low = jnp.where(line == 0, 0.0, pltpu.roll(warm, 1, 0))
            high = jnp.where(line == north - 1, 0.0, pltpu.roll(warm, north - 1, 0))
            bent += (factors[1] / factors[0]) * ((low - warm) + (high - warm))
            heat_list.append((supply_ref[x] + 2.0 * warm) + factors[0] * bent)
            warm_list.append(warm)
            edges_ref[pl.ds(i, 1)] = warm[:1]
            edges_ref[pl.ds(east + i, 1)] = warm[north - 1 :]
        solved_up = upward_dot(jnp.concatenate(heat_list, axis=0), up_ref)
        for k in range(group):
            i = g * group + k
            first = solved_up[k * north : (k + 1) * north]
            heads = pltpu.roll(first[:, : 2 * east], i, 1)
            tails = pltpu.roll(first[:, upward - 2 * east :], east + 1 + i, 1)
            both = jnp.where(lane == i, heads, both_ref[...])
            both_ref[...] = jnp.where(lane == east + i, tails, both)
            solved = north_dot(north_ref, first - 2.0 * warm_list[k])
            north_ends_ref[0, pl.ds(i, 1), :] = solved[:1]
            north_ends_ref[1, pl.ds(i, 1), :] = solved[north - 1 :]
            scale, ratio = (tables_ref[pl.ds(sweep + n * east + i, 1), :] for n in range(2))
            swept = scale * solved + ratio * east_ends_ref[count - 1]
            swept_ref[i] = swept
            east_ends_ref[count - 1] = swept
            if not pair:
                east_ends_ref[0] += tables_ref[pl.ds(sweep + 2 * east + i, 1), :] * swept
        return 0

    lax.fori_loop(0, groups, body, 0)

    ends = end_places(count, east)
    planes = [warmth_ref[place(i) + 1] for i, _ in ends]
    solved_up = upward_dot(jnp.concatenate([edges_ref[...]] + planes, axis=0), up_ref)
    height = north_ends_ref.shape[1]
    rows = [[], []]
    for p in range(count):
        solved = north_dot(north_ref, solved_up[2 * east + p * north : 2 * east + (p + 1) * north])
        rows[0].append(solved[:1])
        rows[1].append(solved[north - 1 :])
        east_ends_ref[p] += 2.0 * solved
    north_ends = []
    for end in range(2):
        north_ends_ref[end, :east] += 2.0 * solved_up[end * east : (end + 1) * east]
        north_ends_ref[end, east:] = stacked(rows[end], height - east)
        north_ends.append(north_ends_ref[end])
    send_all(north_ends, sending[1], lax.axis_index("gy"), north_refs)

    half = north // 2
    top, bottom = both_ref[:half], both_ref[half:]
    folded = (
        jnp.where(lane < east, top, pltpu.roll(bottom, east, 1)),
        jnp.where(lane < east, pltpu.roll(top, east, 1), bottom),
    )
    upward_ends = []
    for end, column in enumerate((slice(0, 1), slice(upward - 1, upward))):
        extra = [as_row(solved_up[k * north : (k + 1) * north, column]) for k in range(1 + count)]
        upward_ends.append(stacked([folded[end]] + extra, upward_ends_ref.shape[1]))
        upward_ends_ref[end] = upward_ends[end]
    send_all(upward_ends, sending[0], lax.axis_index("gz"), up_refs)


def upward_kernel(
    count, taking, sending,
    ends_ref, north_inverse_ref, east_twice_ref, *rest,
):
    taken = (taking.shape[1] - 8) // 2
    message_refs = rest[:taken]
    columns_ref, tiny_ref, plane_ref, *out_refs = rest[taken:]
    north, lanes = columns_ref.shape
    east, half = lanes // 2, north // 2
    lane = lax.broadcasted_iota(jnp.int32, (1, lanes), 1)
    before, after = take_all(
        (ends_ref[0], ends_ref[1]), taking, lax.axis_index("gz"), [ref[...] for ref in message_refs]
    )

    def paired(end, rows):
        if end == 0:
            return jnp.where(lane < east, before[rows], pltpu.roll(after[rows], east, 1))
        return jnp.where(lane < east, pltpu.roll(before[rows], east, 1), after[rows])

    solved = exact_dot(north_inverse_ref[...], jnp.concatenate([paired(0, slice(0, half)), paired(1, slice(0, half))], axis=0))
    columns = exact_dot(solved, east_twice_ref[...])
    columns_ref[...] = columns
    planes = []
    for p in range(count):
        row = slice(half + 1 + p, half + 2 + p)
        planes.append([
            jnp.sum(north_inverse_ref[...] * side[row], axis=1, keepdims=True) for side in (before, after)
        ])
    tiny = []
    for end, y in enumerate((0, north - 1)):
        first = solved[y : y + 1] + 2.0 * paired(end, slice(half, half + 1))
        second = jnp.zeros((1, lanes), F32)
        for p in range(count):
            for side in range(2):
                second = jnp.where(lane == side * east + p, planes[p][side][y : y + 1], second)
        tiny.append(stacked([first, second], 8))
        tiny_ref[end] = tiny[end]
    send_all(tiny, sending, lax.axis_index("gy"), out_refs)
    for p, (i, _) in enumerate(end_places(count, east)):
        rows = []
        for side in range(2):
            column = columns[:, side * east + i : side * east + i + 1] + 2.0 * planes[p][side]
            rows.append(as_row(column))
        plane_ref[p] = stacked(rows, 8)


def north_kernel(
    count, taking,
    ends_ref, tiny_ref, plane_ref, east_inverse_ref, spread_ref, *rest,
):
    taken = (taking.shape[1] - 8) // 2
    message_refs, tiny_refs = rest[:taken], rest[taken : 2 * taken]
    rows_ref, small_ref = rest[2 * taken :]
    _, east, upward = rows_ref.shape
    height = ends_ref.shape[1]
    me = lax.axis_index("gy")
    sides = take_all((ends_ref[0], ends_ref[1]), taking, me, [ref[...] for ref in message_refs])
    tiny = take_all((tiny_ref[0], tiny_ref[1]), taking, me, [ref[...] for ref in tiny_refs])
    shape = (height, 2 * east)
    row = lax.broadcasted_iota(jnp.int32, shape, 0)
    lane = lax.broadcasted_iota(jnp.int32, shape, 1) % east
    own = (row < east) & (lane == row)
    behind = (row >= east) & (row < east + count) & (lane == row - east)
    picked = [jnp.where(own, side[:1], 0.0) + jnp.where(behind, side[1:2], 0.0) for side in tiny]
    added = exact_dot(jnp.concatenate(picked, axis=0), spread_ref[...])
    sides = [side + added[n * height : (n + 1) * height] for n, side in enumerate(sides)]
    swept = [exact_dot(east_inverse_ref[...], side[:east]) for side in sides]
    for n in range(2):
        rows_ref[n] = swept[n]
    for p, (i, k) in enumerate(end_places(count, east)):
        rows = [swept[n][i : i + 1] + 2.0 * sides[n][east + k : east + k + 1] for n in range(2)]
        wide = jnp.concatenate([plane_ref[p], jnp.zeros((8, upward - plane_ref.shape[2]), F32)], axis=1)
        small_ref[p] = stacked(rows + [wide[:2]], 8)


def final_kernel(
    pair, table, tile,
    sweep_ref, own_ref, other_ref, own_small_ref, other_small_ref,
    swept_ref, warmth_ref, columns_ref, rows_ref, upward_spikes_ref, north_spikes_ref,
    out_hbm,
    out_ref, sides_ref, sems,
):
    east, north, upward = out_ref.shape
    place = ordered(pair, east)

    def widened(plane, small):
        for side in range(2):
            plane += north_spikes_ref[side] * small[side : side + 1]
            plane += as_column(small[2 + side : 3 + side, :north]) * upward_spikes_ref[side : side + 1, :]
        return plane

    if pair:
        near, far = float(table[0]), float(table[1])
        sides_ref[0] = widened(
            near * other_ref[0] + far * own_ref[0], near * other_small_ref[0] + far * own_small_ref[0]
        )
    else:
        me = lax.axis_index("gx")
        members = table.shape[0]
        for side in range(2):
            plane, small = 0.0, 0.0
            for m in range(members):
                for end in range(2):
                    weight = pick(table[:, side, 2 * m + end], me)
                    plane += weight * other_ref[m, end]
                    small += weight * other_small_ref[m, end]
            sides_ref[side] = widened(plane, small)
    last = sides_ref.shape[0] - 1

    def send(t):
        block = pl.ds(pl.multiple_of(t * tile, tile), tile)
        return pltpu.make_async_copy(out_ref.at[:, block], out_hbm.at[:, block], sems.at[t])

    def body(t, _):
        block = pl.ds(pl.multiple_of(t * tile, tile), tile)
        value = sides_ref[last, block]
        columns = columns_ref[block]
        first_spike, last_spike = north_spikes_ref[0, block], north_spikes_ref[1, block]
        for i in reversed(range(east)):
            value = swept_ref[i, block] + sweep_ref[1, i] * value
            if not pair:
                value += sweep_ref[3, i] * sides_ref[0, block]
            added = (
                columns[:, i : i + 1] * upward_spikes_ref[0:1, :]
                + columns[:, east + i : east + i + 1] * upward_spikes_ref[1:2, :]
            )
            added += first_spike * rows_ref[0, i : i + 1, :] + last_spike * rows_ref[1, i : i + 1, :]
            x = place(i)
            out_ref[x, block] = warmth_ref[x + 1, block] + value + added
        send(t).start()
        return 0

    lax.fori_loop(0, north // tile, body, 0)
    for t in range(north // tile):
        send(t).wait()


def spread_out(messages, axis):
    members = lax.axis_size(axis)
    return [
        lax.ppermute(message, axis, [(k, peers(k, members, d + 1)[0]) for k in range(members)])
        for d, message in enumerate(messages)
    ]


def local(initial_warmth, heat_supply):
    shape = east, north, upward = initial_warmth.shape
    members = [lax.axis_size(axis) for axis in ("gx", "gy", "gz")]
    factors = [float((n * m) ** 2 // 4) for n, m in zip(shape, members)]
    lines = [line_tables(n, factor) for n, factor in zip(shape, factors)]
    sweep = sweep_table(east, factors[0]).astype(np.float32)
    exchanges = [exchange_tables(line[1], line[2], m) for line, m in zip(lines, members)]
    upward_high, upward_low = split(lines[2][0], 0)
    north_high, north_low = split(lines[1][0], 1)
    north_stack = np.block([[north_high, north_high], [north_low, np.zeros_like(north_low)]])
    tables = np.concatenate([
        np.concatenate([upward_high, upward_high, upward_low]).astype(np.float32),
        np.pad(north_stack.astype(np.float32), ((0, 0), (0, max(upward - 2 * north, 0)))),
        np.repeat(sweep.reshape(-1, 1), upward, axis=1),
    ])
    east_inverse = lines[0][0].astype(np.float32)
    north_inverse = lines[1][0].astype(np.float32)
    east_twice = np.kron(np.eye(2), lines[0][0]).astype(np.float32)
    upward_spikes = np.stack(lines[2][1:]).astype(np.float32)
    spread = np.repeat(upward_spikes, east, axis=0)
    north_spikes = np.broadcast_to(np.stack(lines[1][1:])[:, :, None], (2, north, upward)).astype(np.float32)

    pair = members[0] == 2
    count = 1 if pair else 2
    height = east + 8
    to_up, to_north = members[2] - 1, members[1] - 1
    vmem = pl.BlockSpec(memory_space=pltpu.VMEM)
    smem = pl.BlockSpec(memory_space=pltpu.SMEM)
    hbm = pl.BlockSpec(memory_space=pltpu.HBM)

    def kept(*sizes):
        return jax.ShapeDtypeStruct(sizes, F32)

    group = 4
    folded = kept(north // 2 + 8, 2 * east)
    swept, warmth, upward_ends, north_ends, own, *messages = pl.pallas_call(
        functools.partial(local_kernel, pair, group, factors, (exchanges[2][0], exchanges[1][0])),
        in_specs=[hbm] * 3,
        out_specs=[vmem] * (5 + to_up + to_north),
        out_shape=[
            pltpu.VMEM(shape, F32),
            pltpu.VMEM((east + 2, north, upward), F32),
            kept(2, *folded.shape),
            kept(2, height, upward),
            kept(count, north, upward),
        ]
        + [folded] * to_up
        + [kept(height, upward)] * to_north,
        scratch_shapes=[
            pltpu.VMEM(shape, F32),
            pltpu.VMEM((north, 2 * east), F32),
            pltpu.VMEM((2 * east, upward), F32),
            pltpu.VMEM(tables.shape, F32),
            pltpu.VMEM((3 * upward, upward), BF16),
            pltpu.VMEM((2 * north, 2 * north), BF16),
            pltpu.SemaphoreType.DMA((2, east // group + 1)),
        ],
        compiler_params=pltpu.CompilerParams(vmem_limit_bytes=32 * MIB),
    )(tables, initial_warmth, heat_supply)

    up_messages = spread_out(messages[:to_up], "gz")
    north_messages = spread_out(messages[to_up:], "gy")
    if pair:
        other = lax.ppermute(own, "gx", [(0, 1), (1, 0)])
    else:
        other = lax.all_gather(own, "gx")
    columns, tiny, planes, *messages = pl.pallas_call(
        functools.partial(upward_kernel, count, exchanges[2][1], exchanges[1][0]),
        in_specs=[vmem] * (3 + to_up),
        out_specs=[vmem] * (3 + to_north),
        out_shape=[kept(north, 2 * east), kept(2, 8, 2 * east), kept(count, 8, north)]
        + [kept(8, 2 * east)] * to_north,
        compiler_params=pltpu.CompilerParams(vmem_limit_bytes=6 * MIB),
    )(upward_ends, north_inverse, east_twice, *up_messages)

    tiny_messages = spread_out(messages, "gy")
    rows, own_small = pl.pallas_call(
        functools.partial(north_kernel, count, exchanges[1][1]),
        in_specs=[vmem] * (5 + 2 * to_north),
        out_specs=[vmem] * 2,
        out_shape=[kept(2, east, upward), kept(count, 8, upward)],
        compiler_params=pltpu.CompilerParams(vmem_limit_bytes=6 * MIB),
    )(north_ends, tiny, planes, east_inverse, spread, *north_messages, *tiny_messages)

    if pair:
        other_small = lax.ppermute(own_small, "gx", [(0, 1), (1, 0)])
        near = lines[0][1][0]
        table = np.array([1.0, near]) / (1.0 - near**2)
    else:
        other_small = lax.all_gather(own_small, "gx")
        table = interface_table(lines[0][1], lines[0][2], members[0])
    swept = pltpu.with_memory_space_constraint(swept, pltpu.VMEM)
    warmth = pltpu.with_memory_space_constraint(warmth, pltpu.VMEM)
    tile = 32
    return pl.pallas_call(
        functools.partial(final_kernel, pair, table, tile),
        in_specs=[smem] + [vmem] * 10,
        out_specs=hbm,
        out_shape=kept(*shape),
        scratch_shapes=[
            pltpu.VMEM(shape, F32),
            pltpu.VMEM((count, north, upward), F32),
            pltpu.SemaphoreType.DMA((north // tile,)),
        ],
        compiler_params=pltpu.CompilerParams(vmem_limit_bytes=16 * MIB),
    )(sweep, own, other, own_small, other_small, swept, warmth, columns, rows, upward_spikes, north_spikes)


def solution(mesh):
    return jax.shard_map(
        local,
        mesh=mesh,
        in_specs=(P("gx", "gy", "gz"), P("gx", "gy", "gz")),
        out_specs=P("gx", "gy", "gz"),
        check_vma=False,
    )
```

time: 53.3 us -> 53.3 us (level)
  starting transfers between devices: 9.21 us -> 13.5 us
  local copies, waits for them, and re-layouts: 4.18 us -> 1.35 us
  Pallas kernels: 25.4 us -> 24.6 us
    ppermute x1, waiting for transfers between devices: 3.99 us -> 0.01 us  [local(): other = lax.ppermute(own, 'gx', [(0, 1), (1, 0)])]
    ppermute x0 -> x1, waiting for transfers between devices: none -> 3.14 us  [local(): other_small = lax.ppermute(own_small, 'gx', [(0, 1), (1, 0)])]
    unnamed x30 -> x16, local copies, waits for them, and re-layouts: 4.18 us -> 1.35 us
    ppermute x6 -> x9, starting transfers between devices: 7.61 us -> 9.84 us  [spread_out(): lax.ppermute(message, axis, [(k, peers(k, members, d + 1)[0]) for k in ra...]
    ppermute x1, starting transfers between devices: 1.6 us -> 3.03 us  [local(): other = lax.ppermute(own, 'gx', [(0, 1), (1, 0)])]
    pallas_call x4, Pallas kernels: 25.4 us -> 24.6 us  [the longest x1 17.5 us: local(): pl.pallas_call(functools.partial(local_kernel, pair, group, factors, (exc...]
    ppermute x0 -> x1, starting transfers between devices: none -> 0.57 us  [local(): other_small = lax.ppermute(own_small, 'gx', [(0, 1), (1, 0)])]
    ppermute x6 -> x9, waiting for transfers between devices: 10.3 us -> 10.5 us  [spread_out(): lax.ppermute(message, axis, [(k, peers(k, members, d + 1)[0]) for k in ra...]
  transfers between devices with their start and end apart: 7 -> 11, of which waited for: 5 -> 6; matrix products, arithmetic and copies ran while one was open for 0% -> 0% of each run, Pallas kernels for 0% -> 2%
where the time goes in v3:
time: 53.3 us; the launch traced here: 53.2 us
  Pallas kernels  24.6 us (46%)
  waiting for transfers between devices  13.7 us (26%)
  starting transfers between devices  13.5 us (25%)
  local copies, waits for them, and re-layouts  1.35 us (3%)
    pallas_call x1, Pallas kernels, local(): pl.pallas_call(functools.partial(local_kernel, pair, group, factors, (exc...  17.5 us
    ppermute x9, waiting for transfers between devices, spread_out(): lax.ppermute(message, axis, [(k, peers(k, members, d + 1)[0]) for k in ra...  10.5 us
    ppermute x9, starting transfers between devices, spread_out(): lax.ppermute(message, axis, [(k, peers(k, members, d + 1)[0]) for k in ra...  9.84 us
    pallas_call x1, Pallas kernels, local(): pl.pallas_call(functools.partial(final_kernel, pair, table, tile), in_spe...  5.78 us
    ppermute x1, waiting for transfers between devices, local(): other_small = lax.ppermute(own_small, 'gx', [(0, 1), (1, 0)])  3.14 us
    ppermute x1, starting transfers between devices, local(): other = lax.ppermute(own, 'gx', [(0, 1), (1, 0)])  3.03 us
    unnamed x16, local copies, waits for them, and re-layouts  1.35 us
  transfers between devices with their start and end apart: 11, of which 6 were waited for; matrix products, arithmetic and copies ran while one was open for 0% of the time, Pallas kernels for 2%

profile of v3, /device:TPU:0, one launch (start us, length us, event | category | flops | bytes accessed | tf_op | source)
XLA Modules:
  0.0 53.2 jit_solution(17743382592815394992)
XLA Ops:
  0.0 0.0 copy-start
  0.0 1.3 %copy-done = f32[1280,256]{1,0:T(8,128)S(1)} copy-done((f32[1280,256]{1,0:T(8,128)S(1)}, f32[1280,256]{1,0:T(8,128)}, u32[]{:S(2)}) %copy-start) | copy-done | bytes 1310744
  1.3 0.0 copy-start.3
  1.3 0.0 copy-start.4
  1.3 0.0 copy-start.2
  1.3 0.0 copy-start.5
  1.3 0.0 copy-start.1
  1.3 0.0 copy-start.6
  1.4 0.0 copy-start.7
  1.4 17.5 %shard_map.100 = (f32[64,128,256]{2,1,0:T(8,128)S(1)}, f32[66,128,256]{2,1,0:T(8,128)S(1)}, f32[2,72,128]{2,1,0:T(8,128)S(1)}, f32[2,72,256]{2,1,0:T(8,128)S(1)}...) custom-call(f32[1280,256]{1,0:T(8,128)S(1)} %copy-done, ...), custom_call_target="tpu_custom_call" | custom-call | tf_op jit(solution)/shard_map/pallas_call | solution.py:475
  18.9 3.0 %collective-permute-start = (f32[1,128,256]{2,1,0:T(8,128)S(1)}, f32[1,128,256]{2,1,0:T(8,128)S(1)}, u32[]{:S(2)}, u32[]{:S(2)}) collective-permute-start(f32[1,128,256]{2,1,0:T(8,128)S(1)} %get-tuple-element.24.own_ref), channel_id=1, source_target_pairs={{0,16},{16,0},{1,17},{17,1},{2,18},{18,2},{3,19},{19,3},{4,20},{20... | collective-permute-start | bytes 393224 | tf_op jit(solution)/shard_map/ppermute | solution.py:503
  21.9 1.6 %collective-permute-start.1 = (f32[72,128]{1,0:T(8,128)S(1)}, f32[72,128]{1,0:T(8,128)S(1)}, u32[]{:S(2)}, u32[]{:S(2)}) collective-permute-start(f32[72,128]{1,0:T(8,128)S(1)} %get-tuple-element.27), channel_id=1, source_target_pairs={{0,1},{1,0},{2,3},{3,2},{4,5},{5,4},{6,7},{7,6},{8,9},{9,8},{10,11... | collective-permute-start | bytes 110600 | tf_op jit(solution)/shard_map/ppermute | solution.py:435
  23.5 2.6 %collective-permute-start.2 = (f32[72,128]{1,0:T(8,128)S(1)}, f32[72,128]{1,0:T(8,128)S(1)}, u32[]{:S(2)}, u32[]{:S(2)}) collective-permute-start(f32[72,128]{1,0:T(8,128)S(1)} %get-tuple-element.28), channel_id=1, source_target_pairs={{0,2},{1,3},{2,0},{3,1},{4,6},{5,7},{6,4},{7,5},{8,10},{9,11},{10,... | collective-permute-start | bytes 110600 | tf_op jit(solution)/shard_map/ppermute | solution.py:435
  26.1 0.0 collective-permute-start.4
  26.1 1.5 %collective-permute-start.5 = (f32[72,256]{1,0:T(8,128)S(1)}, f32[72,256]{1,0:T(8,128)S(1)}, u32[]{:S(2)}, u32[]{:S(2)}) collective-permute-start(f32[72,256]{1,0:T(8,128)S(1)} %get-tuple-element.33), channel_id=1, source_target_pairs={{0,8},{4,12},{8,0},{12,4},{1,9},{5,13},{9,1},{13,5},{2,10},{6,14},... | collective-permute-start | bytes 221192 | tf_op jit(solution)/shard_map/ppermute | solution.py:435
  27.6 0.0 collective-permute-done.1.rest_0_
  27.6 0.4 collective-permute-start.6
  27.9 0.7 %collective-permute-done.2.rest_1_ = f32[72,128]{1,0:T(8,128)S(1)} collective-permute-done((f32[72,128]{1,0:T(8,128)S(1)}, f32[72,128]{1,0:T(8,128)S(1)}, u32[]{:S(2)}, u32[]{:S(2)}) %collective-permute-start.2) | collective-permute-done | bytes 36896 | tf_op jit(solution)/shard_map/ppermute | solution.py:435
  28.7 2.1 %collective-permute-start.3 = (f32[72,128]{1,0:T(8,128)S(1)}, f32[72,128]{1,0:T(8,128)S(1)}, u32[]{:S(2)}, u32[]{:S(2)}) collective-permute-start(f32[72,128]{1,0:T(8,128)S(1)} %get-tuple-element.29), channel_id=1, source_target_pairs={{0,3},{1,2},{2,1},{3,0},{4,7},{5,6},{6,5},{7,4},{8,11},{9,10},{10,... | collective-permute-start | bytes 110600 | tf_op jit(solution)/shard_map/ppermute | solution.py:435
  30.8 3.6 %collective-permute-done.3.rest_2_ = f32[72,128]{1,0:T(8,128)S(1)} collective-permute-done((f32[72,128]{1,0:T(8,128)S(1)}, f32[72,128]{1,0:T(8,128)S(1)}, u32[]{:S(2)}, u32[]{:S(2)}) %collective-permute-start.3) | collective-permute-done | bytes 36896 | tf_op jit(solution)/shard_map/ppermute | solution.py:435
  34.4 0.0 copy-done.3
  34.4 0.0 copy-done.4
  34.4 0.6 %shard_map.101 = (f32[128,128]{1,0:T(8,128)S(1)}, f32[2,8,128]{2,1,0:T(8,128)S(1)}, f32[1,8,128]{2,1,0:T(8,128)S(1)}, f32[8,128]{1,0:T(8,128)S(1)}, f32[8,128]{1,0:T(8,128)S(1)}, /*index=5*/f32[8,128]{1,0:T(8,128)S(1)}) custom-call(f32[2,72,128]{2,1,0:T(8,128)S(1)} %get-tuple-element.26.ends_ref, f32[128,128]{1,0:T(8,128)S(1)} %copy-done.4, ...), custom_call_target="tpu_custom_call" | custom-call | tf_op jit(solution)/shard_map/pallas_call | solution.py:506
  35.1 0.1 collective-permute-start.7
  35.2 1.2 %collective-permute-done.7.rest_3_ = f32[8,128]{1,0:T(8,128)S(1)} collective-permute-done((f32[8,128]{1,0:T(8,128)S(1)}, f32[8,128]{1,0:T(8,128)S(1)}, u32[]{:S(2)}, u32[]{:S(2)}) %collective-permute-start.7) | collective-permute-done | bytes 4128 | tf_op jit(solution)/shard_map/ppermute | solution.py:435
  36.3 1.5 %collective-permute-start.8 = (f32[8,128]{1,0:T(8,128)S(1)}, f32[8,128]{1,0:T(8,128)S(1)}, u32[]{:S(2)}, u32[]{:S(2)}) collective-permute-start(f32[8,128]{1,0:T(8,128)S(1)} %get-tuple-element.36), channel_id=1, source_target_pairs={{0,8},{4,12},{8,0},{12,4},{1,9},{5,13},{9,1},{13,5},{2,10},{6,14},... | collective-permute-start | bytes 12296 | tf_op jit(solution)/shard_map/ppermute | solution.py:435
  37.8 2.1 %collective-permute-done.8.rest_4_ = f32[8,128]{1,0:T(8,128)S(1)} collective-permute-done((f32[8,128]{1,0:T(8,128)S(1)}, f32[8,128]{1,0:T(8,128)S(1)}, u32[]{:S(2)}, u32[]{:S(2)}) %collective-permute-start.8) | collective-permute-done | bytes 4128 | tf_op jit(solution)/shard_map/ppermute | solution.py:435
  39.9 0.1 collective-permute-start.9
  40.0 2.9 %collective-permute-done.9.rest_5_ = f32[8,128]{1,0:T(8,128)S(1)} collective-permute-done((f32[8,128]{1,0:T(8,128)S(1)}, f32[8,128]{1,0:T(8,128)S(1)}, u32[]{:S(2)}, u32[]{:S(2)}) %collective-permute-start.9) | collective-permute-done | bytes 4128 | tf_op jit(solution)/shard_map/ppermute | solution.py:435
  43.0 0.0 collective-permute-done.4.rest_0_
  43.0 0.0 collective-permute-done.5.rest_1_
  43.0 0.0 collective-permute-done.6.rest_2_
  43.0 0.0 copy-done.2
  43.0 0.0 copy-done.5
  43.0 0.7 %shard_map.102 = (f32[2,64,256]{2,1,0:T(8,128)S(1)}, f32[1,8,256]{2,1,0:T(8,128)S(1)}) custom-call(f32[2,72,256]{2,1,0:T(8,128)S(1)} %get-tuple-element.25.ends_ref, f32[2,8,128]{2,1,0:T(8,128)S(1)} %get-tuple-element.30.tiny_ref, f32[1,8,128]{2,1,0:T(8,128)S(1)} %get-tuple-element.31.plane_ref, f32[64,64]{1,0:T(8,128)S(1)} %copy-done.5, ...), custom_call_target="tpu_custom_call" | custom-call | tf_op jit(solution)/shard_map/pallas_call | solution.py:516
  43.7 0.6 %collective-permute-start.10 = (f32[1,8,256]{2,1,0:T(8,128)S(1)}, f32[1,8,256]{2,1,0:T(8,128)S(1)}, u32[]{:S(2)}, u32[]{:S(2)}) collective-permute-start(f32[1,8,256]{2,1,0:T(8,128)S(1)} %get-tuple-element.38.own_small_ref), channel_id=1, source_target_pairs={{0,16},{16,0},{1,17},{17,1},{2,18},{18,2},{3,19},{19,3},{4,20},{20... | collective-permute-start | bytes 24584 | tf_op jit(solution)/shard_map/ppermute | solution.py:525
  44.2 3.1 %collective-permute-done.10.other_small_ref = f32[1,8,256]{2,1,0:T(8,128)S(1)} collective-permute-done((f32[1,8,256]{2,1,0:T(8,128)S(1)}, f32[1,8,256]{2,1,0:T(8,128)S(1)}, u32[]{:S(2)}, u32[]{:S(2)}) %collective-permute-start.10) | collective-permute-done | bytes 8224 | tf_op jit(solution)/shard_map/ppermute | solution.py:525
  47.4 0.0 collective-permute-done.other_ref
  47.4 0.0 copy-done.1
  47.4 0.0 copy-done.6
  47.4 0.0 copy-done.7
  47.4 5.8 %shard_map.103 = f32[64,128,256]{2,1,0:T(8,128)} custom-call(f32[4,64]{1,0:T(4,128)S(1)} %copy-done.7, f32[1,128,256]{2,1,0:T(8,128)S(1)} %get-tuple-element.24.own_ref, f32[1,128,256]{2,1,0:T(8,128)S(1)} %collective-permute-done.other_ref, f32[1,8,256]{2,1,0:T(8,128)S(1)} %get-tuple-element.38.own_small_ref, ...), custom_call_target="tpu_custom_call" | custom-call | tf_op jit(solution)/shard_map/pallas_call | solution.py:534
Async XLA Ops:
  0.0 1.3 %copy-start = (f32[1280,256]{1,0:T(8,128)S(1)}, f32[1280,256]{1,0:T(8,128)}, u32[]{:S(2)}) copy-start(f32[1280,256]{1,0:T(8,128)} %constant.16.clone.tables_hbm) | copy-start | bytes 3932164
  1.3 33.1 %copy-start.3 = (f32[128,128]{1,0:T(8,128)S(1)}, f32[128,128]{1,0:T(8,128)}, u32[]{:S(2)}) copy-start(f32[128,128]{1,0:T(8,128)} %constant.18.clone.east_twice_ref) | copy-start | bytes 196612
  1.3 33.1 %copy-start.4 = (f32[128,128]{1,0:T(8,128)S(1)}, f32[128,128]{1,0:T(8,128)}, u32[]{:S(2)}) copy-start(f32[128,128]{1,0:T(8,128)} %constant.17.clone.north_inverse_ref) | copy-start | bytes 196612
  1.3 41.6 %copy-start.2 = (f32[128,256]{1,0:T(8,128)S(1)}, f32[128,256]{1,0:T(8,128)}, u32[]{:S(2)}) copy-start(f32[128,256]{1,0:T(8,128)} %constant.20.clone.spread_ref) | copy-start | bytes 393220
  1.3 41.7 %copy-start.5 = (f32[64,64]{1,0:T(8,128)S(1)}, f32[64,64]{1,0:T(8,128)}, u32[]{:S(2)}) copy-start(f32[64,64]{1,0:T(8,128)} %constant.19.clone.east_inverse_ref) | copy-start | bytes 49156
  1.3 46.0 %copy-start.1 = (f32[2,128,256]{2,1,0:T(8,128)S(1)}, f32[2,128,256]{2,1,0:T(8,128)}, u32[]{:S(2)}) copy-start(f32[2,128,256]{2,1,0:T(8,128)} %constant.23.clone.north_spikes_ref) | copy-start | bytes 786436
  1.3 46.0 %copy-start.6 = (f32[2,256]{1,0:T(2,128)S(1)}, f32[2,256]{1,0:T(2,128)}, u32[]{:S(2)}) copy-start(f32[2,256]{1,0:T(2,128)} %constant.22.clone.upward_spikes_ref) | copy-start | bytes 6148
  1.4 46.0 %copy-start.7 = (f32[4,64]{1,0:T(4,128)S(1)}, f32[4,64]{1,0:T(4,128)}, u32[]{:S(2)}) copy-start(f32[4,64]{1,0:T(4,128)} %constant.21.clone.sweep_ref) | copy-start | bytes 3076
  18.9 28.5 %collective-permute-start = (f32[1,128,256]{2,1,0:T(8,128)S(1)}, f32[1,128,256]{2,1,0:T(8,128)S(1)}, u32[]{:S(2)}, u32[]{:S(2)}) collective-permute-start(f32[1,128,256]{2,1,0:T(8,128)S(1)} %get-tuple-element.24.own_ref), channel_id=1, source_target_pairs={{0,16},{16,0},{1,17},{17,1},{2,18},{18,2},{3,19},{19,3},{4,20},{20... | collective-permute-start | bytes 393224 | tf_op jit(solution)/shard_map/ppermute | solution.py:503
  21.9 5.7 %collective-permute-start.1 = (f32[72,128]{1,0:T(8,128)S(1)}, f32[72,128]{1,0:T(8,128)S(1)}, u32[]{:S(2)}, u32[]{:S(2)}) collective-permute-start(f32[72,128]{1,0:T(8,128)S(1)} %get-tuple-element.27), channel_id=1, source_target_pairs={{0,1},{1,0},{2,3},{3,2},{4,5},{5,4},{6,7},{7,6},{8,9},{9,8},{10,11... | collective-permute-start | bytes 110600 | tf_op jit(solution)/shard_map/ppermute | solution.py:435
  23.5 5.2 %collective-permute-start.2 = (f32[72,128]{1,0:T(8,128)S(1)}, f32[72,128]{1,0:T(8,128)S(1)}, u32[]{:S(2)}, u32[]{:S(2)}) collective-permute-start(f32[72,128]{1,0:T(8,128)S(1)} %get-tuple-element.28), channel_id=1, source_target_pairs={{0,2},{1,3},{2,0},{3,1},{4,6},{5,7},{6,4},{7,5},{8,10},{9,11},{10,... | collective-permute-start | bytes 110600 | tf_op jit(solution)/shard_map/ppermute | solution.py:435
  26.1 16.9 %collective-permute-start.4 = (f32[72,256]{1,0:T(8,128)S(1)}, f32[72,256]{1,0:T(8,128)S(1)}, u32[]{:S(2)}, u32[]{:S(2)}) collective-permute-start(f32[72,256]{1,0:T(8,128)S(1)} %get-tuple-element.32), channel_id=1, source_target_pairs={{0,4},{4,0},{8,12},{12,8},{1,5},{5,1},{9,13},{13,9},{2,6},{6,2},{1... | collective-permute-start | bytes 221192 | tf_op jit(solution)/shard_map/ppermute | solution.py:435
  26.1 16.9 %collective-permute-start.5 = (f32[72,256]{1,0:T(8,128)S(1)}, f32[72,256]{1,0:T(8,128)S(1)}, u32[]{:S(2)}, u32[]{:S(2)}) collective-permute-start(f32[72,256]{1,0:T(8,128)S(1)} %get-tuple-element.33), channel_id=1, source_target_pairs={{0,8},{4,12},{8,0},{12,4},{1,9},{5,13},{9,1},{13,5},{2,10},{6,14},... | collective-permute-start | bytes 221192 | tf_op jit(solution)/shard_map/ppermute | solution.py:435
  27.6 15.4 %collective-permute-start.6 = (f32[72,256]{1,0:T(8,128)S(1)}, f32[72,256]{1,0:T(8,128)S(1)}, u32[]{:S(2)}, u32[]{:S(2)}) collective-permute-start(f32[72,256]{1,0:T(8,128)S(1)} %get-tuple-element.34), channel_id=1, source_target_pairs={{0,12},{4,8},{8,4},{12,0},{1,13},{5,9},{9,5},{13,1},{2,14},{6,10},... | collective-permute-start | bytes 221192 | tf_op jit(solution)/shard_map/ppermute | solution.py:435
  28.7 5.8 %collective-permute-start.3 = (f32[72,128]{1,0:T(8,128)S(1)}, f32[72,128]{1,0:T(8,128)S(1)}, u32[]{:S(2)}, u32[]{:S(2)}) collective-permute-start(f32[72,128]{1,0:T(8,128)S(1)} %get-tuple-element.29), channel_id=1, source_target_pairs={{0,3},{1,2},{2,1},{3,0},{4,7},{5,6},{6,5},{7,4},{8,11},{9,10},{10,... | collective-permute-start | bytes 110600 | tf_op jit(solution)/shard_map/ppermute | solution.py:435
  35.1 1.2 %collective-permute-start.7 = (f32[8,128]{1,0:T(8,128)S(1)}, f32[8,128]{1,0:T(8,128)S(1)}, u32[]{:S(2)}, u32[]{:S(2)}) collective-permute-start(f32[8,128]{1,0:T(8,128)S(1)} %get-tuple-element.35), channel_id=1, source_target_pairs={{0,4},{4,0},{8,12},{12,8},{1,5},{5,1},{9,13},{13,9},{2,6},{6,2},{1... | collective-permute-start | bytes 12296 | tf_op jit(solution)/shard_map/ppermute | solution.py:435
  36.3 3.6 %collective-permute-start.8 = (f32[8,128]{1,0:T(8,128)S(1)}, f32[8,128]{1,0:T(8,128)S(1)}, u32[]{:S(2)}, u32[]{:S(2)}) collective-permute-start(f32[8,128]{1,0:T(8,128)S(1)} %get-tuple-element.36), channel_id=1, source_target_pairs={{0,8},{4,12},{8,0},{12,4},{1,9},{5,13},{9,1},{13,5},{2,10},{6,14},... | collective-permute-start | bytes 12296 | tf_op jit(solution)/shard_map/ppermute | solution.py:435
  39.9 3.0 %collective-permute-start.9 = (f32[8,128]{1,0:T(8,128)S(1)}, f32[8,128]{1,0:T(8,128)S(1)}, u32[]{:S(2)}, u32[]{:S(2)}) collective-permute-start(f32[8,128]{1,0:T(8,128)S(1)} %get-tuple-element.37), channel_id=1, source_target_pairs={{0,12},{4,8},{8,4},{12,0},{1,13},{5,9},{9,5},{13,1},{2,14},{6,10},... | collective-permute-start | bytes 12296 | tf_op jit(solution)/shard_map/ppermute | solution.py:435
  43.7 3.7 %collective-permute-start.10 = (f32[1,8,256]{2,1,0:T(8,128)S(1)}, f32[1,8,256]{2,1,0:T(8,128)S(1)}, u32[]{:S(2)}, u32[]{:S(2)}) collective-permute-start(f32[1,8,256]{2,1,0:T(8,128)S(1)} %get-tuple-element.38.own_small_ref), channel_id=1, source_target_pairs={{0,16},{16,0},{1,17},{17,1},{2,18},{18,2},{3,19},{19,3},{4,20},{20... | collective-permute-start | bytes 24584 | tf_op jit(solution)/shard_map/ppermute | solution.py:525

commit v4 on v3

--- a/solution.py
+++ b/solution.py
@@ -161,10 +161,6 @@
     return jnp.sum(jnp.where(diagonal(column.shape[0]), column, 0.0), axis=0, keepdims=True)
 
 
-def as_column(row):
-    return jnp.sum(jnp.where(diagonal(row.shape[1]), row, 0.0), axis=1, keepdims=True)
-
-
 def stacked(rows, height):
     filler = jnp.zeros((height - sum(row.shape[0] for row in rows), rows[0].shape[1]), F32)
     return jnp.concatenate(list(rows) + [filler], axis=0)
@@ -188,9 +184,9 @@
     tables_hbm, warmth_hbm, supply_hbm,
     swept_ref, warmth_ref, upward_ends_ref, north_ends_ref, east_ends_ref, *rest,
 ):
-    to_up, to_north = (table.shape[1] // 2 for table in sending)
-    up_refs, north_refs = rest[:to_up], rest[to_up : to_up + to_north]
-    supply_ref, both_ref, edges_ref, tables_ref, up_ref, north_ref, sems = rest[to_up + to_north :]
+    to_up = sending.shape[1] // 2
+    up_refs = rest[:to_up]
+    supply_ref, both_ref, edges_ref, tables_ref, up_ref, north_ref, even_ref, odd_ref, sems = rest[to_up:]
     east, north, upward = supply_ref.shape
     groups = east // group
     count = east_ends_ref.shape[0]
@@ -220,14 +216,15 @@
     sweep = 3 * upward + 2 * north
     fetch(0, 0).wait()
 
-    def body(g, _):
+    def arrive(g):
         fetch(1, g).wait()
 
         @pl.when(g + 1 < groups)
         def _():
             fetch(0, g + 1).wait()
 
-        warm_list, heat_list = [], []
+    def upward_part(g, slot_ref):
+        heat_list = []
         for k in range(group):
             i = g * group + k
             x = place(i)
@@ -237,18 +234,19 @@
             high = jnp.where(line == north - 1, 0.0, pltpu.roll(warm, north - 1, 0))
             bent += (factors[1] / factors[0]) * ((low - warm) + (high - warm))
             heat_list.append((supply_ref[x] + 2.0 * warm) + factors[0] * bent)
-            warm_list.append(warm)
             edges_ref[pl.ds(i, 1)] = warm[:1]
             edges_ref[pl.ds(east + i, 1)] = warm[north - 1 :]
-        solved_up = upward_dot(jnp.concatenate(heat_list, axis=0), up_ref)
+        slot_ref[...] = upward_dot(jnp.concatenate(heat_list, axis=0), up_ref)
+
+    def north_part(g, slot_ref):
         for k in range(group):
             i = g * group + k
-            first = solved_up[k * north : (k + 1) * north]
+            first = slot_ref[k * north : (k + 1) * north]
             heads = pltpu.roll(first[:, : 2 * east], i, 1)
             tails = pltpu.roll(first[:, upward - 2 * east :], east + 1 + i, 1)
             both = jnp.where(lane == i, heads, both_ref[...])
             both_ref[...] = jnp.where(lane == east + i, tails, both)
-            solved = north_dot(north_ref, first - 2.0 * warm_list[k])
+            solved = north_dot(north_ref, first - 2.0 * warmth_ref[place(i) + 1])
             north_ends_ref[0, pl.ds(i, 1), :] = solved[:1]
             north_ends_ref[1, pl.ds(i, 1), :] = solved[north - 1 :]
             scale, ratio = (tables_ref[pl.ds(sweep + n * east + i, 1), :] for n in range(2))
@@ -257,9 +255,26 @@
             east_ends_ref[count - 1] = swept
             if not pair:
                 east_ends_ref[0] += tables_ref[pl.ds(sweep + 2 * east + i, 1), :] * swept
+
+    arrive(0)
+    upward_part(0, even_ref)
+
+    def body(j, _):
+        g = 2 * j
+        arrive(g + 1)
+        upward_part(g + 1, odd_ref)
+        north_part(g, even_ref)
+        later = jnp.minimum(g + 2, groups - 1)
+
+        @pl.when(g + 2 < groups)
+        def _():
+            arrive(g + 2)
+
+        upward_part(later, even_ref)
+        north_part(g + 1, odd_ref)
         return 0
 
-    lax.fori_loop(0, groups, body, 0)
+    lax.fori_loop(0, groups // 2, body, 0)
 
     ends = end_places(count, east)
     planes = [warmth_ref[place(i) + 1] for i, _ in ends]
@@ -271,12 +286,9 @@
         rows[0].append(solved[:1])
         rows[1].append(solved[north - 1 :])
         east_ends_ref[p] += 2.0 * solved
-    north_ends = []
     for end in range(2):
         north_ends_ref[end, :east] += 2.0 * solved_up[end * east : (end + 1) * east]
         north_ends_ref[end, east:] = stacked(rows[end], height - east)
-        north_ends.append(north_ends_ref[end])
-    send_all(north_ends, sending[1], lax.axis_index("gy"), north_refs)
 
     half = north // 2
     top, bottom = both_ref[:half], both_ref[half:]
@@ -289,16 +301,16 @@
         extra = [as_row(solved_up[k * north : (k + 1) * north, column]) for k in range(1 + count)]
         upward_ends.append(stacked([folded[end]] + extra, upward_ends_ref.shape[1]))
         upward_ends_ref[end] = upward_ends[end]
-    send_all(upward_ends, sending[0], lax.axis_index("gz"), up_refs)
+    send_all(upward_ends, sending, lax.axis_index("gz"), up_refs)
 
 
 def upward_kernel(
     count, taking, sending,
-    ends_ref, north_inverse_ref, east_twice_ref, *rest,
+    ends_ref, north_ends_ref, east_ends_ref, north_inverse_ref, east_twice_ref, spikes_ref, spread_ref, *rest,
 ):
     taken = (taking.shape[1] - 8) // 2
     message_refs = rest[:taken]
-    columns_ref, tiny_ref, plane_ref, *out_refs = rest[taken:]
+    columns_ref, north_out_ref, east_out_ref, *out_refs = rest[taken:]
     north, lanes = columns_ref.shape
     east, half = lanes // 2, north // 2
     lane = lax.broadcasted_iota(jnp.int32, (1, lanes), 1)
@@ -320,56 +332,56 @@
         planes.append([
             jnp.sum(north_inverse_ref[...] * side[row], axis=1, keepdims=True) for side in (before, after)
         ])
-    tiny = []
+    height = north_ends_ref.shape[1]
+    shape = (height, lanes)
+    row = lax.broadcasted_iota(jnp.int32, shape, 0)
+    short = lax.broadcasted_iota(jnp.int32, shape, 1) % east
+    own = (row < east) & (short == row)
+    behind = (row >= east) & (row < east + count) & (short == row - east)
+    picked = []
     for end, y in enumerate((0, north - 1)):
         first = solved[y : y + 1] + 2.0 * paired(end, slice(half, half + 1))
         second = jnp.zeros((1, lanes), F32)
-        for p in range(count):
+        for _, k in end_places(count, east):
             for side in range(2):
-                second = jnp.where(lane == side * east + p, planes[p][side][y : y + 1], second)
-        tiny.append(stacked([first, second], 8))
-        tiny_ref[end] = tiny[end]
-    send_all(tiny, sending, lax.axis_index("gy"), out_refs)
-    for p, (i, _) in enumerate(end_places(count, east)):
-        rows = []
+                second = jnp.where(lane == side * east + k, planes[k][side][y : y + 1], second)
+        picked.append(jnp.where(own, first, 0.0) + jnp.where(behind, second, 0.0))
+    added = exact_dot(jnp.concatenate(picked, axis=0), spread_ref[...])
+    ends = []
+    for end in range(2):
+        ends.append(north_ends_ref[end] + added[end * height : (end + 1) * height])
+        north_out_ref[end] = ends[end]
+    send_all(ends, sending, lax.axis_index("gy"), out_refs)
+    for i, k in end_places(count, east):
+        total = east_ends_ref[k]
         for side in range(2):
-            column = columns[:, side * east + i : side * east + i + 1] + 2.0 * planes[p][side]
-            rows.append(as_row(column))
-        plane_ref[p] = stacked(rows, 8)
+            column = columns[:, side * east + i : side * east + i + 1] + 2.0 * planes[k][side]
+            total += column * spikes_ref[side : side + 1, :]
+        east_out_ref[k] = total
 
 
 def north_kernel(
     count, taking,
-    ends_ref, tiny_ref, plane_ref, east_inverse_ref, spread_ref, *rest,
+    ends_ref, east_ends_ref, east_inverse_ref, spikes_ref, *rest,
 ):
     taken = (taking.shape[1] - 8) // 2
-    message_refs, tiny_refs = rest[:taken], rest[taken : 2 * taken]
-    rows_ref, small_ref = rest[2 * taken :]
-    _, east, upward = rows_ref.shape
-    height = ends_ref.shape[1]
-    me = lax.axis_index("gy")
-    sides = take_all((ends_ref[0], ends_ref[1]), taking, me, [ref[...] for ref in message_refs])
-    tiny = take_all((tiny_ref[0], tiny_ref[1]), taking, me, [ref[...] for ref in tiny_refs])
-    shape = (height, 2 * east)
-    row = lax.broadcasted_iota(jnp.int32, shape, 0)
-    lane = lax.broadcasted_iota(jnp.int32, shape, 1) % east
-    own = (row < east) & (lane == row)
-    behind = (row >= east) & (row < east + count) & (lane == row - east)
-    picked = [jnp.where(own, side[:1], 0.0) + jnp.where(behind, side[1:2], 0.0) for side in tiny]
-    added = exact_dot(jnp.concatenate(picked, axis=0), spread_ref[...])
-    sides = [side + added[n * height : (n + 1) * height] for n, side in enumerate(sides)]
+    message_refs = rest[:taken]
+    rows_ref, east_out_ref = rest[taken:]
+    east = rows_ref.shape[1]
+    sides = take_all((ends_ref[0], ends_ref[1]), taking, lax.axis_index("gy"), [ref[...] for ref in message_refs])
     swept = [exact_dot(east_inverse_ref[...], side[:east]) for side in sides]
     for n in range(2):
         rows_ref[n] = swept[n]
-    for p, (i, k) in enumerate(end_places(count, east)):
-        rows = [swept[n][i : i + 1] + 2.0 * sides[n][east + k : east + k + 1] for n in range(2)]
-        wide = jnp.concatenate([plane_ref[p], jnp.zeros((8, upward - plane_ref.shape[2]), F32)], axis=1)
-        small_ref[p] = stacked(rows + [wide[:2]], 8)
+    for i, k in end_places(count, east):
+        total = east_ends_ref[k]
+        for n in range(2):
+            total += spikes_ref[n] * (swept[n][i : i + 1] + 2.0 * sides[n][east + k : east + k + 1])
+        east_out_ref[k] = total
 
 
 def final_kernel(
     pair, table, tile,
-    sweep_ref, own_ref, other_ref, own_small_ref, other_small_ref,
+    sweep_ref, own_ref, other_ref,
     swept_ref, warmth_ref, columns_ref, rows_ref, upward_spikes_ref, north_spikes_ref,
     out_hbm,
     out_ref, sides_ref, sems,
@@ -377,28 +389,16 @@
     east, north, upward = out_ref.shape
     place = ordered(pair, east)
 
-    def widened(plane, small):
-        for side in range(2):
-            plane += north_spikes_ref[side] * small[side : side + 1]
-            plane += as_column(small[2 + side : 3 + side, :north]) * upward_spikes_ref[side : side + 1, :]
-        return plane
-
     if pair:
-        near, far = float(table[0]), float(table[1])
-        sides_ref[0] = widened(
-            near * other_ref[0] + far * own_ref[0], near * other_small_ref[0] + far * own_small_ref[0]
-        )
+        sides_ref[0] = float(table[0]) * other_ref[0] + float(table[1]) * own_ref[0]
     else:
         me = lax.axis_index("gx")
-        members = table.shape[0]
         for side in range(2):
-            plane, small = 0.0, 0.0
-            for m in range(members):
+            plane = 0.0
+            for m in range(table.shape[0]):
                 for end in range(2):
-                    weight = pick(table[:, side, 2 * m + end], me)
-                    plane += weight * other_ref[m, end]
-                    small += weight * other_small_ref[m, end]
-            sides_ref[side] = widened(plane, small)
+                    plane += pick(table[:, side, 2 * m + end], me) * other_ref[m, end]
+            sides_ref[side] = plane
     last = sides_ref.shape[0] - 1
 
     def send(t):
@@ -472,10 +472,10 @@
 
     group = 4
     folded = kept(north // 2 + 8, 2 * east)
-    swept, warmth, upward_ends, north_ends, own, *messages = pl.pallas_call(
-        functools.partial(local_kernel, pair, group, factors, (exchanges[2][0], exchanges[1][0])),
+    swept, warmth, upward_ends, north_ends, east_ends, *messages = pl.pallas_call(
+        functools.partial(local_kernel, pair, group, factors, exchanges[2][0]),
         in_specs=[hbm] * 3,
-        out_specs=[vmem] * (5 + to_up + to_north),
+        out_specs=[vmem] * (5 + to_up),
         out_shape=[
             pltpu.VMEM(shape, F32),
             pltpu.VMEM((east + 2, north, upward), F32),
@@ -483,8 +483,7 @@
             kept(2, height, upward),
             kept(count, north, upward),
         ]
-        + [folded] * to_up
-        + [kept(height, upward)] * to_north,
+        + [folded] * to_up,
         scratch_shapes=[
             pltpu.VMEM(shape, F32),
             pltpu.VMEM((north, 2 * east), F32),
@@ -492,48 +491,45 @@
             pltpu.VMEM(tables.shape, F32),
             pltpu.VMEM((3 * upward, upward), BF16),
             pltpu.VMEM((2 * north, 2 * north), BF16),
+            pltpu.VMEM((group * north, upward), F32),
+            pltpu.VMEM((group * north, upward), F32),
             pltpu.SemaphoreType.DMA((2, east // group + 1)),
         ],
         compiler_params=pltpu.CompilerParams(vmem_limit_bytes=32 * MIB),
-    )(tables, initial_warmth, heat_supply)
-
-    up_messages = spread_out(messages[:to_up], "gz")
-    north_messages = spread_out(messages[to_up:], "gy")
+    )(pltpu.with_memory_space_constraint(jnp.asarray(tables), pltpu.HBM), initial_warmth, heat_supply)
+
+    messages = spread_out(messages, "gz")
+    columns, north_ends, east_ends, *messages = pl.pallas_call(
+        functools.partial(upward_kernel, count, exchanges[2][1], exchanges[1][0]),
+        in_specs=[vmem] * (7 + to_up),
+        out_specs=[vmem] * (3 + to_north),
+        out_shape=[kept(north, 2 * east), kept(2, height, upward), kept(count, north, upward)]
+        + [kept(height, upward)] * to_north,
+        compiler_params=pltpu.CompilerParams(vmem_limit_bytes=6 * MIB),
+    )(upward_ends, north_ends, east_ends, north_inverse, east_twice, upward_spikes, spread, *messages)
+
+    messages = spread_out(messages, "gy")
+    rows, own = pl.pallas_call(
+        functools.partial(north_kernel, count, exchanges[1][1]),
+        in_specs=[vmem] * (4 + to_north),
+        out_specs=[vmem] * 2,
+        out_shape=[kept(2, east, upward), kept(count, north, upward)],
+        compiler_params=pltpu.CompilerParams(vmem_limit_bytes=6 * MIB),
+    )(north_ends, east_ends, east_inverse, north_spikes, *messages)
+
     if pair:
         other = lax.ppermute(own, "gx", [(0, 1), (1, 0)])
-    else:
-        other = lax.all_gather(own, "gx")
-    columns, tiny, planes, *messages = pl.pallas_call(
-        functools.partial(upward_kernel, count, exchanges[2][1], exchanges[1][0]),
-        in_specs=[vmem] * (3 + to_up),
-        out_specs=[vmem] * (3 + to_north),
-        out_shape=[kept(north, 2 * east), kept(2, 8, 2 * east), kept(count, 8, north)]
-        + [kept(8, 2 * east)] * to_north,
-        compiler_params=pltpu.CompilerParams(vmem_limit_bytes=6 * MIB),
-    )(upward_ends, north_inverse, east_twice, *up_messages)
-
-    tiny_messages = spread_out(messages, "gy")
-    rows, own_small = pl.pallas_call(
-        functools.partial(north_kernel, count, exchanges[1][1]),
-        in_specs=[vmem] * (5 + 2 * to_north),
-        out_specs=[vmem] * 2,
-        out_shape=[kept(2, east, upward), kept(count, 8, upward)],
-        compiler_params=pltpu.CompilerParams(vmem_limit_bytes=6 * MIB),
-    )(north_ends, tiny, planes, east_inverse, spread, *north_messages, *tiny_messages)
-
-    if pair:
-        other_small = lax.ppermute(own_small, "gx", [(0, 1), (1, 0)])
         near = lines[0][1][0]
         table = np.array([1.0, near]) / (1.0 - near**2)
     else:
-        other_small = lax.all_gather(own_small, "gx")
+        other = lax.all_gather(own, "gx")
         table = interface_table(lines[0][1], lines[0][2], members[0])
     swept = pltpu.with_memory_space_constraint(swept, pltpu.VMEM)
     warmth = pltpu.with_memory_space_constraint(warmth, pltpu.VMEM)
     tile = 32
     return pl.pallas_call(
         functools.partial(final_kernel, pair, table, tile),
-        in_specs=[smem] + [vmem] * 10,
+        in_specs=[smem] + [vmem] * 8,
         out_specs=hbm,
         out_shape=kept(*shape),
         scratch_shapes=[
@@ -542,7 +538,7 @@
             pltpu.SemaphoreType.DMA((north // tile,)),
         ],
         compiler_params=pltpu.CompilerParams(vmem_limit_bytes=16 * MIB),
-    )(sweep, own, other, own_small, other_small, swept, warmth, columns, rows, upward_spikes, north_spikes)
+    )(sweep, own, other, swept, warmth, columns, rows, upward_spikes, north_spikes)
 
 
 def solution(mesh):

time: 53.3 us -> 46.1 us (0.86)
  starting transfers between devices: 13.5 us -> 9.24 us
  Pallas kernels: 24.6 us -> 22.7 us
  local copies, waits for them, and re-layouts: 1.35 us -> 0.03 us
    ppermute x1, waiting for transfers between devices: 0.01 us -> 4 us  [local(): other = lax.ppermute(own, 'gx', [(0, 1), (1, 0)])]
    ppermute x1 -> x0, waiting for transfers between devices: 3.14 us -> none  [local(): other_small = lax.ppermute(own_small, 'gx', [(0, 1), (1, 0)])]
    ppermute x9 -> x6, starting transfers between devices: 9.84 us -> 7.66 us  [spread_out(): lax.ppermute(message, axis, [(k, peers(k, members, d + 1)[0]) for k in ra...]
    pallas_call x1, Pallas kernels: 17.5 us -> 15.8 us  [local(): pl.pallas_call(functools.partial(local_kernel, pair, group, factors, exch...]
    ppermute x1, starting transfers between devices: 3.03 us -> 1.58 us  [local(): other = lax.ppermute(own, 'gx', [(0, 1), (1, 0)])]
    unnamed x16 -> x14, local copies, waits for them, and re-layouts: 1.35 us -> 0.03 us
    ppermute x9 -> x6, waiting for transfers between devices: 10.5 us -> 9.94 us  [spread_out(): lax.ppermute(message, axis, [(k, peers(k, members, d + 1)[0]) for k in ra...]
    ppermute x1 -> x0, starting transfers between devices: 0.57 us -> none  [local(): other_small = lax.ppermute(own_small, 'gx', [(0, 1), (1, 0)])]
  transfers between devices with their start and end apart: 11 -> 7, of which waited for: 6 -> 5; matrix products, arithmetic and copies ran while one was open for 0% -> 0% of each run, Pallas kernels for 2% -> 0%
where the time goes in v4:
time: 46.1 us; the launch traced here: 46 us
  Pallas kernels  22.7 us (49%)
  waiting for transfers between devices  13.9 us (30%)
  starting transfers between devices  9.24 us (20%)
    pallas_call x1, Pallas kernels, local(): pl.pallas_call(functools.partial(local_kernel, pair, group, factors, exch...  15.8 us
    ppermute x6, waiting for transfers between devices, spread_out(): lax.ppermute(message, axis, [(k, peers(k, members, d + 1)[0]) for k in ra...  9.94 us
    ppermute x6, starting transfers between devices, spread_out(): lax.ppermute(message, axis, [(k, peers(k, members, d + 1)[0]) for k in ra...  7.66 us
    pallas_call x1, Pallas kernels, local(): pl.pallas_call(functools.partial(final_kernel, pair, table, tile), in_spe...  5.79 us
    ppermute x1, waiting for transfers between devices, local(): other = lax.ppermute(own, 'gx', [(0, 1), (1, 0)])  4 us
    ppermute x1, starting transfers between devices, local(): other = lax.ppermute(own, 'gx', [(0, 1), (1, 0)])  1.58 us
  transfers between devices with their start and end apart: 7, of which 5 were waited for; matrix products, arithmetic and copies ran while one was open for 0% of the time, Pallas kernels for 0%

profile of v4, /device:TPU:0, one launch (start us, length us, event | category | flops | bytes accessed | tf_op | source)
XLA Modules:
  0.0 46.0 jit_solution(4889374319149703349)
XLA Ops:
  0.0 0.0 copy-start.1
  0.0 0.0 copy-start.2
  0.0 0.0 copy-start.3
  0.0 0.0 copy-start.5
  0.0 0.0 copy-start
  0.0 0.0 copy-start.4
  0.0 0.0 copy-start.6
  0.0 15.8 %shard_map.100 = (f32[64,128,256]{2,1,0:T(8,128)S(1)}, f32[66,128,256]{2,1,0:T(8,128)S(1)}, f32[2,72,128]{2,1,0:T(8,128)S(1)}, f32[2,72,256]{2,1,0:T(8,128)S(1)}...) custom-call(f32[1280,256]{1,0:T(8,128)} %constant.16.clone.tables_hbm, ...), custom_call_target="tpu_custom_call" | custom-call | tf_op jit(solution)/shard_map/pallas_call | solution.py:475
  15.9 3.1 %collective-permute-start = (f32[72,128]{1,0:T(8,128)S(1)}, f32[72,128]{1,0:T(8,128)S(1)}, u32[]{:S(2)}, u32[]{:S(2)}) collective-permute-start(f32[72,128]{1,0:T(8,128)S(1)} %get-tuple-element.24), channel_id=1, source_target_pairs={{0,1},{1,0},{2,3},{3,2},{4,5},{5,4},{6,7},{7,6},{8,9},{9,8},{10,11... | collective-permute-start | bytes 110600 | tf_op jit(solution)/shard_map/ppermute | solution.py:435
  19.0 2.6 %collective-permute-start.1 = (f32[72,128]{1,0:T(8,128)S(1)}, f32[72,128]{1,0:T(8,128)S(1)}, u32[]{:S(2)}, u32[]{:S(2)}) collective-permute-start(f32[72,128]{1,0:T(8,128)S(1)} %get-tuple-element.25), channel_id=1, source_target_pairs={{0,2},{1,3},{2,0},{3,1},{4,6},{5,7},{6,4},{7,5},{8,10},{9,11},{10,... | collective-permute-start | bytes 110600 | tf_op jit(solution)/shard_map/ppermute | solution.py:435
  21.6 0.0 collective-permute-start.2
  21.6 0.0 collective-permute-done.rest_0_
  21.6 2.9 %collective-permute-done.1.rest_1_ = f32[72,128]{1,0:T(8,128)S(1)} collective-permute-done((f32[72,128]{1,0:T(8,128)S(1)}, f32[72,128]{1,0:T(8,128)S(1)}, u32[]{:S(2)}, u32[]{:S(2)}) %collective-permute-start.1) | collective-permute-done | bytes 36896 | tf_op jit(solution)/shard_map/ppermute | solution.py:435
  24.6 2.8 %collective-permute-done.2.rest_2_ = f32[72,128]{1,0:T(8,128)S(1)} collective-permute-done((f32[72,128]{1,0:T(8,128)S(1)}, f32[72,128]{1,0:T(8,128)S(1)}, u32[]{:S(2)}, u32[]{:S(2)}) %collective-permute-start.2) | collective-permute-done | bytes 36896 | tf_op jit(solution)/shard_map/ppermute | solution.py:435
  27.4 0.0 copy-done.1
  27.4 0.0 copy-done.2
  27.4 0.0 copy-done.3
  27.4 0.0 copy-done.5
  27.4 0.7 %shard_map.101 = (f32[128,128]{1,0:T(8,128)S(1)}, f32[2,72,256]{2,1,0:T(8,128)S(1)}, f32[1,128,256]{2,1,0:T(8,128)S(1)}, f32[72,256]{1,0:T(8,128)S(1)}, f32[72,256]{1,0:T(8,128)S(1)}, /*index=5*/f32[72,256]{1,0:T(8,128)S(1)}) custom-call(f32[2,72,128]{2,1,0:T(8,128)S(1)} %get-tuple-element.21.ends_ref, f32[2,72,256]{2,1,0:T(8,128)S(1)} %get-tuple-element.22.north_ends_ref, ...), custom_call_target="tpu_custom_call" | custom-call | tf_op jit(solution)/shard_map/pallas_call | solution.py:502
  28.1 0.1 collective-permute-start.3
  28.2 1.6 %collective-permute-start.4 = (f32[72,256]{1,0:T(8,128)S(1)}, f32[72,256]{1,0:T(8,128)S(1)}, u32[]{:S(2)}, u32[]{:S(2)}) collective-permute-start(f32[72,256]{1,0:T(8,128)S(1)} %get-tuple-element.30), channel_id=1, source_target_pairs={{0,8},{4,12},{8,0},{12,4},{1,9},{5,13},{9,1},{13,5},{2,10},{6,14},... | collective-permute-start | bytes 221192 | tf_op jit(solution)/shard_map/ppermute | solution.py:435
  29.7 0.3 collective-permute-start.5
  30.0 0.0 collective-permute-done.3.rest_0_
  30.0 3.0 %collective-permute-done.4.rest_1_ = f32[72,256]{1,0:T(8,128)S(1)} collective-permute-done((f32[72,256]{1,0:T(8,128)S(1)}, f32[72,256]{1,0:T(8,128)S(1)}, u32[]{:S(2)}, u32[]{:S(2)}) %collective-permute-start.4) | collective-permute-done | bytes 73760 | tf_op jit(solution)/shard_map/ppermute | solution.py:435
  33.0 1.2 %collective-permute-done.5.rest_2_ = f32[72,256]{1,0:T(8,128)S(1)} collective-permute-done((f32[72,256]{1,0:T(8,128)S(1)}, f32[72,256]{1,0:T(8,128)S(1)}, u32[]{:S(2)}, u32[]{:S(2)}) %collective-permute-start.5) | collective-permute-done | bytes 73760 | tf_op jit(solution)/shard_map/ppermute | solution.py:435
  34.2 0.0 copy-done
  34.2 0.0 copy-done.4
  34.2 0.3 shard_map.102
  34.6 1.6 %collective-permute-start.6 = (f32[1,128,256]{2,1,0:T(8,128)S(1)}, f32[1,128,256]{2,1,0:T(8,128)S(1)}, u32[]{:S(2)}, u32[]{:S(2)}) collective-permute-start(f32[1,128,256]{2,1,0:T(8,128)S(1)} %get-tuple-element.32.own_ref), channel_id=1, source_target_pairs={{0,16},{16,0},{1,17},{17,1},{2,18},{18,2},{3,19},{19,3},{4,20},{20... | collective-permute-start | bytes 393224 | tf_op jit(solution)/shard_map/ppermute | solution.py:521
  36.2 4.0 %collective-permute-done.6.other_ref = f32[1,128,256]{2,1,0:T(8,128)S(1)} collective-permute-done((f32[1,128,256]{2,1,0:T(8,128)S(1)}, f32[1,128,256]{2,1,0:T(8,128)S(1)}, u32[]{:S(2)}, u32[]{:S(2)}) %collective-permute-start.6) | collective-permute-done | bytes 131104 | tf_op jit(solution)/shard_map/ppermute | solution.py:521
  40.2 0.0 copy-done.6
  40.2 5.8 %shard_map.103 = f32[64,128,256]{2,1,0:T(8,128)} custom-call(f32[4,64]{1,0:T(4,128)S(1)} %copy-done.6, f32[1,128,256]{2,1,0:T(8,128)S(1)} %get-tuple-element.32.own_ref, f32[1,128,256]{2,1,0:T(8,128)S(1)} %collective-permute-done.6.other_ref, f32[64,128,256]{2,1,0:T(8,128)S(1)} %get-tuple-element.33.swept_ref, ...), custom_call_target="tpu_custom_call" | custom-call | tf_op jit(solution)/shard_map/pallas_call | solution.py:530
Async XLA Ops:
  0.0 27.4 %copy-start.1 = (f32[128,256]{1,0:T(8,128)S(1)}, f32[128,256]{1,0:T(8,128)}, u32[]{:S(2)}) copy-start(f32[128,256]{1,0:T(8,128)} %constant.20.clone.spread_ref) | copy-start | bytes 393220
  0.0 27.4 %copy-start.2 = (f32[128,128]{1,0:T(8,128)S(1)}, f32[128,128]{1,0:T(8,128)}, u32[]{:S(2)}) copy-start(f32[128,128]{1,0:T(8,128)} %constant.18.clone.east_twice_ref) | copy-start | bytes 196612
  0.0 27.4 %copy-start.3 = (f32[128,128]{1,0:T(8,128)S(1)}, f32[128,128]{1,0:T(8,128)}, u32[]{:S(2)}) copy-start(f32[128,128]{1,0:T(8,128)} %constant.17.clone.north_inverse_ref) | copy-start | bytes 196612
  0.0 27.4 %copy-start.5 = (f32[2,256]{1,0:T(2,128)S(1)}, f32[2,256]{1,0:T(2,128)}, u32[]{:S(2)}) copy-start(f32[2,256]{1,0:T(2,128)} %constant.19.clone.spikes_ref.upward_spikes_ref) | copy-start | bytes 6148
  0.0 34.2 %copy-start = (f32[2,128,256]{2,1,0:T(8,128)S(1)}, f32[2,128,256]{2,1,0:T(8,128)}, u32[]{:S(2)}) copy-start(f32[2,128,256]{2,1,0:T(8,128)} %constant.22.clone.spikes_ref.north_spikes_ref) | copy-start | bytes 786436
  0.0 34.2 %copy-start.4 = (f32[64,64]{1,0:T(8,128)S(1)}, f32[64,64]{1,0:T(8,128)}, u32[]{:S(2)}) copy-start(f32[64,64]{1,0:T(8,128)} %constant.21.clone.east_inverse_ref) | copy-start | bytes 49156
  0.0 40.1 %copy-start.6 = (f32[4,64]{1,0:T(4,128)S(1)}, f32[4,64]{1,0:T(4,128)}, u32[]{:S(2)}) copy-start(f32[4,64]{1,0:T(4,128)} %constant.23.clone.sweep_ref) | copy-start | bytes 3076
  15.9 5.7 %collective-permute-start = (f32[72,128]{1,0:T(8,128)S(1)}, f32[72,128]{1,0:T(8,128)S(1)}, u32[]{:S(2)}, u32[]{:S(2)}) collective-permute-start(f32[72,128]{1,0:T(8,128)S(1)} %get-tuple-element.24), channel_id=1, source_target_pairs={{0,1},{1,0},{2,3},{3,2},{4,5},{5,4},{6,7},{7,6},{8,9},{9,8},{10,11... | collective-permute-start | bytes 110600 | tf_op jit(solution)/shard_map/ppermute | solution.py:435
  19.0 5.5 %collective-permute-start.1 = (f32[72,128]{1,0:T(8,128)S(1)}, f32[72,128]{1,0:T(8,128)S(1)}, u32[]{:S(2)}, u32[]{:S(2)}) collective-permute-start(f32[72,128]{1,0:T(8,128)S(1)} %get-tuple-element.25), channel_id=1, source_target_pairs={{0,2},{1,3},{2,0},{3,1},{4,6},{5,7},{6,4},{7,5},{8,10},{9,11},{10,... | collective-permute-start | bytes 110600 | tf_op jit(solution)/shard_map/ppermute | solution.py:435
  21.6 5.8 %collective-permute-start.2 = (f32[72,128]{1,0:T(8,128)S(1)}, f32[72,128]{1,0:T(8,128)S(1)}, u32[]{:S(2)}, u32[]{:S(2)}) collective-permute-start(f32[72,128]{1,0:T(8,128)S(1)} %get-tuple-element.26), channel_id=1, source_target_pairs={{0,3},{1,2},{2,1},{3,0},{4,7},{5,6},{6,5},{7,4},{8,11},{9,10},{10,... | collective-permute-start | bytes 110600 | tf_op jit(solution)/shard_map/ppermute | solution.py:435
  28.1 1.9 %collective-permute-start.3 = (f32[72,256]{1,0:T(8,128)S(1)}, f32[72,256]{1,0:T(8,128)S(1)}, u32[]{:S(2)}, u32[]{:S(2)}) collective-permute-start(f32[72,256]{1,0:T(8,128)S(1)} %get-tuple-element.29), channel_id=1, source_target_pairs={{0,4},{4,0},{8,12},{12,8},{1,5},{5,1},{9,13},{13,9},{2,6},{6,2},{1... | collective-permute-start | bytes 221192 | tf_op jit(solution)/shard_map/ppermute | solution.py:435
  28.2 4.8 %collective-permute-start.4 = (f32[72,256]{1,0:T(8,128)S(1)}, f32[72,256]{1,0:T(8,128)S(1)}, u32[]{:S(2)}, u32[]{:S(2)}) collective-permute-start(f32[72,256]{1,0:T(8,128)S(1)} %get-tuple-element.30), channel_id=1, source_target_pairs={{0,8},{4,12},{8,0},{12,4},{1,9},{5,13},{9,1},{13,5},{2,10},{6,14},... | collective-permute-start | bytes 221192 | tf_op jit(solution)/shard_map/ppermute | solution.py:435
  29.7 4.5 %collective-permute-start.5 = (f32[72,256]{1,0:T(8,128)S(1)}, f32[72,256]{1,0:T(8,128)S(1)}, u32[]{:S(2)}, u32[]{:S(2)}) collective-permute-start(f32[72,256]{1,0:T(8,128)S(1)} %get-tuple-element.31), channel_id=1, source_target_pairs={{0,12},{4,8},{8,4},{12,0},{1,13},{5,9},{9,5},{13,1},{2,14},{6,10},... | collective-permute-start | bytes 221192 | tf_op jit(solution)/shard_map/ppermute | solution.py:435
  34.6 5.6 %collective-permute-start.6 = (f32[1,128,256]{2,1,0:T(8,128)S(1)}, f32[1,128,256]{2,1,0:T(8,128)S(1)}, u32[]{:S(2)}, u32[]{:S(2)}) collective-permute-start(f32[1,128,256]{2,1,0:T(8,128)S(1)} %get-tuple-element.32.own_ref), channel_id=1, source_target_pairs={{0,16},{16,0},{1,17},{17,1},{2,18},{18,2},{3,19},{19,3},{4,20},{20... | collective-permute-start | bytes 393224 | tf_op jit(solution)/shard_map/ppermute | solution.py:521

commit v5 on v4

--- a/solution.py
+++ b/solution.py
@@ -88,13 +88,11 @@
 def sweep_table(length, factor):
     half = 0.5 * factor
     ratio = np.zeros(length)
-    scale = np.zeros(length)
     last = 0.0
     for i in range(length):
-        scale[i] = 1.0 / (1.0 + factor - half * last)
-        ratio[i] = last = half * scale[i]
-    head = np.concatenate([[1.0], np.cumprod(ratio)[:-1]])
-    return np.stack([scale, ratio, head, np.cumprod(ratio)])
+        ratio[i] = last = half / (1.0 + factor - half * last)
+    decay = np.cumprod(ratio)
+    return np.stack([ratio, decay, decay])
 
 
 def split(table, axis):
@@ -121,8 +119,7 @@
     return jnp.dot(a, b, precision=lax.Precision.HIGHEST, preferred_element_type=F32)
 
 
-def upward_dot(values, table_ref):
-    high, low = parts(values)
+def upward_dot(high, low, table_ref):
     return dot(jnp.concatenate([high, low, high], axis=1), table_ref[...])
 
 
@@ -186,7 +183,7 @@
 ):
     to_up = sending.shape[1] // 2
     up_refs = rest[:to_up]
-    supply_ref, both_ref, edges_ref, tables_ref, up_ref, north_ref, even_ref, odd_ref, sems = rest[to_up:]
+    supply_ref, both_ref, edges_ref, tables_ref, up_ref, north_ref, halves_ref, even_ref, odd_ref, sems = rest[to_up:]
     east, north, upward = supply_ref.shape
     groups = east // group
     count = east_ends_ref.shape[0]
@@ -209,7 +206,10 @@
     both_ref[...] = jnp.zeros_like(both_ref)
     east_ends_ref[...] = jnp.zeros_like(east_ends_ref)
     lane = lax.broadcasted_iota(jnp.int32, (1, 2 * east), 1)
-    line = lax.broadcasted_iota(jnp.int32, (north, 1), 0)
+    line = lax.broadcasted_iota(jnp.int32, (8, 1), 0)
+    half_factor = 0.5 * factors[0]
+    width = min(upward, 128)
+    swept_ref[0] = jnp.zeros((north, upward), F32)
     tables.wait()
     up_ref[...] = tables_ref[: 3 * upward].astype(BF16)
     north_ref[...] = tables_ref[3 * upward : 3 * upward + 2 * north, : 2 * north].astype(BF16)
@@ -223,38 +223,57 @@
         def _():
             fetch(0, g + 1).wait()
 
+    def shifted(values, step):
+        turned = pltpu.roll(values, step % north, 0)
+        if step > 0:
+            return jnp.concatenate([jnp.where(line == 0, 0.0, turned[:8]), turned[8:]], axis=0)
+        return jnp.concatenate([turned[:-8], jnp.where(line == 7, 0.0, turned[-8:])], axis=0)
+
     def upward_part(g, slot_ref):
-        heat_list = []
         for k in range(group):
             i = g * group + k
             x = place(i)
-            warm = warmth_ref[x + 1]
-            bent = (warmth_ref[x] - warm) + (warmth_ref[x + 2] - warm)
-            low = jnp.where(line == 0, 0.0, pltpu.roll(warm, 1, 0))
-            high = jnp.where(line == north - 1, 0.0, pltpu.roll(warm, north - 1, 0))
-            bent += (factors[1] / factors[0]) * ((low - warm) + (high - warm))
-            heat_list.append((supply_ref[x] + 2.0 * warm) + factors[0] * bent)
-            edges_ref[pl.ds(i, 1)] = warm[:1]
-            edges_ref[pl.ds(east + i, 1)] = warm[north - 1 :]
-        slot_ref[...] = upward_dot(jnp.concatenate(heat_list, axis=0), up_ref)
+            rows = slice(k * north, (k + 1) * north)
+            edges_ref[pl.ds(i, 1)] = warmth_ref[x + 1, :1]
+            edges_ref[pl.ds(east + i, 1)] = warmth_ref[x + 1, north - 1 :]
+            for start in range(0, upward, width):
+                lanes = slice(start, start + width)
+                warm = warmth_ref[x + 1, :, lanes]
+                bent = (warmth_ref[x, :, lanes] - warm) + (warmth_ref[x + 2, :, lanes] - warm)
+                across = (shifted(warm, 1) - warm) + (shifted(warm, -1) - warm)
+                heat = (supply_ref[x, :, lanes] + 2.0 * warm) + (factors[0] * bent + factors[1] * across)
+                high, low = parts(heat)
+                halves_ref[rows, lanes] = high
+                halves_ref[rows, start + upward : start + upward + width] = low
+        slot_ref[...] = upward_dot(halves_ref[:, :upward], halves_ref[:, upward:], up_ref)
 
     def north_part(g, slot_ref):
         for k in range(group):
             i = g * group + k
-            first = slot_ref[k * north : (k + 1) * north]
-            heads = pltpu.roll(first[:, : 2 * east], i, 1)
-            tails = pltpu.roll(first[:, upward - 2 * east :], east + 1 + i, 1)
+            x = place(i)
+            rows = slice(k * north, (k + 1) * north)
+            heads = pltpu.roll(slot_ref[rows, : 2 * east], i, 1)
+            tails = pltpu.roll(slot_ref[rows, upward - 2 * east :], east + 1 + i, 1)
             both = jnp.where(lane == i, heads, both_ref[...])
             both_ref[...] = jnp.where(lane == east + i, tails, both)
-            solved = north_dot(north_ref, first - 2.0 * warmth_ref[place(i) + 1])
-            north_ends_ref[0, pl.ds(i, 1), :] = solved[:1]
-            north_ends_ref[1, pl.ds(i, 1), :] = solved[north - 1 :]
-            scale, ratio = (tables_ref[pl.ds(sweep + n * east + i, 1), :] for n in range(2))
-            swept = scale * solved + ratio * east_ends_ref[count - 1]
-            swept_ref[i] = swept
-            east_ends_ref[count - 1] = swept
-            if not pair:
-                east_ends_ref[0] += tables_ref[pl.ds(sweep + 2 * east + i, 1), :] * swept
+            pieces = []
+            for start in range(0, upward, width):
+                lanes = slice(start, start + width)
+                pieces.append(jnp.concatenate(parts(slot_ref[rows, lanes] - 2.0 * warmth_ref[x + 1, :, lanes]), axis=0))
+            solved = dot(north_ref[...], jnp.concatenate(pieces, axis=1))
+            before = jnp.maximum(i - 1, 0)
+            north_ends_ref[0, pl.ds(i, 1)] = half_factor * (solved[:1] + solved[north : north + 1])
+            north_ends_ref[1, pl.ds(i, 1)] = half_factor * (solved[north - 1 : north] + solved[2 * north - 1 :])
+            ratio = tables_ref[pl.ds(sweep + i, 1), :]
+            weight = tables_ref[pl.ds(sweep + east + i, 1), :]
+            for start in range(0, upward, width):
+                lanes = slice(start, start + width)
+                whole = solved[:north, lanes] + solved[north:, lanes]
+                swept = whole + ratio[:, lanes] * swept_ref[before, :, lanes]
+                swept_ref[i, :, lanes] = swept
+                if not pair:
+                    east_ends_ref[0, :, lanes] += weight[:, lanes] * swept
+        return 0
 
     arrive(0)
     upward_part(0, even_ref)
@@ -278,11 +297,12 @@
 
     ends = end_places(count, east)
     planes = [warmth_ref[place(i) + 1] for i, _ in ends]
-    solved_up = upward_dot(jnp.concatenate([edges_ref[...]] + planes, axis=0), up_ref)
+    solved_up = upward_dot(*parts(jnp.concatenate([edges_ref[...]] + planes, axis=0)), up_ref)
+    east_ends_ref[count - 1] = tables_ref[sweep + 2 * east : sweep + 2 * east + 1, :] * swept_ref[east - 1]
     height = north_ends_ref.shape[1]
     rows = [[], []]
     for p in range(count):
-        solved = north_dot(north_ref, solved_up[2 * east + p * north : 2 * east + (p + 1) * north])
+        solved = half_factor * north_dot(north_ref, solved_up[2 * east + p * north : 2 * east + (p + 1) * north])
         rows[0].append(solved[:1])
         rows[1].append(solved[north - 1 :])
         east_ends_ref[p] += 2.0 * solved
@@ -411,9 +431,9 @@
         columns = columns_ref[block]
         first_spike, last_spike = north_spikes_ref[0, block], north_spikes_ref[1, block]
         for i in reversed(range(east)):
-            value = swept_ref[i, block] + sweep_ref[1, i] * value
+            value = sweep_ref[0, i] * (swept_ref[i, block] + value)
             if not pair:
-                value += sweep_ref[3, i] * sides_ref[0, block]
+                value += sweep_ref[2, i] * sides_ref[0, block]
             added = (
                 columns[:, i : i + 1] * upward_spikes_ref[0:1, :]
                 + columns[:, east + i : east + i + 1] * upward_spikes_ref[1:2, :]
@@ -442,15 +462,17 @@
     members = [lax.axis_size(axis) for axis in ("gx", "gy", "gz")]
     factors = [float((n * m) ** 2 // 4) for n, m in zip(shape, members)]
     lines = [line_tables(n, factor) for n, factor in zip(shape, factors)]
-    sweep = sweep_table(east, factors[0]).astype(np.float32)
+    sweep = sweep_table(east, factors[0])
+    ratio, weights = sweep[:2]
+    sweep = sweep.astype(np.float32)
     exchanges = [exchange_tables(line[1], line[2], m) for line, m in zip(lines, members)]
     upward_high, upward_low = split(lines[2][0], 0)
-    north_high, north_low = split(lines[1][0], 1)
+    north_high, north_low = split(lines[1][0] / (0.5 * factors[0]), 1)
     north_stack = np.block([[north_high, north_high], [north_low, np.zeros_like(north_low)]])
     tables = np.concatenate([
         np.concatenate([upward_high, upward_high, upward_low]).astype(np.float32),
         np.pad(north_stack.astype(np.float32), ((0, 0), (0, max(upward - 2 * north, 0)))),
-        np.repeat(sweep.reshape(-1, 1), upward, axis=1),
+        np.repeat(np.concatenate([[0.0], ratio[:-1], weights, ratio[-1:], np.zeros(7)])[:, None], upward, axis=1).astype(np.float32),
     ])
     east_inverse = lines[0][0].astype(np.float32)
     north_inverse = lines[1][0].astype(np.float32)
@@ -491,6 +513,7 @@
             pltpu.VMEM(tables.shape, F32),
             pltpu.VMEM((3 * upward, upward), BF16),
             pltpu.VMEM((2 * north, 2 * north), BF16),
+            pltpu.VMEM((group * north, 2 * upward), BF16),
             pltpu.VMEM((group * north, upward), F32),
             pltpu.VMEM((group * north, upward), F32),
             pltpu.SemaphoreType.DMA((2, east // group + 1)),
@@ -526,7 +549,7 @@
         table = interface_table(lines[0][1], lines[0][2], members[0])
     swept = pltpu.with_memory_space_constraint(swept, pltpu.VMEM)
     warmth = pltpu.with_memory_space_constraint(warmth, pltpu.VMEM)
-    tile = 32
+    tile = 16
     return pl.pallas_call(
         functools.partial(final_kernel, pair, table, tile),
         in_specs=[smem] + [vmem] * 8,

time: 46.1 us -> 47.6 us (1.033)
  Pallas kernels: 22.7 us -> 24.2 us
    pallas_call x1, Pallas kernels: 15.8 us -> 17.3 us  [local(): pl.pallas_call(functools.partial(local_kernel, pair, group, factors, exch...]
where the time goes in v5:
time: 47.6 us; the launch traced here: 47.4 us
  Pallas kernels  24.2 us (51%)
  waiting for transfers between devices  13.9 us (29%)
  starting transfers between devices  9.26 us (19%)
    pallas_call x1, Pallas kernels, local(): pl.pallas_call(functools.partial(local_kernel, pair, group, factors, exch...  17.3 us
    ppermute x6, waiting for transfers between devices, spread_out(): lax.ppermute(message, axis, [(k, peers(k, members, d + 1)[0]) for k in ra...  9.94 us
    ppermute x6, starting transfers between devices, spread_out(): lax.ppermute(message, axis, [(k, peers(k, members, d + 1)[0]) for k in ra...  7.66 us
    pallas_call x1, Pallas kernels, local(): pl.pallas_call(functools.partial(final_kernel, pair, table, tile), in_spe...  5.81 us
    ppermute x1, waiting for transfers between devices, local(): other = lax.ppermute(own, 'gx', [(0, 1), (1, 0)])  3.98 us
    ppermute x1, starting transfers between devices, local(): other = lax.ppermute(own, 'gx', [(0, 1), (1, 0)])  1.6 us
  transfers between devices with their start and end apart: 7, of which 5 were waited for; matrix products, arithmetic and copies ran while one was open for 0% of the time, Pallas kernels for 0%

profile of v5, /device:TPU:0, one launch (start us, length us, event | category | flops | bytes accessed | tf_op | source)
XLA Modules:
  0.0 47.4 jit_solution(3338543409697926908)
XLA Ops:
  0.0 0.0 copy-start.1
  0.0 0.0 copy-start.2
  0.0 0.0 copy-start.3
  0.0 0.0 copy-start.5
  0.0 0.0 copy-start
  0.0 0.0 copy-start.4
  0.0 0.0 copy-start.6
  0.0 17.3 %shard_map.100 = (f32[64,128,256]{2,1,0:T(8,128)S(1)}, f32[66,128,256]{2,1,0:T(8,128)S(1)}, f32[2,72,128]{2,1,0:T(8,128)S(1)}, f32[2,72,256]{2,1,0:T(8,128)S(1)}...) custom-call(f32[1160,256]{1,0:T(8,128)} %constant.16.clone.tables_hbm, ...), custom_call_target="tpu_custom_call" | custom-call | tf_op jit(solution)/shard_map/pallas_call | solution.py:497
  17.4 3.1 %collective-permute-start = (f32[72,128]{1,0:T(8,128)S(1)}, f32[72,128]{1,0:T(8,128)S(1)}, u32[]{:S(2)}, u32[]{:S(2)}) collective-permute-start(f32[72,128]{1,0:T(8,128)S(1)} %get-tuple-element.24), channel_id=1, source_target_pairs={{0,1},{1,0},{2,3},{3,2},{4,5},{5,4},{6,7},{7,6},{8,9},{9,8},{10,11... | collective-permute-start | bytes 110600 | tf_op jit(solution)/shard_map/ppermute | solution.py:455
  20.5 2.6 %collective-permute-start.1 = (f32[72,128]{1,0:T(8,128)S(1)}, f32[72,128]{1,0:T(8,128)S(1)}, u32[]{:S(2)}, u32[]{:S(2)}) collective-permute-start(f32[72,128]{1,0:T(8,128)S(1)} %get-tuple-element.25), channel_id=1, source_target_pairs={{0,2},{1,3},{2,0},{3,1},{4,6},{5,7},{6,4},{7,5},{8,10},{9,11},{10,... | collective-permute-start | bytes 110600 | tf_op jit(solution)/shard_map/ppermute | solution.py:455
  23.1 0.0 collective-permute-start.2
  23.1 0.0 collective-permute-done.rest_0_
  23.1 2.9 %collective-permute-done.1.rest_1_ = f32[72,128]{1,0:T(8,128)S(1)} collective-permute-done((f32[72,128]{1,0:T(8,128)S(1)}, f32[72,128]{1,0:T(8,128)S(1)}, u32[]{:S(2)}, u32[]{:S(2)}) %collective-permute-start.1) | collective-permute-done | bytes 36896 | tf_op jit(solution)/shard_map/ppermute | solution.py:455
  26.0 2.8 %collective-permute-done.2.rest_2_ = f32[72,128]{1,0:T(8,128)S(1)} collective-permute-done((f32[72,128]{1,0:T(8,128)S(1)}, f32[72,128]{1,0:T(8,128)S(1)}, u32[]{:S(2)}, u32[]{:S(2)}) %collective-permute-start.2) | collective-permute-done | bytes 36896 | tf_op jit(solution)/shard_map/ppermute | solution.py:455
  28.8 0.0 copy-done.1
  28.8 0.0 copy-done.2
  28.8 0.0 copy-done.3
  28.9 0.0 copy-done.5
  28.9 0.7 %shard_map.101 = (f32[128,128]{1,0:T(8,128)S(1)}, f32[2,72,256]{2,1,0:T(8,128)S(1)}, f32[1,128,256]{2,1,0:T(8,128)S(1)}, f32[72,256]{1,0:T(8,128)S(1)}, f32[72,256]{1,0:T(8,128)S(1)}, /*index=5*/f32[72,256]{1,0:T(8,128)S(1)}) custom-call(f32[2,72,128]{2,1,0:T(8,128)S(1)} %get-tuple-element.21.ends_ref, f32[2,72,256]{2,1,0:T(8,128)S(1)} %get-tuple-element.22.north_ends_ref, ...), custom_call_target="tpu_custom_call" | custom-call | tf_op jit(solution)/shard_map/pallas_call | solution.py:525
  29.6 0.1 collective-permute-start.3
  29.6 1.6 %collective-permute-start.4 = (f32[72,256]{1,0:T(8,128)S(1)}, f32[72,256]{1,0:T(8,128)S(1)}, u32[]{:S(2)}, u32[]{:S(2)}) collective-permute-start(f32[72,256]{1,0:T(8,128)S(1)} %get-tuple-element.30), channel_id=1, source_target_pairs={{0,8},{4,12},{8,0},{12,4},{1,9},{5,13},{9,1},{13,5},{2,10},{6,14},... | collective-permute-start | bytes 221192 | tf_op jit(solution)/shard_map/ppermute | solution.py:455
  31.2 0.3 collective-permute-start.5
  31.5 0.0 collective-permute-done.3.rest_0_
  31.5 3.0 %collective-permute-done.4.rest_1_ = f32[72,256]{1,0:T(8,128)S(1)} collective-permute-done((f32[72,256]{1,0:T(8,128)S(1)}, f32[72,256]{1,0:T(8,128)S(1)}, u32[]{:S(2)}, u32[]{:S(2)}) %collective-permute-start.4) | collective-permute-done | bytes 73760 | tf_op jit(solution)/shard_map/ppermute | solution.py:455
  34.5 1.2 %collective-permute-done.5.rest_2_ = f32[72,256]{1,0:T(8,128)S(1)} collective-permute-done((f32[72,256]{1,0:T(8,128)S(1)}, f32[72,256]{1,0:T(8,128)S(1)}, u32[]{:S(2)}, u32[]{:S(2)}) %collective-permute-start.5) | collective-permute-done | bytes 73760 | tf_op jit(solution)/shard_map/ppermute | solution.py:455
  35.7 0.0 copy-done
  35.7 0.0 copy-done.4
  35.7 0.3 shard_map.102
  36.0 1.6 %collective-permute-start.6 = (f32[1,128,256]{2,1,0:T(8,128)S(1)}, f32[1,128,256]{2,1,0:T(8,128)S(1)}, u32[]{:S(2)}, u32[]{:S(2)}) collective-permute-start(f32[1,128,256]{2,1,0:T(8,128)S(1)} %get-tuple-element.32.own_ref), channel_id=1, source_target_pairs={{0,16},{16,0},{1,17},{17,1},{2,18},{18,2},{3,19},{19,3},{4,20},{20... | collective-permute-start | bytes 393224 | tf_op jit(solution)/shard_map/ppermute | solution.py:544
  37.7 4.0 %collective-permute-done.6.other_ref = f32[1,128,256]{2,1,0:T(8,128)S(1)} collective-permute-done((f32[1,128,256]{2,1,0:T(8,128)S(1)}, f32[1,128,256]{2,1,0:T(8,128)S(1)}, u32[]{:S(2)}, u32[]{:S(2)}) %collective-permute-start.6) | collective-permute-done | bytes 131104 | tf_op jit(solution)/shard_map/ppermute | solution.py:544
  41.6 0.0 copy-done.6
  41.6 5.8 %shard_map.103 = f32[64,128,256]{2,1,0:T(8,128)} custom-call(f32[3,64]{1,0:T(4,128)S(1)} %copy-done.6, f32[1,128,256]{2,1,0:T(8,128)S(1)} %get-tuple-element.32.own_ref, f32[1,128,256]{2,1,0:T(8,128)S(1)} %collective-permute-done.6.other_ref, f32[64,128,256]{2,1,0:T(8,128)S(1)} %get-tuple-element.33.swept_ref, ...), custom_call_target="tpu_custom_call" | custom-call | tf_op jit(solution)/shard_map/pallas_call | solution.py:553
Async XLA Ops:
  0.0 28.8 %copy-start.1 = (f32[128,256]{1,0:T(8,128)S(1)}, f32[128,256]{1,0:T(8,128)}, u32[]{:S(2)}) copy-start(f32[128,256]{1,0:T(8,128)} %constant.20.clone.spread_ref) | copy-start | bytes 393220
  0.0 28.8 %copy-start.2 = (f32[128,128]{1,0:T(8,128)S(1)}, f32[128,128]{1,0:T(8,128)}, u32[]{:S(2)}) copy-start(f32[128,128]{1,0:T(8,128)} %constant.18.clone.east_twice_ref) | copy-start | bytes 196612
  0.0 28.8 %copy-start.3 = (f32[128,128]{1,0:T(8,128)S(1)}, f32[128,128]{1,0:T(8,128)}, u32[]{:S(2)}) copy-start(f32[128,128]{1,0:T(8,128)} %constant.17.clone.north_inverse_ref) | copy-start | bytes 196612
  0.0 28.8 %copy-start.5 = (f32[2,256]{1,0:T(2,128)S(1)}, f32[2,256]{1,0:T(2,128)}, u32[]{:S(2)}) copy-start(f32[2,256]{1,0:T(2,128)} %constant.19.clone.spikes_ref.upward_spikes_ref) | copy-start | bytes 6148
  0.0 35.7 %copy-start = (f32[2,128,256]{2,1,0:T(8,128)S(1)}, f32[2,128,256]{2,1,0:T(8,128)}, u32[]{:S(2)}) copy-start(f32[2,128,256]{2,1,0:T(8,128)} %constant.22.clone.spikes_ref.north_spikes_ref) | copy-start | bytes 786436
  0.0 35.7 %copy-start.4 = (f32[64,64]{1,0:T(8,128)S(1)}, f32[64,64]{1,0:T(8,128)}, u32[]{:S(2)}) copy-start(f32[64,64]{1,0:T(8,128)} %constant.21.clone.east_inverse_ref) | copy-start | bytes 49156
  0.0 41.6 %copy-start.6 = (f32[3,64]{1,0:T(4,128)S(1)}, f32[3,64]{1,0:T(4,128)}, u32[]{:S(2)}) copy-start(f32[3,64]{1,0:T(4,128)} %constant.23.clone.sweep_ref) | copy-start | bytes 2308
  17.4 5.7 %collective-permute-start = (f32[72,128]{1,0:T(8,128)S(1)}, f32[72,128]{1,0:T(8,128)S(1)}, u32[]{:S(2)}, u32[]{:S(2)}) collective-permute-start(f32[72,128]{1,0:T(8,128)S(1)} %get-tuple-element.24), channel_id=1, source_target_pairs={{0,1},{1,0},{2,3},{3,2},{4,5},{5,4},{6,7},{7,6},{8,9},{9,8},{10,11... | collective-permute-start | bytes 110600 | tf_op jit(solution)/shard_map/ppermute | solution.py:455
  20.5 5.5 %collective-permute-start.1 = (f32[72,128]{1,0:T(8,128)S(1)}, f32[72,128]{1,0:T(8,128)S(1)}, u32[]{:S(2)}, u32[]{:S(2)}) collective-permute-start(f32[72,128]{1,0:T(8,128)S(1)} %get-tuple-element.25), channel_id=1, source_target_pairs={{0,2},{1,3},{2,0},{3,1},{4,6},{5,7},{6,4},{7,5},{8,10},{9,11},{10,... | collective-permute-start | bytes 110600 | tf_op jit(solution)/shard_map/ppermute | solution.py:455
  23.1 5.8 %collective-permute-start.2 = (f32[72,128]{1,0:T(8,128)S(1)}, f32[72,128]{1,0:T(8,128)S(1)}, u32[]{:S(2)}, u32[]{:S(2)}) collective-permute-start(f32[72,128]{1,0:T(8,128)S(1)} %get-tuple-element.26), channel_id=1, source_target_pairs={{0,3},{1,2},{2,1},{3,0},{4,7},{5,6},{6,5},{7,4},{8,11},{9,10},{10,... | collective-permute-start | bytes 110600 | tf_op jit(solution)/shard_map/ppermute | solution.py:455
  29.6 1.9 %collective-permute-start.3 = (f32[72,256]{1,0:T(8,128)S(1)}, f32[72,256]{1,0:T(8,128)S(1)}, u32[]{:S(2)}, u32[]{:S(2)}) collective-permute-start(f32[72,256]{1,0:T(8,128)S(1)} %get-tuple-element.29), channel_id=1, source_target_pairs={{0,4},{4,0},{8,12},{12,8},{1,5},{5,1},{9,13},{13,9},{2,6},{6,2},{1... | collective-permute-start | bytes 221192 | tf_op jit(solution)/shard_map/ppermute | solution.py:455
  29.6 4.8 %collective-permute-start.4 = (f32[72,256]{1,0:T(8,128)S(1)}, f32[72,256]{1,0:T(8,128)S(1)}, u32[]{:S(2)}, u32[]{:S(2)}) collective-permute-start(f32[72,256]{1,0:T(8,128)S(1)} %get-tuple-element.30), channel_id=1, source_target_pairs={{0,8},{4,12},{8,0},{12,4},{1,9},{5,13},{9,1},{13,5},{2,10},{6,14},... | collective-permute-start | bytes 221192 | tf_op jit(solution)/shard_map/ppermute | solution.py:455
  31.2 4.5 %collective-permute-start.5 = (f32[72,256]{1,0:T(8,128)S(1)}, f32[72,256]{1,0:T(8,128)S(1)}, u32[]{:S(2)}, u32[]{:S(2)}) collective-permute-start(f32[72,256]{1,0:T(8,128)S(1)} %get-tuple-element.31), channel_id=1, source_target_pairs={{0,12},{4,8},{8,4},{12,0},{1,13},{5,9},{9,5},{13,1},{2,14},{6,10},... | collective-permute-start | bytes 221192 | tf_op jit(solution)/shard_map/ppermute | solution.py:455
  36.0 5.6 %collective-permute-start.6 = (f32[1,128,256]{2,1,0:T(8,128)S(1)}, f32[1,128,256]{2,1,0:T(8,128)S(1)}, u32[]{:S(2)}, u32[]{:S(2)}) collective-permute-start(f32[1,128,256]{2,1,0:T(8,128)S(1)} %get-tuple-element.32.own_ref), channel_id=1, source_target_pairs={{0,16},{16,0},{1,17},{17,1},{2,18},{18,2},{3,19},{19,3},{4,20},{20... | collective-permute-start | bytes 393224 | tf_op jit(solution)/shard_map/ppermute | solution.py:544

commit v6 on v4

--- a/solution.py
+++ b/solution.py
@@ -88,13 +88,11 @@
 def sweep_table(length, factor):
     half = 0.5 * factor
     ratio = np.zeros(length)
-    scale = np.zeros(length)
     last = 0.0
     for i in range(length):
-        scale[i] = 1.0 / (1.0 + factor - half * last)
-        ratio[i] = last = half * scale[i]
-    head = np.concatenate([[1.0], np.cumprod(ratio)[:-1]])
-    return np.stack([scale, ratio, head, np.cumprod(ratio)])
+        ratio[i] = last = half / (1.0 + factor - half * last)
+    decay = np.cumprod(ratio)
+    return np.stack([ratio, decay, decay])
 
 
 def split(table, axis):
@@ -123,7 +121,9 @@
 
 def upward_dot(values, table_ref):
     high, low = parts(values)
-    return dot(jnp.concatenate([high, low, high], axis=1), table_ref[...])
+    count, depth = values.shape
+    both = dot(jnp.concatenate([high, low], axis=0), table_ref[:depth])
+    return both[:count] + both[count:] + dot(high, table_ref[depth:])
 
 
 def north_dot(table_ref, values):
@@ -209,11 +209,12 @@
     both_ref[...] = jnp.zeros_like(both_ref)
     east_ends_ref[...] = jnp.zeros_like(east_ends_ref)
     lane = lax.broadcasted_iota(jnp.int32, (1, 2 * east), 1)
-    line = lax.broadcasted_iota(jnp.int32, (north, 1), 0)
+    line = lax.broadcasted_iota(jnp.int32, (8, 1), 0)
+    half_factor = 0.5 * factors[0]
     tables.wait()
-    up_ref[...] = tables_ref[: 3 * upward].astype(BF16)
-    north_ref[...] = tables_ref[3 * upward : 3 * upward + 2 * north, : 2 * north].astype(BF16)
-    sweep = 3 * upward + 2 * north
+    up_ref[...] = tables_ref[: 2 * upward].astype(BF16)
+    north_ref[...] = tables_ref[2 * upward : 2 * upward + 2 * north, : 2 * north].astype(BF16)
+    sweep = 2 * upward + 2 * north
     fetch(0, 0).wait()
 
     def arrive(g):
@@ -222,6 +223,12 @@
         @pl.when(g + 1 < groups)
         def _():
             fetch(0, g + 1).wait()
+
+    def shifted(values, step):
+        turned = pltpu.roll(values, step % north, 0)
+        if step > 0:
+            return jnp.concatenate([jnp.where(line == 0, 0.0, turned[:8]), turned[8:]], axis=0)
+        return jnp.concatenate([turned[:-8], jnp.where(line == 7, 0.0, turned[-8:])], axis=0)
 
     def upward_part(g, slot_ref):
         heat_list = []
@@ -230,10 +237,8 @@
             x = place(i)
             warm = warmth_ref[x + 1]
             bent = (warmth_ref[x] - warm) + (warmth_ref[x + 2] - warm)
-            low = jnp.where(line == 0, 0.0, pltpu.roll(warm, 1, 0))
-            high = jnp.where(line == north - 1, 0.0, pltpu.roll(warm, north - 1, 0))
-            bent += (factors[1] / factors[0]) * ((low - warm) + (high - warm))
-            heat_list.append((supply_ref[x] + 2.0 * warm) + factors[0] * bent)
+            across = (shifted(warm, 1) - warm) + (shifted(warm, -1) - warm)
+            heat_list.append((supply_ref[x] + 2.0 * warm) + (factors[0] * bent + factors[1] * across))
             edges_ref[pl.ds(i, 1)] = warm[:1]
             edges_ref[pl.ds(east + i, 1)] = warm[north - 1 :]
         slot_ref[...] = upward_dot(jnp.concatenate(heat_list, axis=0), up_ref)
@@ -247,14 +252,13 @@
             both = jnp.where(lane == i, heads, both_ref[...])
             both_ref[...] = jnp.where(lane == east + i, tails, both)
             solved = north_dot(north_ref, first - 2.0 * warmth_ref[place(i) + 1])
-            north_ends_ref[0, pl.ds(i, 1), :] = solved[:1]
-            north_ends_ref[1, pl.ds(i, 1), :] = solved[north - 1 :]
-            scale, ratio = (tables_ref[pl.ds(sweep + n * east + i, 1), :] for n in range(2))
-            swept = scale * solved + ratio * east_ends_ref[count - 1]
+            north_ends_ref[0, pl.ds(i, 1)] = half_factor * solved[:1]
+            north_ends_ref[1, pl.ds(i, 1)] = half_factor * solved[north - 1 :]
+            swept = solved + tables_ref[pl.ds(sweep + i, 1), :] * east_ends_ref[count - 1]
             swept_ref[i] = swept
             east_ends_ref[count - 1] = swept
             if not pair:
-                east_ends_ref[0] += tables_ref[pl.ds(sweep + 2 * east + i, 1), :] * swept
+                east_ends_ref[0] += tables_ref[pl.ds(sweep + east + i, 1), :] * swept
 
     arrive(0)
     upward_part(0, even_ref)
@@ -279,10 +283,11 @@
     ends = end_places(count, east)
     planes = [warmth_ref[place(i) + 1] for i, _ in ends]
     solved_up = upward_dot(jnp.concatenate([edges_ref[...]] + planes, axis=0), up_ref)
+    east_ends_ref[count - 1] = tables_ref[sweep + 2 * east : sweep + 2 * east + 1, :] * east_ends_ref[count - 1]
     height = north_ends_ref.shape[1]
     rows = [[], []]
     for p in range(count):
-        solved = north_dot(north_ref, solved_up[2 * east + p * north : 2 * east + (p + 1) * north])
+        solved = half_factor * north_dot(north_ref, solved_up[2 * east + p * north : 2 * east + (p + 1) * north])
         rows[0].append(solved[:1])
         rows[1].append(solved[north - 1 :])
         east_ends_ref[p] += 2.0 * solved
@@ -411,9 +416,9 @@
         columns = columns_ref[block]
         first_spike, last_spike = north_spikes_ref[0, block], north_spikes_ref[1, block]
         for i in reversed(range(east)):
-            value = swept_ref[i, block] + sweep_ref[1, i] * value
+            value = sweep_ref[0, i] * (swept_ref[i, block] + value)
             if not pair:
-                value += sweep_ref[3, i] * sides_ref[0, block]
+                value += sweep_ref[2, i] * sides_ref[0, block]
             added = (
                 columns[:, i : i + 1] * upward_spikes_ref[0:1, :]
                 + columns[:, east + i : east + i + 1] * upward_spikes_ref[1:2, :]
@@ -431,10 +436,11 @@
 
 def spread_out(messages, axis):
     members = lax.axis_size(axis)
-    return [
-        lax.ppermute(message, axis, [(k, peers(k, members, d + 1)[0]) for k in range(members)])
-        for d, message in enumerate(messages)
+    taken = [
+        lax.ppermute(messages[d], axis, [(k, peers(k, members, d + 1)[0]) for k in range(members)])
+        for d in reversed(range(len(messages)))
     ]
+    return taken[::-1]
 
 
 def local(initial_warmth, heat_supply):
@@ -442,15 +448,17 @@
     members = [lax.axis_size(axis) for axis in ("gx", "gy", "gz")]
     factors = [float((n * m) ** 2 // 4) for n, m in zip(shape, members)]
     lines = [line_tables(n, factor) for n, factor in zip(shape, factors)]
-    sweep = sweep_table(east, factors[0]).astype(np.float32)
+    sweep = sweep_table(east, factors[0])
+    ratio, weights = sweep[:2]
+    sweep = sweep.astype(np.float32)
     exchanges = [exchange_tables(line[1], line[2], m) for line, m in zip(lines, members)]
     upward_high, upward_low = split(lines[2][0], 0)
-    north_high, north_low = split(lines[1][0], 1)
+    north_high, north_low = split(lines[1][0] / (0.5 * factors[0]), 1)
     north_stack = np.block([[north_high, north_high], [north_low, np.zeros_like(north_low)]])
     tables = np.concatenate([
-        np.concatenate([upward_high, upward_high, upward_low]).astype(np.float32),
+        np.concatenate([upward_high, upward_low]).astype(np.float32),
         np.pad(north_stack.astype(np.float32), ((0, 0), (0, max(upward - 2 * north, 0)))),
-        np.repeat(sweep.reshape(-1, 1), upward, axis=1),
+        np.repeat(np.concatenate([[0.0], ratio[:-1], weights, ratio[-1:], np.zeros(7)])[:, None], upward, axis=1).astype(np.float32),
     ])
     east_inverse = lines[0][0].astype(np.float32)
     north_inverse = lines[1][0].astype(np.float32)
@@ -489,7 +497,7 @@
             pltpu.VMEM((north, 2 * east), F32),
             pltpu.VMEM((2 * east, upward), F32),
             pltpu.VMEM(tables.shape, F32),
-            pltpu.VMEM((3 * upward, upward), BF16),
+            pltpu.VMEM((2 * upward, upward), BF16),
             pltpu.VMEM((2 * north, 2 * north), BF16),
             pltpu.VMEM((group * north, upward), F32),
             pltpu.VMEM((group * north, upward), F32),

time: 46.1 us -> 46.2 us (level)
  no operation moved by 1% of the time
where the time goes in v6:
time: 46.2 us; the launch traced here: 46.1 us
  Pallas kernels  22.8 us (49%)
  waiting for transfers between devices  14 us (30%)
  starting transfers between devices  9.15 us (20%)
    pallas_call x1, Pallas kernels, local(): pl.pallas_call(functools.partial(local_kernel, pair, group, factors, exch...  16 us
    ppermute x6, waiting for transfers between devices, spread_out(): lax.ppermute(messages[d], axis, [(k, peers(k, members, d + 1)[0]) for k i...  9.94 us
    ppermute x6, starting transfers between devices, spread_out(): lax.ppermute(messages[d], axis, [(k, peers(k, members, d + 1)[0]) for k i...  7.66 us
    pallas_call x1, Pallas kernels, local(): pl.pallas_call(functools.partial(final_kernel, pair, table, tile), in_spe...  5.79 us
    ppermute x1, waiting for transfers between devices, local(): other = lax.ppermute(own, 'gx', [(0, 1), (1, 0)])  4.1 us
    ppermute x1, starting transfers between devices, local(): other = lax.ppermute(own, 'gx', [(0, 1), (1, 0)])  1.49 us
  transfers between devices with their start and end apart: 7, of which 5 were waited for; matrix products, arithmetic and copies ran while one was open for 0% of the time, Pallas kernels for 0%

profile of v6, /device:TPU:0, one launch (start us, length us, event | category | flops | bytes accessed | tf_op | source)
XLA Modules:
  0.0 46.1 jit_solution(13761023260602359142)
XLA Ops:
  0.0 0.0 copy-start.1
  0.0 0.0 copy-start.2
  0.0 0.0 copy-start.3
  0.0 0.0 copy-start.5
  0.0 0.0 copy-start
  0.0 0.0 copy-start.4
  0.0 0.0 copy-start.6
  0.0 16.0 %shard_map.100 = (f32[64,128,256]{2,1,0:T(8,128)S(1)}, f32[66,128,256]{2,1,0:T(8,128)S(1)}, f32[2,72,128]{2,1,0:T(8,128)S(1)}, f32[2,72,256]{2,1,0:T(8,128)S(1)}...) custom-call(f32[904,256]{1,0:T(8,128)} %constant.16.clone.tables_hbm, ...), custom_call_target="tpu_custom_call" | custom-call | tf_op jit(solution)/shard_map/pallas_call | solution.py:483
  16.0 3.1 %collective-permute-start = (f32[72,128]{1,0:T(8,128)S(1)}, f32[72,128]{1,0:T(8,128)S(1)}, u32[]{:S(2)}, u32[]{:S(2)}) collective-permute-start(f32[72,128]{1,0:T(8,128)S(1)} %get-tuple-element.24), channel_id=1, source_target_pairs={{0,1},{1,0},{2,3},{3,2},{4,5},{5,4},{6,7},{7,6},{8,9},{9,8},{10,11... | collective-permute-start | bytes 110600 | tf_op jit(solution)/shard_map/ppermute | solution.py:440
  19.2 2.6 %collective-permute-start.1 = (f32[72,128]{1,0:T(8,128)S(1)}, f32[72,128]{1,0:T(8,128)S(1)}, u32[]{:S(2)}, u32[]{:S(2)}) collective-permute-start(f32[72,128]{1,0:T(8,128)S(1)} %get-tuple-element.25), channel_id=1, source_target_pairs={{0,2},{1,3},{2,0},{3,1},{4,6},{5,7},{6,4},{7,5},{8,10},{9,11},{10,... | collective-permute-start | bytes 110600 | tf_op jit(solution)/shard_map/ppermute | solution.py:440
  21.8 0.0 collective-permute-start.2
  21.8 0.0 collective-permute-done.rest_0_
  21.8 2.9 %collective-permute-done.1.rest_1_ = f32[72,128]{1,0:T(8,128)S(1)} collective-permute-done((f32[72,128]{1,0:T(8,128)S(1)}, f32[72,128]{1,0:T(8,128)S(1)}, u32[]{:S(2)}, u32[]{:S(2)}) %collective-permute-start.1) | collective-permute-done | bytes 36896 | tf_op jit(solution)/shard_map/ppermute | solution.py:440
  24.7 2.8 %collective-permute-done.2.rest_2_ = f32[72,128]{1,0:T(8,128)S(1)} collective-permute-done((f32[72,128]{1,0:T(8,128)S(1)}, f32[72,128]{1,0:T(8,128)S(1)}, u32[]{:S(2)}, u32[]{:S(2)}) %collective-permute-start.2) | collective-permute-done | bytes 36896 | tf_op jit(solution)/shard_map/ppermute | solution.py:440
  27.5 0.0 copy-done.1
  27.5 0.0 copy-done.2
  27.5 0.0 copy-done.3
  27.5 0.0 copy-done.5
  27.5 0.7 %shard_map.101 = (f32[128,128]{1,0:T(8,128)S(1)}, f32[2,72,256]{2,1,0:T(8,128)S(1)}, f32[1,128,256]{2,1,0:T(8,128)S(1)}, f32[72,256]{1,0:T(8,128)S(1)}, f32[72,256]{1,0:T(8,128)S(1)}, /*index=5*/f32[72,256]{1,0:T(8,128)S(1)}) custom-call(f32[2,72,128]{2,1,0:T(8,128)S(1)} %get-tuple-element.21.ends_ref, f32[2,72,256]{2,1,0:T(8,128)S(1)} %get-tuple-element.22.north_ends_ref, ...), custom_call_target="tpu_custom_call" | custom-call | tf_op jit(solution)/shard_map/pallas_call | solution.py:510
  28.2 0.1 collective-permute-start.3
  28.3 1.6 %collective-permute-start.4 = (f32[72,256]{1,0:T(8,128)S(1)}, f32[72,256]{1,0:T(8,128)S(1)}, u32[]{:S(2)}, u32[]{:S(2)}) collective-permute-start(f32[72,256]{1,0:T(8,128)S(1)} %get-tuple-element.30), channel_id=1, source_target_pairs={{0,8},{4,12},{8,0},{12,4},{1,9},{5,13},{9,1},{13,5},{2,10},{6,14},... | collective-permute-start | bytes 221192 | tf_op jit(solution)/shard_map/ppermute | solution.py:440
  29.9 0.3 collective-permute-start.5
  30.2 0.0 collective-permute-done.3.rest_0_
  30.2 3.0 %collective-permute-done.4.rest_1_ = f32[72,256]{1,0:T(8,128)S(1)} collective-permute-done((f32[72,256]{1,0:T(8,128)S(1)}, f32[72,256]{1,0:T(8,128)S(1)}, u32[]{:S(2)}, u32[]{:S(2)}) %collective-permute-start.4) | collective-permute-done | bytes 73760 | tf_op jit(solution)/shard_map/ppermute | solution.py:440
  33.2 1.2 %collective-permute-done.5.rest_2_ = f32[72,256]{1,0:T(8,128)S(1)} collective-permute-done((f32[72,256]{1,0:T(8,128)S(1)}, f32[72,256]{1,0:T(8,128)S(1)}, u32[]{:S(2)}, u32[]{:S(2)}) %collective-permute-start.5) | collective-permute-done | bytes 73760 | tf_op jit(solution)/shard_map/ppermute | solution.py:440
  34.4 0.0 copy-done
  34.4 0.0 copy-done.4
  34.4 0.3 shard_map.102
  34.7 1.5 %collective-permute-start.6 = (f32[1,128,256]{2,1,0:T(8,128)S(1)}, f32[1,128,256]{2,1,0:T(8,128)S(1)}, u32[]{:S(2)}, u32[]{:S(2)}) collective-permute-start(f32[1,128,256]{2,1,0:T(8,128)S(1)} %get-tuple-element.32.own_ref), channel_id=1, source_target_pairs={{0,16},{16,0},{1,17},{17,1},{2,18},{18,2},{3,19},{19,3},{4,20},{20... | collective-permute-start | bytes 393224 | tf_op jit(solution)/shard_map/ppermute | solution.py:529
  36.2 4.1 %collective-permute-done.6.other_ref = f32[1,128,256]{2,1,0:T(8,128)S(1)} collective-permute-done((f32[1,128,256]{2,1,0:T(8,128)S(1)}, f32[1,128,256]{2,1,0:T(8,128)S(1)}, u32[]{:S(2)}, u32[]{:S(2)}) %collective-permute-start.6) | collective-permute-done | bytes 131104 | tf_op jit(solution)/shard_map/ppermute | solution.py:529
  40.3 0.0 copy-done.6
  40.3 5.8 %shard_map.103 = f32[64,128,256]{2,1,0:T(8,128)} custom-call(f32[3,64]{1,0:T(4,128)S(1)} %copy-done.6, f32[1,128,256]{2,1,0:T(8,128)S(1)} %get-tuple-element.32.own_ref, f32[1,128,256]{2,1,0:T(8,128)S(1)} %collective-permute-done.6.other_ref, f32[64,128,256]{2,1,0:T(8,128)S(1)} %get-tuple-element.33.swept_ref, ...), custom_call_target="tpu_custom_call" | custom-call | tf_op jit(solution)/shard_map/pallas_call | solution.py:538
Async XLA Ops:
  0.0 27.5 %copy-start.1 = (f32[128,256]{1,0:T(8,128)S(1)}, f32[128,256]{1,0:T(8,128)}, u32[]{:S(2)}) copy-start(f32[128,256]{1,0:T(8,128)} %constant.20.clone.spread_ref) | copy-start | bytes 393220
  0.0 27.5 %copy-start.2 = (f32[128,128]{1,0:T(8,128)S(1)}, f32[128,128]{1,0:T(8,128)}, u32[]{:S(2)}) copy-start(f32[128,128]{1,0:T(8,128)} %constant.18.clone.east_twice_ref) | copy-start | bytes 196612
  0.0 27.5 %copy-start.3 = (f32[128,128]{1,0:T(8,128)S(1)}, f32[128,128]{1,0:T(8,128)}, u32[]{:S(2)}) copy-start(f32[128,128]{1,0:T(8,128)} %constant.17.clone.north_inverse_ref) | copy-start | bytes 196612
  0.0 27.5 %copy-start.5 = (f32[2,256]{1,0:T(2,128)S(1)}, f32[2,256]{1,0:T(2,128)}, u32[]{:S(2)}) copy-start(f32[2,256]{1,0:T(2,128)} %constant.19.clone.spikes_ref.upward_spikes_ref) | copy-start | bytes 6148
  0.0 34.4 %copy-start = (f32[2,128,256]{2,1,0:T(8,128)S(1)}, f32[2,128,256]{2,1,0:T(8,128)}, u32[]{:S(2)}) copy-start(f32[2,128,256]{2,1,0:T(8,128)} %constant.22.clone.spikes_ref.north_spikes_ref) | copy-start | bytes 786436
  0.0 34.4 %copy-start.4 = (f32[64,64]{1,0:T(8,128)S(1)}, f32[64,64]{1,0:T(8,128)}, u32[]{:S(2)}) copy-start(f32[64,64]{1,0:T(8,128)} %constant.21.clone.east_inverse_ref) | copy-start | bytes 49156
  0.0 40.3 %copy-start.6 = (f32[3,64]{1,0:T(4,128)S(1)}, f32[3,64]{1,0:T(4,128)}, u32[]{:S(2)}) copy-start(f32[3,64]{1,0:T(4,128)} %constant.23.clone.sweep_ref) | copy-start | bytes 2308
  16.0 5.7 %collective-permute-start = (f32[72,128]{1,0:T(8,128)S(1)}, f32[72,128]{1,0:T(8,128)S(1)}, u32[]{:S(2)}, u32[]{:S(2)}) collective-permute-start(f32[72,128]{1,0:T(8,128)S(1)} %get-tuple-element.24), channel_id=1, source_target_pairs={{0,1},{1,0},{2,3},{3,2},{4,5},{5,4},{6,7},{7,6},{8,9},{9,8},{10,11... | collective-permute-start | bytes 110600 | tf_op jit(solution)/shard_map/ppermute | solution.py:440
  19.2 5.5 %collective-permute-start.1 = (f32[72,128]{1,0:T(8,128)S(1)}, f32[72,128]{1,0:T(8,128)S(1)}, u32[]{:S(2)}, u32[]{:S(2)}) collective-permute-start(f32[72,128]{1,0:T(8,128)S(1)} %get-tuple-element.25), channel_id=1, source_target_pairs={{0,2},{1,3},{2,0},{3,1},{4,6},{5,7},{6,4},{7,5},{8,10},{9,11},{10,... | collective-permute-start | bytes 110600 | tf_op jit(solution)/shard_map/ppermute | solution.py:440
  21.8 5.8 %collective-permute-start.2 = (f32[72,128]{1,0:T(8,128)S(1)}, f32[72,128]{1,0:T(8,128)S(1)}, u32[]{:S(2)}, u32[]{:S(2)}) collective-permute-start(f32[72,128]{1,0:T(8,128)S(1)} %get-tuple-element.26), channel_id=1, source_target_pairs={{0,3},{1,2},{2,1},{3,0},{4,7},{5,6},{6,5},{7,4},{8,11},{9,10},{10,... | collective-permute-start | bytes 110600 | tf_op jit(solution)/shard_map/ppermute | solution.py:440
  28.2 1.9 %collective-permute-start.3 = (f32[72,256]{1,0:T(8,128)S(1)}, f32[72,256]{1,0:T(8,128)S(1)}, u32[]{:S(2)}, u32[]{:S(2)}) collective-permute-start(f32[72,256]{1,0:T(8,128)S(1)} %get-tuple-element.29), channel_id=1, source_target_pairs={{0,4},{4,0},{8,12},{12,8},{1,5},{5,1},{9,13},{13,9},{2,6},{6,2},{1... | collective-permute-start | bytes 221192 | tf_op jit(solution)/shard_map/ppermute | solution.py:440
  28.3 4.8 %collective-permute-start.4 = (f32[72,256]{1,0:T(8,128)S(1)}, f32[72,256]{1,0:T(8,128)S(1)}, u32[]{:S(2)}, u32[]{:S(2)}) collective-permute-start(f32[72,256]{1,0:T(8,128)S(1)} %get-tuple-element.30), channel_id=1, source_target_pairs={{0,8},{4,12},{8,0},{12,4},{1,9},{5,13},{9,1},{13,5},{2,10},{6,14},... | collective-permute-start | bytes 221192 | tf_op jit(solution)/shard_map/ppermute | solution.py:440
  29.9 4.5 %collective-permute-start.5 = (f32[72,256]{1,0:T(8,128)S(1)}, f32[72,256]{1,0:T(8,128)S(1)}, u32[]{:S(2)}, u32[]{:S(2)}) collective-permute-start(f32[72,256]{1,0:T(8,128)S(1)} %get-tuple-element.31), channel_id=1, source_target_pairs={{0,12},{4,8},{8,4},{12,0},{1,13},{5,9},{9,5},{13,1},{2,14},{6,10},... | collective-permute-start | bytes 221192 | tf_op jit(solution)/shard_map/ppermute | solution.py:440
  34.7 5.6 %collective-permute-start.6 = (f32[1,128,256]{2,1,0:T(8,128)S(1)}, f32[1,128,256]{2,1,0:T(8,128)S(1)}, u32[]{:S(2)}, u32[]{:S(2)}) collective-permute-start(f32[1,128,256]{2,1,0:T(8,128)S(1)} %get-tuple-element.32.own_ref), channel_id=1, source_target_pairs={{0,16},{16,0},{1,17},{17,1},{2,18},{18,2},{3,19},{19,3},{4,20},{20... | collective-permute-start | bytes 393224 | tf_op jit(solution)/shard_map/ppermute | solution.py:529

commit v7 on v6

--- a/solution.py
+++ b/solution.py
@@ -161,6 +161,10 @@
     return jnp.sum(jnp.where(diagonal(column.shape[0]), column, 0.0), axis=0, keepdims=True)
 
 
+def as_column(row):
+    return jnp.sum(jnp.where(diagonal(row.shape[1]), row, 0.0), axis=1, keepdims=True)
+
+
 def stacked(rows, height):
     filler = jnp.zeros((height - sum(row.shape[0] for row in rows), rows[0].shape[1]), F32)
     return jnp.concatenate(list(rows) + [filler], axis=0)
@@ -247,10 +251,10 @@
         for k in range(group):
             i = g * group + k
             first = slot_ref[k * north : (k + 1) * north]
-            heads = pltpu.roll(first[:, : 2 * east], i, 1)
-            tails = pltpu.roll(first[:, upward - 2 * east :], east + 1 + i, 1)
-            both = jnp.where(lane == i, heads, both_ref[...])
-            both_ref[...] = jnp.where(lane == east + i, tails, both)
+            both = jnp.where(lane < east, first[:, : 2 * east], first[:, upward - 2 * east :])
+            both = pltpu.roll(both, i, 1)
+            both_ref[0] = jnp.where(lane == i, both, both_ref[0])
+            both_ref[1] = jnp.where(lane == lax.rem(i + 2 * east - 1, 2 * east), both, both_ref[1])
             solved = north_dot(north_ref, first - 2.0 * warmth_ref[place(i) + 1])
             north_ends_ref[0, pl.ds(i, 1)] = half_factor * solved[:1]
             north_ends_ref[1, pl.ds(i, 1)] = half_factor * solved[north - 1 :]
@@ -296,11 +300,11 @@
         north_ends_ref[end, east:] = stacked(rows[end], height - east)
 
     half = north // 2
-    top, bottom = both_ref[:half], both_ref[half:]
-    folded = (
-        jnp.where(lane < east, top, pltpu.roll(bottom, east, 1)),
-        jnp.where(lane < east, pltpu.roll(top, east, 1), bottom),
-    )
+    folded = []
+    for end in range(2):
+        top, bottom = both_ref[end, :half], both_ref[end, half:]
+        top, bottom = pltpu.roll(top, end, 1), pltpu.roll(bottom, east + end, 1)
+        folded.append(jnp.where(lane < east, top, bottom))
     upward_ends = []
     for end, column in enumerate((slice(0, 1), slice(upward - 1, upward))):
         extra = [as_row(solved_up[k * north : (k + 1) * north, column]) for k in range(1 + count)]
@@ -311,11 +315,11 @@
 
 def upward_kernel(
     count, taking, sending,
-    ends_ref, north_ends_ref, east_ends_ref, north_inverse_ref, east_twice_ref, spikes_ref, spread_ref, *rest,
+    ends_ref, north_ends_ref, north_inverse_ref, east_twice_ref, spread_ref, *rest,
 ):
     taken = (taking.shape[1] - 8) // 2
     message_refs = rest[:taken]
-    columns_ref, north_out_ref, east_out_ref, *out_refs = rest[taken:]
+    columns_ref, north_out_ref, plane_ref, *out_refs = rest[taken:]
     north, lanes = columns_ref.shape
     east, half = lanes // 2, north // 2
     lane = lax.broadcasted_iota(jnp.int32, (1, lanes), 1)
@@ -358,35 +362,33 @@
         north_out_ref[end] = ends[end]
     send_all(ends, sending, lax.axis_index("gy"), out_refs)
     for i, k in end_places(count, east):
-        total = east_ends_ref[k]
+        rows = []
         for side in range(2):
-            column = columns[:, side * east + i : side * east + i + 1] + 2.0 * planes[k][side]
-            total += column * spikes_ref[side : side + 1, :]
-        east_out_ref[k] = total
+            rows.append(as_row(columns[:, side * east + i : side * east + i + 1] + 2.0 * planes[k][side]))
+        plane_ref[k] = stacked(rows, 8)
 
 
 def north_kernel(
     count, taking,
-    ends_ref, east_ends_ref, east_inverse_ref, spikes_ref, *rest,
+    ends_ref, plane_ref, east_inverse_ref, *rest,
 ):
     taken = (taking.shape[1] - 8) // 2
     message_refs = rest[:taken]
-    rows_ref, east_out_ref = rest[taken:]
-    east = rows_ref.shape[1]
+    rows_ref, small_ref = rest[taken:]
+    _, east, upward = rows_ref.shape
     sides = take_all((ends_ref[0], ends_ref[1]), taking, lax.axis_index("gy"), [ref[...] for ref in message_refs])
     swept = [exact_dot(east_inverse_ref[...], side[:east]) for side in sides]
     for n in range(2):
         rows_ref[n] = swept[n]
     for i, k in end_places(count, east):
-        total = east_ends_ref[k]
-        for n in range(2):
-            total += spikes_ref[n] * (swept[n][i : i + 1] + 2.0 * sides[n][east + k : east + k + 1])
-        east_out_ref[k] = total
+        rows = [swept[n][i : i + 1] + 2.0 * sides[n][east + k : east + k + 1] for n in range(2)]
+        wide = jnp.concatenate([plane_ref[k], jnp.zeros((8, upward - plane_ref.shape[2]), F32)], axis=1)
+        small_ref[k] = stacked(rows + [wide[:2]], 8)
 
 
 def final_kernel(
     pair, table, tile,
-    sweep_ref, own_ref, other_ref,
+    sweep_ref, own_ref, other_ref, own_small_ref, other_small_ref,
     swept_ref, warmth_ref, columns_ref, rows_ref, upward_spikes_ref, north_spikes_ref,
     out_hbm,
     out_ref, sides_ref, sems,
@@ -394,16 +396,28 @@
     east, north, upward = out_ref.shape
     place = ordered(pair, east)
 
+    def widened(plane, small):
+        for side in range(2):
+            plane += north_spikes_ref[side] * small[side : side + 1]
+            plane += as_column(small[2 + side : 3 + side, :north]) * upward_spikes_ref[side : side + 1, :]
+        return plane
+
     if pair:
-        sides_ref[0] = float(table[0]) * other_ref[0] + float(table[1]) * own_ref[0]
+        near, far = float(table[0]), float(table[1])
+        sides_ref[0] = widened(
+            near * other_ref[0] + far * own_ref[0], near * other_small_ref[0] + far * own_small_ref[0]
+        )
     else:
         me = lax.axis_index("gx")
+        members = table.shape[0]
         for side in range(2):
-            plane = 0.0
-            for m in range(table.shape[0]):
+            plane, small = 0.0, 0.0
+            for m in range(members):
                 for end in range(2):
-                    plane += pick(table[:, side, 2 * m + end], me) * other_ref[m, end]
-            sides_ref[side] = plane
+                    weight = pick(table[:, side, 2 * m + end], me)
+                    plane += weight * other_ref[m, end]
+                    small += weight * other_small_ref[m, end]
+            sides_ref[side] = widened(plane, small)
     last = sides_ref.shape[0] - 1
 
     def send(t):
@@ -480,7 +494,7 @@
 
     group = 4
     folded = kept(north // 2 + 8, 2 * east)
-    swept, warmth, upward_ends, north_ends, east_ends, *messages = pl.pallas_call(
+    swept, warmth, upward_ends, north_ends, own, *messages = pl.pallas_call(
         functools.partial(local_kernel, pair, group, factors, exchanges[2][0]),
         in_specs=[hbm] * 3,
         out_specs=[vmem] * (5 + to_up),
@@ -494,7 +508,7 @@
         + [folded] * to_up,
         scratch_shapes=[
             pltpu.VMEM(shape, F32),
-            pltpu.VMEM((north, 2 * east), F32),
+            pltpu.VMEM((2, north, 2 * east), F32),
             pltpu.VMEM((2 * east, upward), F32),
             pltpu.VMEM(tables.shape, F32),
             pltpu.VMEM((2 * upward, upward), BF16),
@@ -507,37 +521,41 @@
     )(pltpu.with_memory_space_constraint(jnp.asarray(tables), pltpu.HBM), initial_warmth, heat_supply)
 
     messages = spread_out(messages, "gz")
-    columns, north_ends, east_ends, *messages = pl.pallas_call(
+    if pair:
+        other = lax.ppermute(own, "gx", [(0, 1), (1, 0)])
+    else:
+        other = lax.all_gather(own, "gx")
+    columns, north_ends, planes, *messages = pl.pallas_call(
         functools.partial(upward_kernel, count, exchanges[2][1], exchanges[1][0]),
-        in_specs=[vmem] * (7 + to_up),
+        in_specs=[vmem] * (5 + to_up),
         out_specs=[vmem] * (3 + to_north),
-        out_shape=[kept(north, 2 * east), kept(2, height, upward), kept(count, north, upward)]
+        out_shape=[kept(north, 2 * east), kept(2, height, upward), kept(count, 8, north)]
         + [kept(height, upward)] * to_north,
         compiler_params=pltpu.CompilerParams(vmem_limit_bytes=6 * MIB),
-    )(upward_ends, north_ends, east_ends, north_inverse, east_twice, upward_spikes, spread, *messages)
+    )(upward_ends, north_ends, north_inverse, east_twice, spread, *messages)
 
     messages = spread_out(messages, "gy")
-    rows, own = pl.pallas_call(
+    rows, own_small = pl.pallas_call(
         functools.partial(north_kernel, count, exchanges[1][1]),
-        in_specs=[vmem] * (4 + to_north),
+        in_specs=[vmem] * (3 + to_north),
         out_specs=[vmem] * 2,
-        out_shape=[kept(2, east, upward), kept(count, north, upward)],
+        out_shape=[kept(2, east, upward), kept(count, 8, upward)],
         compiler_params=pltpu.CompilerParams(vmem_limit_bytes=6 * MIB),
-    )(north_ends, east_ends, east_inverse, north_spikes, *messages)
+    )(north_ends, planes, east_inverse, *messages)
 
     if pair:
-        other = lax.ppermute(own, "gx", [(0, 1), (1, 0)])
+        other_small = lax.ppermute(own_small, "gx", [(0, 1), (1, 0)])
         near = lines[0][1][0]
         table = np.array([1.0, near]) / (1.0 - near**2)
     else:
-        other = lax.all_gather(own, "gx")
+        other_small = lax.all_gather(own_small, "gx")
         table = interface_table(lines[0][1], lines[0][2], members[0])
     swept = pltpu.with_memory_space_constraint(swept, pltpu.VMEM)
     warmth = pltpu.with_memory_space_constraint(warmth, pltpu.VMEM)
     tile = 32
     return pl.pallas_call(
         functools.partial(final_kernel, pair, table, tile),
-        in_specs=[smem] + [vmem] * 8,
+        in_specs=[smem] + [vmem] * 10,
         out_specs=hbm,
         out_shape=kept(*shape),
         scratch_shapes=[
@@ -546,7 +564,7 @@
             pltpu.SemaphoreType.DMA((north // tile,)),
         ],
         compiler_params=pltpu.CompilerParams(vmem_limit_bytes=16 * MIB),
-    )(sweep, own, other, swept, warmth, columns, rows, upward_spikes, north_spikes)
+    )(sweep, own, other, own_small, other_small, swept, warmth, columns, rows, upward_spikes, north_spikes)
 
 
 def solution(mesh):

time: 46.2 us -> 45.9 us (level)
  waiting for transfers between devices: 14 us -> 12.9 us
  starting transfers between devices: 9.15 us -> 9.96 us
    ppermute x1, waiting for transfers between devices: 4.1 us -> 0.01 us  [local(): other = lax.ppermute(own, 'gx', [(0, 1), (1, 0)])]
    ppermute x0 -> x1, waiting for transfers between devices: none -> 3.14 us  [local(): other_small = lax.ppermute(own_small, 'gx', [(0, 1), (1, 0)])]
    ppermute x1, starting transfers between devices: 1.49 us -> 3.07 us  [local(): other = lax.ppermute(own, 'gx', [(0, 1), (1, 0)])]
    ppermute x6, starting transfers between devices: 7.66 us -> 6.32 us  [spread_out(): lax.ppermute(messages[d], axis, [(k, peers(k, members, d + 1)[0]) for k i...]
    ppermute x0 -> x1, starting transfers between devices: none -> 0.57 us  [local(): other_small = lax.ppermute(own_small, 'gx', [(0, 1), (1, 0)])]
  transfers between devices with their start and end apart: 7 -> 8, of which waited for: 5 -> 5; matrix products, arithmetic and copies ran while one was open for 0% -> 0% of each run, Pallas kernels for 0% -> 2%
where the time goes in v7:
time: 45.9 us; the launch traced here: 45.8 us
  Pallas kernels  22.9 us (50%)
  waiting for transfers between devices  12.9 us (28%)
  starting transfers between devices  9.96 us (22%)
    pallas_call x1, Pallas kernels, local(): pl.pallas_call(functools.partial(local_kernel, pair, group, factors, exch...  16 us
    ppermute x6, waiting for transfers between devices, spread_out(): lax.ppermute(messages[d], axis, [(k, peers(k, members, d + 1)[0]) for k i...  9.7 us
    ppermute x6, starting transfers between devices, spread_out(): lax.ppermute(messages[d], axis, [(k, peers(k, members, d + 1)[0]) for k i...  6.32 us
    pallas_call x1, Pallas kernels, local(): pl.pallas_call(functools.partial(final_kernel, pair, table, tile), in_spe...  5.9 us
    ppermute x1, waiting for transfers between devices, local(): other_small = lax.ppermute(own_small, 'gx', [(0, 1), (1, 0)])  3.14 us
    ppermute x1, starting transfers between devices, local(): other = lax.ppermute(own, 'gx', [(0, 1), (1, 0)])  3.07 us
  transfers between devices with their start and end apart: 8, of which 5 were waited for; matrix products, arithmetic and copies ran while one was open for 0% of the time, Pallas kernels for 2%

profile of v7, /device:TPU:0, one launch (start us, length us, event | category | flops | bytes accessed | tf_op | source)
XLA Modules:
  0.0 45.8 jit_solution(6611336019665774993)
XLA Ops:
  0.0 0.0 copy-start.1
  0.0 0.0 copy-start.2
  0.0 0.0 copy-start.3
  0.0 0.0 copy-start.4
  0.0 0.0 copy-start
  0.0 0.0 copy-start.5
  0.0 0.0 copy-start.6
  0.0 16.0 %shard_map.100 = (f32[64,128,256]{2,1,0:T(8,128)S(1)}, f32[66,128,256]{2,1,0:T(8,128)S(1)}, f32[2,72,128]{2,1,0:T(8,128)S(1)}, f32[2,72,256]{2,1,0:T(8,128)S(1)}...) custom-call(f32[904,256]{1,0:T(8,128)} %constant.16.clone.tables_hbm, ...), custom_call_target="tpu_custom_call" | custom-call | tf_op jit(solution)/shard_map/pallas_call | solution.py:497
  16.0 3.1 %collective-permute-start = (f32[1,128,256]{2,1,0:T(8,128)S(1)}, f32[1,128,256]{2,1,0:T(8,128)S(1)}, u32[]{:S(2)}, u32[]{:S(2)}) collective-permute-start(f32[1,128,256]{2,1,0:T(8,128)S(1)} %get-tuple-element.21.own_ref), channel_id=1, source_target_pairs={{0,16},{16,0},{1,17},{17,1},{2,18},{18,2},{3,19},{19,3},{4,20},{20... | collective-permute-start | bytes 393224 | tf_op jit(solution)/shard_map/ppermute | solution.py:525
  19.1 1.6 %collective-permute-start.1 = (f32[72,128]{1,0:T(8,128)S(1)}, f32[72,128]{1,0:T(8,128)S(1)}, u32[]{:S(2)}, u32[]{:S(2)}) collective-permute-start(f32[72,128]{1,0:T(8,128)S(1)} %get-tuple-element.24), channel_id=1, source_target_pairs={{0,1},{1,0},{2,3},{3,2},{4,5},{5,4},{6,7},{7,6},{8,9},{9,8},{10,11... | collective-permute-start | bytes 110600 | tf_op jit(solution)/shard_map/ppermute | solution.py:454
  20.7 2.6 %collective-permute-start.2 = (f32[72,128]{1,0:T(8,128)S(1)}, f32[72,128]{1,0:T(8,128)S(1)}, u32[]{:S(2)}, u32[]{:S(2)}) collective-permute-start(f32[72,128]{1,0:T(8,128)S(1)} %get-tuple-element.25), channel_id=1, source_target_pairs={{0,2},{1,3},{2,0},{3,1},{4,6},{5,7},{6,4},{7,5},{8,10},{9,11},{10,... | collective-permute-start | bytes 110600 | tf_op jit(solution)/shard_map/ppermute | solution.py:454
  23.2 0.2 collective-permute-start.3
  23.5 0.0 collective-permute-done.1.rest_0_
  23.5 2.4 %collective-permute-done.2.rest_1_ = f32[72,128]{1,0:T(8,128)S(1)} collective-permute-done((f32[72,128]{1,0:T(8,128)S(1)}, f32[72,128]{1,0:T(8,128)S(1)}, u32[]{:S(2)}, u32[]{:S(2)}) %collective-permute-start.2) | collective-permute-done | bytes 36896 | tf_op jit(solution)/shard_map/ppermute | solution.py:454
  25.9 3.1 %collective-permute-done.3.rest_2_ = f32[72,128]{1,0:T(8,128)S(1)} collective-permute-done((f32[72,128]{1,0:T(8,128)S(1)}, f32[72,128]{1,0:T(8,128)S(1)}, u32[]{:S(2)}, u32[]{:S(2)}) %collective-permute-start.3) | collective-permute-done | bytes 36896 | tf_op jit(solution)/shard_map/ppermute | solution.py:454
  29.0 0.0 copy-done.1
  29.0 0.0 copy-done.2
  29.0 0.0 copy-done.3
  29.0 0.7 %shard_map.101 = (f32[128,128]{1,0:T(8,128)S(1)}, f32[2,72,256]{2,1,0:T(8,128)S(1)}, f32[1,8,128]{2,1,0:T(8,128)S(1)}, f32[72,256]{1,0:T(8,128)S(1)}, f32[72,256]{1,0:T(8,128)S(1)}, /*index=5*/f32[72,256]{1,0:T(8,128)S(1)}) custom-call(f32[2,72,128]{2,1,0:T(8,128)S(1)} %get-tuple-element.22.ends_ref, f32[2,72,256]{2,1,0:T(8,128)S(1)} %get-tuple-element.23.north_ends_ref, ...), custom_call_target="tpu_custom_call" | custom-call | tf_op jit(solution)/shard_map/pallas_call | solution.py:528
  29.7 0.1 collective-permute-start.4
  29.8 1.6 %collective-permute-start.5 = (f32[72,256]{1,0:T(8,128)S(1)}, f32[72,256]{1,0:T(8,128)S(1)}, u32[]{:S(2)}, u32[]{:S(2)}) collective-permute-start(f32[72,256]{1,0:T(8,128)S(1)} %get-tuple-element.30), channel_id=1, source_target_pairs={{0,8},{4,12},{8,0},{12,4},{1,9},{5,13},{9,1},{13,5},{2,10},{6,14},... | collective-permute-start | bytes 221192 | tf_op jit(solution)/shard_map/ppermute | solution.py:454
  31.4 0.3 collective-permute-start.6
  31.7 0.0 collective-permute-done.4.rest_0_
  31.7 3.0 %collective-permute-done.5.rest_1_ = f32[72,256]{1,0:T(8,128)S(1)} collective-permute-done((f32[72,256]{1,0:T(8,128)S(1)}, f32[72,256]{1,0:T(8,128)S(1)}, u32[]{:S(2)}, u32[]{:S(2)}) %collective-permute-start.5) | collective-permute-done | bytes 73760 | tf_op jit(solution)/shard_map/ppermute | solution.py:454
  34.6 1.2 %collective-permute-done.6.rest_2_ = f32[72,256]{1,0:T(8,128)S(1)} collective-permute-done((f32[72,256]{1,0:T(8,128)S(1)}, f32[72,256]{1,0:T(8,128)S(1)}, u32[]{:S(2)}, u32[]{:S(2)}) %collective-permute-start.6) | collective-permute-done | bytes 73760 | tf_op jit(solution)/shard_map/ppermute | solution.py:454
  35.8 0.0 copy-done.4
  35.8 0.3 shard_map.102
  36.2 0.6 %collective-permute-start.7 = (f32[1,8,256]{2,1,0:T(8,128)S(1)}, f32[1,8,256]{2,1,0:T(8,128)S(1)}, u32[]{:S(2)}, u32[]{:S(2)}) collective-permute-start(f32[1,8,256]{2,1,0:T(8,128)S(1)} %get-tuple-element.32.own_small_ref), channel_id=1, source_target_pairs={{0,16},{16,0},{1,17},{17,1},{2,18},{18,2},{3,19},{19,3},{4,20},{20... | collective-permute-start | bytes 24584 | tf_op jit(solution)/shard_map/ppermute | solution.py:547
  36.7 3.1 %collective-permute-done.7.other_small_ref = f32[1,8,256]{2,1,0:T(8,128)S(1)} collective-permute-done((f32[1,8,256]{2,1,0:T(8,128)S(1)}, f32[1,8,256]{2,1,0:T(8,128)S(1)}, u32[]{:S(2)}, u32[]{:S(2)}) %collective-permute-start.7) | collective-permute-done | bytes 8224 | tf_op jit(solution)/shard_map/ppermute | solution.py:547
  39.9 0.0 collective-permute-done.other_ref
  39.9 0.0 copy-done
  39.9 0.0 copy-done.5
  39.9 0.0 copy-done.6
  39.9 5.9 %shard_map.103 = f32[64,128,256]{2,1,0:T(8,128)} custom-call(f32[3,64]{1,0:T(4,128)S(1)} %copy-done.6, f32[1,128,256]{2,1,0:T(8,128)S(1)} %get-tuple-element.21.own_ref, f32[1,128,256]{2,1,0:T(8,128)S(1)} %collective-permute-done.other_ref, f32[1,8,256]{2,1,0:T(8,128)S(1)} %get-tuple-element.32.own_small_ref, ...), custom_call_target="tpu_custom_call" | custom-call | tf_op jit(solution)/shard_map/pallas_call | solution.py:556
Async XLA Ops:
  0.0 29.0 %copy-start.1 = (f32[128,256]{1,0:T(8,128)S(1)}, f32[128,256]{1,0:T(8,128)}, u32[]{:S(2)}) copy-start(f32[128,256]{1,0:T(8,128)} %constant.19.clone.spread_ref) | copy-start | bytes 393220
  0.0 29.0 %copy-start.2 = (f32[128,128]{1,0:T(8,128)S(1)}, f32[128,128]{1,0:T(8,128)}, u32[]{:S(2)}) copy-start(f32[128,128]{1,0:T(8,128)} %constant.18.clone.east_twice_ref) | copy-start | bytes 196612
  0.0 29.0 %copy-start.3 = (f32[128,128]{1,0:T(8,128)S(1)}, f32[128,128]{1,0:T(8,128)}, u32[]{:S(2)}) copy-start(f32[128,128]{1,0:T(8,128)} %constant.17.clone.north_inverse_ref) | copy-start | bytes 196612
  0.0 35.8 %copy-start.4 = (f32[64,64]{1,0:T(8,128)S(1)}, f32[64,64]{1,0:T(8,128)}, u32[]{:S(2)}) copy-start(f32[64,64]{1,0:T(8,128)} %constant.20.clone.east_inverse_ref) | copy-start | bytes 49156
  0.0 39.9 %copy-start = (f32[2,128,256]{2,1,0:T(8,128)S(1)}, f32[2,128,256]{2,1,0:T(8,128)}, u32[]{:S(2)}) copy-start(f32[2,128,256]{2,1,0:T(8,128)} %constant.23.clone.north_spikes_ref) | copy-start | bytes 786436
  0.0 39.9 %copy-start.5 = (f32[2,256]{1,0:T(2,128)S(1)}, f32[2,256]{1,0:T(2,128)}, u32[]{:S(2)}) copy-start(f32[2,256]{1,0:T(2,128)} %constant.22.clone.upward_spikes_ref) | copy-start | bytes 6148
  0.0 39.9 %copy-start.6 = (f32[3,64]{1,0:T(4,128)S(1)}, f32[3,64]{1,0:T(4,128)}, u32[]{:S(2)}) copy-start(f32[3,64]{1,0:T(4,128)} %constant.21.clone.sweep_ref) | copy-start | bytes 2308
  16.0 23.9 %collective-permute-start = (f32[1,128,256]{2,1,0:T(8,128)S(1)}, f32[1,128,256]{2,1,0:T(8,128)S(1)}, u32[]{:S(2)}, u32[]{:S(2)}) collective-permute-start(f32[1,128,256]{2,1,0:T(8,128)S(1)} %get-tuple-element.21.own_ref), channel_id=1, source_target_pairs={{0,16},{16,0},{1,17},{17,1},{2,18},{18,2},{3,19},{19,3},{4,20},{20... | collective-permute-start | bytes 393224 | tf_op jit(solution)/shard_map/ppermute | solution.py:525
  19.1 4.4 %collective-permute-start.1 = (f32[72,128]{1,0:T(8,128)S(1)}, f32[72,128]{1,0:T(8,128)S(1)}, u32[]{:S(2)}, u32[]{:S(2)}) collective-permute-start(f32[72,128]{1,0:T(8,128)S(1)} %get-tuple-element.24), channel_id=1, source_target_pairs={{0,1},{1,0},{2,3},{3,2},{4,5},{5,4},{6,7},{7,6},{8,9},{9,8},{10,11... | collective-permute-start | bytes 110600 | tf_op jit(solution)/shard_map/ppermute | solution.py:454
  20.7 5.2 %collective-permute-start.2 = (f32[72,128]{1,0:T(8,128)S(1)}, f32[72,128]{1,0:T(8,128)S(1)}, u32[]{:S(2)}, u32[]{:S(2)}) collective-permute-start(f32[72,128]{1,0:T(8,128)S(1)} %get-tuple-element.25), channel_id=1, source_target_pairs={{0,2},{1,3},{2,0},{3,1},{4,6},{5,7},{6,4},{7,5},{8,10},{9,11},{10,... | collective-permute-start | bytes 110600 | tf_op jit(solution)/shard_map/ppermute | solution.py:454
  23.2 5.8 %collective-permute-start.3 = (f32[72,128]{1,0:T(8,128)S(1)}, f32[72,128]{1,0:T(8,128)S(1)}, u32[]{:S(2)}, u32[]{:S(2)}) collective-permute-start(f32[72,128]{1,0:T(8,128)S(1)} %get-tuple-element.26), channel_id=1, source_target_pairs={{0,3},{1,2},{2,1},{3,0},{4,7},{5,6},{6,5},{7,4},{8,11},{9,10},{10,... | collective-permute-start | bytes 110600 | tf_op jit(solution)/shard_map/ppermute | solution.py:454
  29.7 1.9 %collective-permute-start.4 = (f32[72,256]{1,0:T(8,128)S(1)}, f32[72,256]{1,0:T(8,128)S(1)}, u32[]{:S(2)}, u32[]{:S(2)}) collective-permute-start(f32[72,256]{1,0:T(8,128)S(1)} %get-tuple-element.29), channel_id=1, source_target_pairs={{0,4},{4,0},{8,12},{12,8},{1,5},{5,1},{9,13},{13,9},{2,6},{6,2},{1... | collective-permute-start | bytes 221192 | tf_op jit(solution)/shard_map/ppermute | solution.py:454
  29.8 4.8 %collective-permute-start.5 = (f32[72,256]{1,0:T(8,128)S(1)}, f32[72,256]{1,0:T(8,128)S(1)}, u32[]{:S(2)}, u32[]{:S(2)}) collective-permute-start(f32[72,256]{1,0:T(8,128)S(1)} %get-tuple-element.30), channel_id=1, source_target_pairs={{0,8},{4,12},{8,0},{12,4},{1,9},{5,13},{9,1},{13,5},{2,10},{6,14},... | collective-permute-start | bytes 221192 | tf_op jit(solution)/shard_map/ppermute | solution.py:454
  31.4 4.5 %collective-permute-start.6 = (f32[72,256]{1,0:T(8,128)S(1)}, f32[72,256]{1,0:T(8,128)S(1)}, u32[]{:S(2)}, u32[]{:S(2)}) collective-permute-start(f32[72,256]{1,0:T(8,128)S(1)} %get-tuple-element.31), channel_id=1, source_target_pairs={{0,12},{4,8},{8,4},{12,0},{1,13},{5,9},{9,5},{13,1},{2,14},{6,10},... | collective-permute-start | bytes 221192 | tf_op jit(solution)/shard_map/ppermute | solution.py:454
  36.2 3.7 %collective-permute-start.7 = (f32[1,8,256]{2,1,0:T(8,128)S(1)}, f32[1,8,256]{2,1,0:T(8,128)S(1)}, u32[]{:S(2)}, u32[]{:S(2)}) collective-permute-start(f32[1,8,256]{2,1,0:T(8,128)S(1)} %get-tuple-element.32.own_small_ref), channel_id=1, source_target_pairs={{0,16},{16,0},{1,17},{17,1},{2,18},{18,2},{3,19},{19,3},{4,20},{20... | collective-permute-start | bytes 24584 | tf_op jit(solution)/shard_map/ppermute | solution.py:547

commit v8 on v7

--- a/solution.py
+++ b/solution.py
@@ -119,9 +119,8 @@
     return jnp.dot(a, b, precision=lax.Precision.HIGHEST, preferred_element_type=F32)
 
 
-def upward_dot(values, table_ref):
-    high, low = parts(values)
-    count, depth = values.shape
+def upward_dot(high, low, table_ref):
+    count, depth = high.shape
     both = dot(jnp.concatenate([high, low], axis=0), table_ref[:depth])
     return both[:count] + both[count:] + dot(high, table_ref[depth:])
 
@@ -234,59 +233,60 @@
             return jnp.concatenate([jnp.where(line == 0, 0.0, turned[:8]), turned[8:]], axis=0)
         return jnp.concatenate([turned[:-8], jnp.where(line == 7, 0.0, turned[-8:])], axis=0)
 
-    def upward_part(g, slot_ref):
-        heat_list = []
+    def bent_plane(g, k):
+        i = g * group + k
+        x = place(i)
+        warm = warmth_ref[x + 1]
+        bent = (warmth_ref[x] - warm) + (warmth_ref[x + 2] - warm)
+        across = (shifted(warm, 1) - warm) + (shifted(warm, -1) - warm)
+        edges_ref[pl.ds(i, 1)] = warm[:1]
+        edges_ref[pl.ds(east + i, 1)] = warm[north - 1 :]
+        return parts((supply_ref[x] + 2.0 * warm) + (factors[0] * bent + factors[1] * across))
+
+    def solve_up(planes, slot_ref):
+        high, low = (jnp.concatenate(half, axis=0) for half in zip(*planes))
+        slot_ref[...] = upward_dot(high, low, up_ref)
+
+    def north_plane(g, k, slot_ref):
+        i = g * group + k
+        first = slot_ref[k * north : (k + 1) * north]
+        both = jnp.where(lane < east, first[:, : 2 * east], first[:, upward - 2 * east :])
+        both = pltpu.roll(both, i, 1)
+        both_ref[0] = jnp.where(lane == i, both, both_ref[0])
+        both_ref[1] = jnp.where(lane == lax.rem(i + 2 * east - 1, 2 * east), both, both_ref[1])
+        solved = north_dot(north_ref, first - 2.0 * warmth_ref[place(i) + 1])
+        north_ends_ref[0, pl.ds(i, 1)] = half_factor * solved[:1]
+        north_ends_ref[1, pl.ds(i, 1)] = half_factor * solved[north - 1 :]
+        swept = solved + tables_ref[pl.ds(sweep + i, 1), :] * east_ends_ref[count - 1]
+        swept_ref[i] = swept
+        east_ends_ref[count - 1] = swept
+        if not pair:
+            east_ends_ref[0] += tables_ref[pl.ds(sweep + east + i, 1), :] * swept
+
+    def step(g, slot_ref, last_ref):
+        arrive(g)
+        planes = []
         for k in range(group):
-            i = g * group + k
-            x = place(i)
-            warm = warmth_ref[x + 1]
-            bent = (warmth_ref[x] - warm) + (warmth_ref[x + 2] - warm)
-            across = (shifted(warm, 1) - warm) + (shifted(warm, -1) - warm)
-            heat_list.append((supply_ref[x] + 2.0 * warm) + (factors[0] * bent + factors[1] * across))
-            edges_ref[pl.ds(i, 1)] = warm[:1]
-            edges_ref[pl.ds(east + i, 1)] = warm[north - 1 :]
-        slot_ref[...] = upward_dot(jnp.concatenate(heat_list, axis=0), up_ref)
-
-    def north_part(g, slot_ref):
-        for k in range(group):
-            i = g * group + k
-            first = slot_ref[k * north : (k + 1) * north]
-            both = jnp.where(lane < east, first[:, : 2 * east], first[:, upward - 2 * east :])
-            both = pltpu.roll(both, i, 1)
-            both_ref[0] = jnp.where(lane == i, both, both_ref[0])
-            both_ref[1] = jnp.where(lane == lax.rem(i + 2 * east - 1, 2 * east), both, both_ref[1])
-            solved = north_dot(north_ref, first - 2.0 * warmth_ref[place(i) + 1])
-            north_ends_ref[0, pl.ds(i, 1)] = half_factor * solved[:1]
-            north_ends_ref[1, pl.ds(i, 1)] = half_factor * solved[north - 1 :]
-            swept = solved + tables_ref[pl.ds(sweep + i, 1), :] * east_ends_ref[count - 1]
-            swept_ref[i] = swept
-            east_ends_ref[count - 1] = swept
-            if not pair:
-                east_ends_ref[0] += tables_ref[pl.ds(sweep + east + i, 1), :] * swept
+            planes.append(bent_plane(g, k))
+            north_plane(g - 1, k, last_ref)
+        solve_up(planes, slot_ref)
 
     arrive(0)
-    upward_part(0, even_ref)
+    solve_up([bent_plane(0, k) for k in range(group)], even_ref)
 
     def body(j, _):
-        g = 2 * j
-        arrive(g + 1)
-        upward_part(g + 1, odd_ref)
-        north_part(g, even_ref)
-        later = jnp.minimum(g + 2, groups - 1)
-
-        @pl.when(g + 2 < groups)
-        def _():
-            arrive(g + 2)
-
-        upward_part(later, even_ref)
-        north_part(g + 1, odd_ref)
+        step(2 * j + 1, odd_ref, even_ref)
+        step(2 * j + 2, even_ref, odd_ref)
         return 0
 
-    lax.fori_loop(0, groups // 2, body, 0)
+    lax.fori_loop(0, groups // 2 - 1, body, 0)
+    step(groups - 1, odd_ref, even_ref)
+    for k in range(group):
+        north_plane(groups - 1, k, odd_ref)
 
     ends = end_places(count, east)
     planes = [warmth_ref[place(i) + 1] for i, _ in ends]
-    solved_up = upward_dot(jnp.concatenate([edges_ref[...]] + planes, axis=0), up_ref)
+    solved_up = upward_dot(*parts(jnp.concatenate([edges_ref[...]] + planes, axis=0)), up_ref)
     east_ends_ref[count - 1] = tables_ref[sweep + 2 * east : sweep + 2 * east + 1, :] * east_ends_ref[count - 1]
     height = north_ends_ref.shape[1]
     rows = [[], []]

time: 45.9 us -> 46.5 us (1.013)
  Pallas kernels: 22.9 us -> 23.4 us
    pallas_call x1, Pallas kernels: 16 us -> 16.5 us  [local(): pl.pallas_call(functools.partial(local_kernel, pair, group, factors, exch...]
where the time goes in v8:
time: 46.5 us; the launch traced here: 46.3 us
  Pallas kernels  23.4 us (50%)
  waiting for transfers between devices  12.8 us (28%)
  starting transfers between devices  9.99 us (21%)
    pallas_call x1, Pallas kernels, local(): pl.pallas_call(functools.partial(local_kernel, pair, group, factors, exch...  16.5 us
    ppermute x6, waiting for transfers between devices, spread_out(): lax.ppermute(messages[d], axis, [(k, peers(k, members, d + 1)[0]) for k i...  9.72 us
    ppermute x6, starting transfers between devices, spread_out(): lax.ppermute(messages[d], axis, [(k, peers(k, members, d + 1)[0]) for k i...  6.32 us
    pallas_call x1, Pallas kernels, local(): pl.pallas_call(functools.partial(final_kernel, pair, table, tile), in_spe...  5.9 us
    ppermute x1, waiting for transfers between devices, local(): other_small = lax.ppermute(own_small, 'gx', [(0, 1), (1, 0)])  3.1 us
    ppermute x1, starting transfers between devices, local(): other = lax.ppermute(own, 'gx', [(0, 1), (1, 0)])  3.06 us
  transfers between devices with their start and end apart: 8, of which 5 were waited for; matrix products, arithmetic and copies ran while one was open for 0% of the time, Pallas kernels for 2%

profile of v8, /device:TPU:0, one launch (start us, length us, event | category | flops | bytes accessed | tf_op | source)
XLA Modules:
  0.0 46.3 jit_solution(13849967268758499552)
XLA Ops:
  0.0 0.0 copy-start.1
  0.0 0.0 copy-start.2
  0.0 0.0 copy-start.3
  0.0 0.0 copy-start.4
  0.0 0.0 copy-start
  0.0 0.0 copy-start.5
  0.0 0.0 copy-start.6
  0.0 16.5 %shard_map.100 = (f32[64,128,256]{2,1,0:T(8,128)S(1)}, f32[66,128,256]{2,1,0:T(8,128)S(1)}, f32[2,72,128]{2,1,0:T(8,128)S(1)}, f32[2,72,256]{2,1,0:T(8,128)S(1)}...) custom-call(f32[904,256]{1,0:T(8,128)} %constant.16.clone.tables_hbm, ...), custom_call_target="tpu_custom_call" | custom-call | tf_op jit(solution)/shard_map/pallas_call | solution.py:497
  16.5 3.1 %collective-permute-start = (f32[1,128,256]{2,1,0:T(8,128)S(1)}, f32[1,128,256]{2,1,0:T(8,128)S(1)}, u32[]{:S(2)}, u32[]{:S(2)}) collective-permute-start(f32[1,128,256]{2,1,0:T(8,128)S(1)} %get-tuple-element.21.own_ref), channel_id=1, source_target_pairs={{0,16},{16,0},{1,17},{17,1},{2,18},{18,2},{3,19},{19,3},{4,20},{20... | collective-permute-start | bytes 393224 | tf_op jit(solution)/shard_map/ppermute | solution.py:525
  19.6 1.6 %collective-permute-start.1 = (f32[72,128]{1,0:T(8,128)S(1)}, f32[72,128]{1,0:T(8,128)S(1)}, u32[]{:S(2)}, u32[]{:S(2)}) collective-permute-start(f32[72,128]{1,0:T(8,128)S(1)} %get-tuple-element.24), channel_id=1, source_target_pairs={{0,1},{1,0},{2,3},{3,2},{4,5},{5,4},{6,7},{7,6},{8,9},{9,8},{10,11... | collective-permute-start | bytes 110600 | tf_op jit(solution)/shard_map/ppermute | solution.py:454
  21.2 2.6 %collective-permute-start.2 = (f32[72,128]{1,0:T(8,128)S(1)}, f32[72,128]{1,0:T(8,128)S(1)}, u32[]{:S(2)}, u32[]{:S(2)}) collective-permute-start(f32[72,128]{1,0:T(8,128)S(1)} %get-tuple-element.25), channel_id=1, source_target_pairs={{0,2},{1,3},{2,0},{3,1},{4,6},{5,7},{6,4},{7,5},{8,10},{9,11},{10,... | collective-permute-start | bytes 110600 | tf_op jit(solution)/shard_map/ppermute | solution.py:454
  23.8 0.2 collective-permute-start.3
  24.0 0.0 collective-permute-done.1.rest_0_
  24.0 2.5 %collective-permute-done.2.rest_1_ = f32[72,128]{1,0:T(8,128)S(1)} collective-permute-done((f32[72,128]{1,0:T(8,128)S(1)}, f32[72,128]{1,0:T(8,128)S(1)}, u32[]{:S(2)}, u32[]{:S(2)}) %collective-permute-start.2) | collective-permute-done | bytes 36896 | tf_op jit(solution)/shard_map/ppermute | solution.py:454
  26.4 3.1 %collective-permute-done.3.rest_2_ = f32[72,128]{1,0:T(8,128)S(1)} collective-permute-done((f32[72,128]{1,0:T(8,128)S(1)}, f32[72,128]{1,0:T(8,128)S(1)}, u32[]{:S(2)}, u32[]{:S(2)}) %collective-permute-start.3) | collective-permute-done | bytes 36896 | tf_op jit(solution)/shard_map/ppermute | solution.py:454
  29.5 0.0 copy-done.1
  29.5 0.0 copy-done.2
  29.5 0.0 copy-done.3
  29.5 0.7 %shard_map.101 = (f32[128,128]{1,0:T(8,128)S(1)}, f32[2,72,256]{2,1,0:T(8,128)S(1)}, f32[1,8,128]{2,1,0:T(8,128)S(1)}, f32[72,256]{1,0:T(8,128)S(1)}, f32[72,256]{1,0:T(8,128)S(1)}, /*index=5*/f32[72,256]{1,0:T(8,128)S(1)}) custom-call(f32[2,72,128]{2,1,0:T(8,128)S(1)} %get-tuple-element.22.ends_ref, f32[2,72,256]{2,1,0:T(8,128)S(1)} %get-tuple-element.23.north_ends_ref, ...), custom_call_target="tpu_custom_call" | custom-call | tf_op jit(solution)/shard_map/pallas_call | solution.py:528
  30.2 0.1 collective-permute-start.4
  30.3 1.6 %collective-permute-start.5 = (f32[72,256]{1,0:T(8,128)S(1)}, f32[72,256]{1,0:T(8,128)S(1)}, u32[]{:S(2)}, u32[]{:S(2)}) collective-permute-start(f32[72,256]{1,0:T(8,128)S(1)} %get-tuple-element.30), channel_id=1, source_target_pairs={{0,8},{4,12},{8,0},{12,4},{1,9},{5,13},{9,1},{13,5},{2,10},{6,14},... | collective-permute-start | bytes 221192 | tf_op jit(solution)/shard_map/ppermute | solution.py:454
  31.9 0.3 collective-permute-start.6
  32.2 0.0 collective-permute-done.4.rest_0_
  32.2 3.0 %collective-permute-done.5.rest_1_ = f32[72,256]{1,0:T(8,128)S(1)} collective-permute-done((f32[72,256]{1,0:T(8,128)S(1)}, f32[72,256]{1,0:T(8,128)S(1)}, u32[]{:S(2)}, u32[]{:S(2)}) %collective-permute-start.5) | collective-permute-done | bytes 73760 | tf_op jit(solution)/shard_map/ppermute | solution.py:454
  35.1 1.2 %collective-permute-done.6.rest_2_ = f32[72,256]{1,0:T(8,128)S(1)} collective-permute-done((f32[72,256]{1,0:T(8,128)S(1)}, f32[72,256]{1,0:T(8,128)S(1)}, u32[]{:S(2)}, u32[]{:S(2)}) %collective-permute-start.6) | collective-permute-done | bytes 73760 | tf_op jit(solution)/shard_map/ppermute | solution.py:454
  36.4 0.0 copy-done.4
  36.4 0.3 shard_map.102
  36.7 0.6 %collective-permute-start.7 = (f32[1,8,256]{2,1,0:T(8,128)S(1)}, f32[1,8,256]{2,1,0:T(8,128)S(1)}, u32[]{:S(2)}, u32[]{:S(2)}) collective-permute-start(f32[1,8,256]{2,1,0:T(8,128)S(1)} %get-tuple-element.32.own_small_ref), channel_id=1, source_target_pairs={{0,16},{16,0},{1,17},{17,1},{2,18},{18,2},{3,19},{19,3},{4,20},{20... | collective-permute-start | bytes 24584 | tf_op jit(solution)/shard_map/ppermute | solution.py:547
  37.3 3.1 %collective-permute-done.7.other_small_ref = f32[1,8,256]{2,1,0:T(8,128)S(1)} collective-permute-done((f32[1,8,256]{2,1,0:T(8,128)S(1)}, f32[1,8,256]{2,1,0:T(8,128)S(1)}, u32[]{:S(2)}, u32[]{:S(2)}) %collective-permute-start.7) | collective-permute-done | bytes 8224 | tf_op jit(solution)/shard_map/ppermute | solution.py:547
  40.4 0.0 collective-permute-done.other_ref
  40.4 0.0 copy-done
  40.4 0.0 copy-done.5
  40.4 0.0 copy-done.6
  40.4 5.9 %shard_map.103 = f32[64,128,256]{2,1,0:T(8,128)} custom-call(f32[3,64]{1,0:T(4,128)S(1)} %copy-done.6, f32[1,128,256]{2,1,0:T(8,128)S(1)} %get-tuple-element.21.own_ref, f32[1,128,256]{2,1,0:T(8,128)S(1)} %collective-permute-done.other_ref, f32[1,8,256]{2,1,0:T(8,128)S(1)} %get-tuple-element.32.own_small_ref, ...), custom_call_target="tpu_custom_call" | custom-call | tf_op jit(solution)/shard_map/pallas_call | solution.py:556
Async XLA Ops:
  0.0 29.5 %copy-start.1 = (f32[128,256]{1,0:T(8,128)S(1)}, f32[128,256]{1,0:T(8,128)}, u32[]{:S(2)}) copy-start(f32[128,256]{1,0:T(8,128)} %constant.19.clone.spread_ref) | copy-start | bytes 393220
  0.0 29.5 %copy-start.2 = (f32[128,128]{1,0:T(8,128)S(1)}, f32[128,128]{1,0:T(8,128)}, u32[]{:S(2)}) copy-start(f32[128,128]{1,0:T(8,128)} %constant.18.clone.east_twice_ref) | copy-start | bytes 196612
  0.0 29.5 %copy-start.3 = (f32[128,128]{1,0:T(8,128)S(1)}, f32[128,128]{1,0:T(8,128)}, u32[]{:S(2)}) copy-start(f32[128,128]{1,0:T(8,128)} %constant.17.clone.north_inverse_ref) | copy-start | bytes 196612
  0.0 36.4 %copy-start.4 = (f32[64,64]{1,0:T(8,128)S(1)}, f32[64,64]{1,0:T(8,128)}, u32[]{:S(2)}) copy-start(f32[64,64]{1,0:T(8,128)} %constant.20.clone.east_inverse_ref) | copy-start | bytes 49156
  0.0 40.4 %copy-start = (f32[2,128,256]{2,1,0:T(8,128)S(1)}, f32[2,128,256]{2,1,0:T(8,128)}, u32[]{:S(2)}) copy-start(f32[2,128,256]{2,1,0:T(8,128)} %constant.23.clone.north_spikes_ref) | copy-start | bytes 786436
  0.0 40.4 %copy-start.5 = (f32[2,256]{1,0:T(2,128)S(1)}, f32[2,256]{1,0:T(2,128)}, u32[]{:S(2)}) copy-start(f32[2,256]{1,0:T(2,128)} %constant.22.clone.upward_spikes_ref) | copy-start | bytes 6148
  0.0 40.4 %copy-start.6 = (f32[3,64]{1,0:T(4,128)S(1)}, f32[3,64]{1,0:T(4,128)}, u32[]{:S(2)}) copy-start(f32[3,64]{1,0:T(4,128)} %constant.21.clone.sweep_ref) | copy-start | bytes 2308
  16.5 23.9 %collective-permute-start = (f32[1,128,256]{2,1,0:T(8,128)S(1)}, f32[1,128,256]{2,1,0:T(8,128)S(1)}, u32[]{:S(2)}, u32[]{:S(2)}) collective-permute-start(f32[1,128,256]{2,1,0:T(8,128)S(1)} %get-tuple-element.21.own_ref), channel_id=1, source_target_pairs={{0,16},{16,0},{1,17},{17,1},{2,18},{18,2},{3,19},{19,3},{4,20},{20... | collective-permute-start | bytes 393224 | tf_op jit(solution)/shard_map/ppermute | solution.py:525
  19.6 4.4 %collective-permute-start.1 = (f32[72,128]{1,0:T(8,128)S(1)}, f32[72,128]{1,0:T(8,128)S(1)}, u32[]{:S(2)}, u32[]{:S(2)}) collective-permute-start(f32[72,128]{1,0:T(8,128)S(1)} %get-tuple-element.24), channel_id=1, source_target_pairs={{0,1},{1,0},{2,3},{3,2},{4,5},{5,4},{6,7},{7,6},{8,9},{9,8},{10,11... | collective-permute-start | bytes 110600 | tf_op jit(solution)/shard_map/ppermute | solution.py:454
  21.2 5.3 %collective-permute-start.2 = (f32[72,128]{1,0:T(8,128)S(1)}, f32[72,128]{1,0:T(8,128)S(1)}, u32[]{:S(2)}, u32[]{:S(2)}) collective-permute-start(f32[72,128]{1,0:T(8,128)S(1)} %get-tuple-element.25), channel_id=1, source_target_pairs={{0,2},{1,3},{2,0},{3,1},{4,6},{5,7},{6,4},{7,5},{8,10},{9,11},{10,... | collective-permute-start | bytes 110600 | tf_op jit(solution)/shard_map/ppermute | solution.py:454
  23.8 5.8 %collective-permute-start.3 = (f32[72,128]{1,0:T(8,128)S(1)}, f32[72,128]{1,0:T(8,128)S(1)}, u32[]{:S(2)}, u32[]{:S(2)}) collective-permute-start(f32[72,128]{1,0:T(8,128)S(1)} %get-tuple-element.26), channel_id=1, source_target_pairs={{0,3},{1,2},{2,1},{3,0},{4,7},{5,6},{6,5},{7,4},{8,11},{9,10},{10,... | collective-permute-start | bytes 110600 | tf_op jit(solution)/shard_map/ppermute | solution.py:454
  30.2 1.9 %collective-permute-start.4 = (f32[72,256]{1,0:T(8,128)S(1)}, f32[72,256]{1,0:T(8,128)S(1)}, u32[]{:S(2)}, u32[]{:S(2)}) collective-permute-start(f32[72,256]{1,0:T(8,128)S(1)} %get-tuple-element.29), channel_id=1, source_target_pairs={{0,4},{4,0},{8,12},{12,8},{1,5},{5,1},{9,13},{13,9},{2,6},{6,2},{1... | collective-permute-start | bytes 221192 | tf_op jit(solution)/shard_map/ppermute | solution.py:454
  30.3 4.8 %collective-permute-start.5 = (f32[72,256]{1,0:T(8,128)S(1)}, f32[72,256]{1,0:T(8,128)S(1)}, u32[]{:S(2)}, u32[]{:S(2)}) collective-permute-start(f32[72,256]{1,0:T(8,128)S(1)} %get-tuple-element.30), channel_id=1, source_target_pairs={{0,8},{4,12},{8,0},{12,4},{1,9},{5,13},{9,1},{13,5},{2,10},{6,14},... | collective-permute-start | bytes 221192 | tf_op jit(solution)/shard_map/ppermute | solution.py:454
  31.9 4.5 %collective-permute-start.6 = (f32[72,256]{1,0:T(8,128)S(1)}, f32[72,256]{1,0:T(8,128)S(1)}, u32[]{:S(2)}, u32[]{:S(2)}) collective-permute-start(f32[72,256]{1,0:T(8,128)S(1)} %get-tuple-element.31), channel_id=1, source_target_pairs={{0,12},{4,8},{8,4},{12,0},{1,13},{5,9},{9,5},{13,1},{2,14},{6,10},... | collective-permute-start | bytes 221192 | tf_op jit(solution)/shard_map/ppermute | solution.py:454
  36.7 3.7 %collective-permute-start.7 = (f32[1,8,256]{2,1,0:T(8,128)S(1)}, f32[1,8,256]{2,1,0:T(8,128)S(1)}, u32[]{:S(2)}, u32[]{:S(2)}) collective-permute-start(f32[1,8,256]{2,1,0:T(8,128)S(1)} %get-tuple-element.32.own_small_ref), channel_id=1, source_target_pairs={{0,16},{16,0},{1,17},{17,1},{2,18},{18,2},{3,19},{19,3},{4,20},{20... | collective-permute-start | bytes 24584 | tf_op jit(solution)/shard_map/ppermute | solution.py:547

commit v9 on v7

--- a/solution.py
+++ b/solution.py
@@ -203,11 +203,15 @@
             return pltpu.make_async_copy(warmth_hbm.at[block], warmth_ref.at[pl.ds(start + 1, group)], sems.at[0, g])
         return pltpu.make_async_copy(supply_hbm.at[block], supply_ref.at[block], sems.at[1, g])
 
+    def begin(g):
+        for which in range(2):
+            fetch(which, g).start()
+
+    ahead = 3
     tables = pltpu.make_async_copy(tables_hbm, tables_ref, sems.at[0, groups])
     tables.start()
-    for g in range(groups):
-        for which in range(2):
-            fetch(which, g).start()
+    for g in range(min(ahead, groups)):
+        begin(g)
     warmth_ref[0] = jnp.zeros((north, upward), F32)
     warmth_ref[east + 1] = jnp.zeros((north, upward), F32)
     both_ref[...] = jnp.zeros_like(both_ref)
@@ -227,6 +231,10 @@
         @pl.when(g + 1 < groups)
         def _():
             fetch(0, g + 1).wait()
+
+        @pl.when(g + ahead < groups)
+        def _():
+            begin(g + ahead)
 
     def shifted(values, step):
         turned = pltpu.roll(values, step % north, 0)

time: 45.9 us -> 45.9 us (level)
  no operation moved by 1% of the time
where the time goes in v9:
time: 45.9 us; the launch traced here: 45.7 us
  Pallas kernels  22.8 us (50%)
  waiting for transfers between devices  12.9 us (28%)
  starting transfers between devices  9.95 us (22%)
    pallas_call x1, Pallas kernels, local(): pl.pallas_call(functools.partial(local_kernel, pair, group, factors, exch...  15.9 us
    ppermute x6, waiting for transfers between devices, spread_out(): lax.ppermute(messages[d], axis, [(k, peers(k, members, d + 1)[0]) for k i...  9.74 us
    ppermute x6, starting transfers between devices, spread_out(): lax.ppermute(messages[d], axis, [(k, peers(k, members, d + 1)[0]) for k i...  6.32 us
    pallas_call x1, Pallas kernels, local(): pl.pallas_call(functools.partial(final_kernel, pair, table, tile), in_spe...  5.9 us
    ppermute x1, waiting for transfers between devices, local(): other_small = lax.ppermute(own_small, 'gx', [(0, 1), (1, 0)])  3.14 us
    ppermute x1, starting transfers between devices, local(): other = lax.ppermute(own, 'gx', [(0, 1), (1, 0)])  3.06 us
  transfers between devices with their start and end apart: 8, of which 5 were waited for; matrix products, arithmetic and copies ran while one was open for 0% of the time, Pallas kernels for 2%

profile of v9, /device:TPU:0, one launch (start us, length us, event | category | flops | bytes accessed | tf_op | source)
XLA Modules:
  0.0 45.7 jit_solution(10679214555298896865)
XLA Ops:
  0.0 0.0 copy-start.1
  0.0 0.0 copy-start.2
  0.0 0.0 copy-start.3
  0.0 0.0 copy-start.4
  0.0 0.0 copy-start
  0.0 0.0 copy-start.5
  0.0 0.0 copy-start.6
  0.0 15.9 %shard_map.100 = (f32[64,128,256]{2,1,0:T(8,128)S(1)}, f32[66,128,256]{2,1,0:T(8,128)S(1)}, f32[2,72,128]{2,1,0:T(8,128)S(1)}, f32[2,72,256]{2,1,0:T(8,128)S(1)}...) custom-call(f32[904,256]{1,0:T(8,128)} %constant.16.clone.tables_hbm, ...), custom_call_target="tpu_custom_call" | custom-call | tf_op jit(solution)/shard_map/pallas_call | solution.py:505
  15.9 3.1 %collective-permute-start = (f32[1,128,256]{2,1,0:T(8,128)S(1)}, f32[1,128,256]{2,1,0:T(8,128)S(1)}, u32[]{:S(2)}, u32[]{:S(2)}) collective-permute-start(f32[1,128,256]{2,1,0:T(8,128)S(1)} %get-tuple-element.21.own_ref), channel_id=1, source_target_pairs={{0,16},{16,0},{1,17},{17,1},{2,18},{18,2},{3,19},{19,3},{4,20},{20... | collective-permute-start | bytes 393224 | tf_op jit(solution)/shard_map/ppermute | solution.py:533
  19.0 1.6 %collective-permute-start.1 = (f32[72,128]{1,0:T(8,128)S(1)}, f32[72,128]{1,0:T(8,128)S(1)}, u32[]{:S(2)}, u32[]{:S(2)}) collective-permute-start(f32[72,128]{1,0:T(8,128)S(1)} %get-tuple-element.24), channel_id=1, source_target_pairs={{0,1},{1,0},{2,3},{3,2},{4,5},{5,4},{6,7},{7,6},{8,9},{9,8},{10,11... | collective-permute-start | bytes 110600 | tf_op jit(solution)/shard_map/ppermute | solution.py:462
  20.6 2.6 %collective-permute-start.2 = (f32[72,128]{1,0:T(8,128)S(1)}, f32[72,128]{1,0:T(8,128)S(1)}, u32[]{:S(2)}, u32[]{:S(2)}) collective-permute-start(f32[72,128]{1,0:T(8,128)S(1)} %get-tuple-element.25), channel_id=1, source_target_pairs={{0,2},{1,3},{2,0},{3,1},{4,6},{5,7},{6,4},{7,5},{8,10},{9,11},{10,... | collective-permute-start | bytes 110600 | tf_op jit(solution)/shard_map/ppermute | solution.py:462
  23.2 0.2 collective-permute-start.3
  23.4 0.0 collective-permute-done.1.rest_0_
  23.4 2.4 %collective-permute-done.2.rest_1_ = f32[72,128]{1,0:T(8,128)S(1)} collective-permute-done((f32[72,128]{1,0:T(8,128)S(1)}, f32[72,128]{1,0:T(8,128)S(1)}, u32[]{:S(2)}, u32[]{:S(2)}) %collective-permute-start.2) | collective-permute-done | bytes 36896 | tf_op jit(solution)/shard_map/ppermute | solution.py:462
  25.8 3.1 %collective-permute-done.3.rest_2_ = f32[72,128]{1,0:T(8,128)S(1)} collective-permute-done((f32[72,128]{1,0:T(8,128)S(1)}, f32[72,128]{1,0:T(8,128)S(1)}, u32[]{:S(2)}, u32[]{:S(2)}) %collective-permute-start.3) | collective-permute-done | bytes 36896 | tf_op jit(solution)/shard_map/ppermute | solution.py:462
  28.9 0.0 copy-done.1
  28.9 0.0 copy-done.2
  28.9 0.0 copy-done.3
  28.9 0.7 %shard_map.101 = (f32[128,128]{1,0:T(8,128)S(1)}, f32[2,72,256]{2,1,0:T(8,128)S(1)}, f32[1,8,128]{2,1,0:T(8,128)S(1)}, f32[72,256]{1,0:T(8,128)S(1)}, f32[72,256]{1,0:T(8,128)S(1)}, /*index=5*/f32[72,256]{1,0:T(8,128)S(1)}) custom-call(f32[2,72,128]{2,1,0:T(8,128)S(1)} %get-tuple-element.22.ends_ref, f32[2,72,256]{2,1,0:T(8,128)S(1)} %get-tuple-element.23.north_ends_ref, ...), custom_call_target="tpu_custom_call" | custom-call | tf_op jit(solution)/shard_map/pallas_call | solution.py:536
  29.6 0.1 collective-permute-start.4
  29.7 1.6 %collective-permute-start.5 = (f32[72,256]{1,0:T(8,128)S(1)}, f32[72,256]{1,0:T(8,128)S(1)}, u32[]{:S(2)}, u32[]{:S(2)}) collective-permute-start(f32[72,256]{1,0:T(8,128)S(1)} %get-tuple-element.30), channel_id=1, source_target_pairs={{0,8},{4,12},{8,0},{12,4},{1,9},{5,13},{9,1},{13,5},{2,10},{6,14},... | collective-permute-start | bytes 221192 | tf_op jit(solution)/shard_map/ppermute | solution.py:462
  31.3 0.3 collective-permute-start.6
  31.6 0.0 collective-permute-done.4.rest_0_
  31.6 3.0 %collective-permute-done.5.rest_1_ = f32[72,256]{1,0:T(8,128)S(1)} collective-permute-done((f32[72,256]{1,0:T(8,128)S(1)}, f32[72,256]{1,0:T(8,128)S(1)}, u32[]{:S(2)}, u32[]{:S(2)}) %collective-permute-start.5) | collective-permute-done | bytes 73760 | tf_op jit(solution)/shard_map/ppermute | solution.py:462
  34.5 1.2 %collective-permute-done.6.rest_2_ = f32[72,256]{1,0:T(8,128)S(1)} collective-permute-done((f32[72,256]{1,0:T(8,128)S(1)}, f32[72,256]{1,0:T(8,128)S(1)}, u32[]{:S(2)}, u32[]{:S(2)}) %collective-permute-start.6) | collective-permute-done | bytes 73760 | tf_op jit(solution)/shard_map/ppermute | solution.py:462
  35.8 0.0 copy-done.4
  35.8 0.3 shard_map.102
  36.1 0.6 %collective-permute-start.7 = (f32[1,8,256]{2,1,0:T(8,128)S(1)}, f32[1,8,256]{2,1,0:T(8,128)S(1)}, u32[]{:S(2)}, u32[]{:S(2)}) collective-permute-start(f32[1,8,256]{2,1,0:T(8,128)S(1)} %get-tuple-element.32.own_small_ref), channel_id=1, source_target_pairs={{0,16},{16,0},{1,17},{17,1},{2,18},{18,2},{3,19},{19,3},{4,20},{20... | collective-permute-start | bytes 24584 | tf_op jit(solution)/shard_map/ppermute | solution.py:555
  36.7 3.1 %collective-permute-done.7.other_small_ref = f32[1,8,256]{2,1,0:T(8,128)S(1)} collective-permute-done((f32[1,8,256]{2,1,0:T(8,128)S(1)}, f32[1,8,256]{2,1,0:T(8,128)S(1)}, u32[]{:S(2)}, u32[]{:S(2)}) %collective-permute-start.7) | collective-permute-done | bytes 8224 | tf_op jit(solution)/shard_map/ppermute | solution.py:555
  39.8 0.0 collective-permute-done.other_ref
  39.8 0.0 copy-done
  39.8 0.0 copy-done.5
  39.8 0.0 copy-done.6
  39.8 5.9 %shard_map.103 = f32[64,128,256]{2,1,0:T(8,128)} custom-call(f32[3,64]{1,0:T(4,128)S(1)} %copy-done.6, f32[1,128,256]{2,1,0:T(8,128)S(1)} %get-tuple-element.21.own_ref, f32[1,128,256]{2,1,0:T(8,128)S(1)} %collective-permute-done.other_ref, f32[1,8,256]{2,1,0:T(8,128)S(1)} %get-tuple-element.32.own_small_ref, ...), custom_call_target="tpu_custom_call" | custom-call | tf_op jit(solution)/shard_map/pallas_call | solution.py:564
Async XLA Ops:
  0.0 28.9 %copy-start.1 = (f32[128,256]{1,0:T(8,128)S(1)}, f32[128,256]{1,0:T(8,128)}, u32[]{:S(2)}) copy-start(f32[128,256]{1,0:T(8,128)} %constant.19.clone.spread_ref) | copy-start | bytes 393220
  0.0 28.9 %copy-start.2 = (f32[128,128]{1,0:T(8,128)S(1)}, f32[128,128]{1,0:T(8,128)}, u32[]{:S(2)}) copy-start(f32[128,128]{1,0:T(8,128)} %constant.18.clone.east_twice_ref) | copy-start | bytes 196612
  0.0 28.9 %copy-start.3 = (f32[128,128]{1,0:T(8,128)S(1)}, f32[128,128]{1,0:T(8,128)}, u32[]{:S(2)}) copy-start(f32[128,128]{1,0:T(8,128)} %constant.17.clone.north_inverse_ref) | copy-start | bytes 196612
  0.0 35.8 %copy-start.4 = (f32[64,64]{1,0:T(8,128)S(1)}, f32[64,64]{1,0:T(8,128)}, u32[]{:S(2)}) copy-start(f32[64,64]{1,0:T(8,128)} %constant.20.clone.east_inverse_ref) | copy-start | bytes 49156
  0.0 39.8 %copy-start = (f32[2,128,256]{2,1,0:T(8,128)S(1)}, f32[2,128,256]{2,1,0:T(8,128)}, u32[]{:S(2)}) copy-start(f32[2,128,256]{2,1,0:T(8,128)} %constant.23.clone.north_spikes_ref) | copy-start | bytes 786436
  0.0 39.8 %copy-start.5 = (f32[2,256]{1,0:T(2,128)S(1)}, f32[2,256]{1,0:T(2,128)}, u32[]{:S(2)}) copy-start(f32[2,256]{1,0:T(2,128)} %constant.22.clone.upward_spikes_ref) | copy-start | bytes 6148
  0.0 39.8 %copy-start.6 = (f32[3,64]{1,0:T(4,128)S(1)}, f32[3,64]{1,0:T(4,128)}, u32[]{:S(2)}) copy-start(f32[3,64]{1,0:T(4,128)} %constant.21.clone.sweep_ref) | copy-start | bytes 2308
  15.9 23.9 %collective-permute-start = (f32[1,128,256]{2,1,0:T(8,128)S(1)}, f32[1,128,256]{2,1,0:T(8,128)S(1)}, u32[]{:S(2)}, u32[]{:S(2)}) collective-permute-start(f32[1,128,256]{2,1,0:T(8,128)S(1)} %get-tuple-element.21.own_ref), channel_id=1, source_target_pairs={{0,16},{16,0},{1,17},{17,1},{2,18},{18,2},{3,19},{19,3},{4,20},{20... | collective-permute-start | bytes 393224 | tf_op jit(solution)/shard_map/ppermute | solution.py:533
  19.0 4.4 %collective-permute-start.1 = (f32[72,128]{1,0:T(8,128)S(1)}, f32[72,128]{1,0:T(8,128)S(1)}, u32[]{:S(2)}, u32[]{:S(2)}) collective-permute-start(f32[72,128]{1,0:T(8,128)S(1)} %get-tuple-element.24), channel_id=1, source_target_pairs={{0,1},{1,0},{2,3},{3,2},{4,5},{5,4},{6,7},{7,6},{8,9},{9,8},{10,11... | collective-permute-start | bytes 110600 | tf_op jit(solution)/shard_map/ppermute | solution.py:462
  20.6 5.3 %collective-permute-start.2 = (f32[72,128]{1,0:T(8,128)S(1)}, f32[72,128]{1,0:T(8,128)S(1)}, u32[]{:S(2)}, u32[]{:S(2)}) collective-permute-start(f32[72,128]{1,0:T(8,128)S(1)} %get-tuple-element.25), channel_id=1, source_target_pairs={{0,2},{1,3},{2,0},{3,1},{4,6},{5,7},{6,4},{7,5},{8,10},{9,11},{10,... | collective-permute-start | bytes 110600 | tf_op jit(solution)/shard_map/ppermute | solution.py:462
  23.2 5.8 %collective-permute-start.3 = (f32[72,128]{1,0:T(8,128)S(1)}, f32[72,128]{1,0:T(8,128)S(1)}, u32[]{:S(2)}, u32[]{:S(2)}) collective-permute-start(f32[72,128]{1,0:T(8,128)S(1)} %get-tuple-element.26), channel_id=1, source_target_pairs={{0,3},{1,2},{2,1},{3,0},{4,7},{5,6},{6,5},{7,4},{8,11},{9,10},{10,... | collective-permute-start | bytes 110600 | tf_op jit(solution)/shard_map/ppermute | solution.py:462
  29.6 1.9 %collective-permute-start.4 = (f32[72,256]{1,0:T(8,128)S(1)}, f32[72,256]{1,0:T(8,128)S(1)}, u32[]{:S(2)}, u32[]{:S(2)}) collective-permute-start(f32[72,256]{1,0:T(8,128)S(1)} %get-tuple-element.29), channel_id=1, source_target_pairs={{0,4},{4,0},{8,12},{12,8},{1,5},{5,1},{9,13},{13,9},{2,6},{6,2},{1... | collective-permute-start | bytes 221192 | tf_op jit(solution)/shard_map/ppermute | solution.py:462
  29.7 4.8 %collective-permute-start.5 = (f32[72,256]{1,0:T(8,128)S(1)}, f32[72,256]{1,0:T(8,128)S(1)}, u32[]{:S(2)}, u32[]{:S(2)}) collective-permute-start(f32[72,256]{1,0:T(8,128)S(1)} %get-tuple-element.30), channel_id=1, source_target_pairs={{0,8},{4,12},{8,0},{12,4},{1,9},{5,13},{9,1},{13,5},{2,10},{6,14},... | collective-permute-start | bytes 221192 | tf_op jit(solution)/shard_map/ppermute | solution.py:462
  31.3 4.5 %collective-permute-start.6 = (f32[72,256]{1,0:T(8,128)S(1)}, f32[72,256]{1,0:T(8,128)S(1)}, u32[]{:S(2)}, u32[]{:S(2)}) collective-permute-start(f32[72,256]{1,0:T(8,128)S(1)} %get-tuple-element.31), channel_id=1, source_target_pairs={{0,12},{4,8},{8,4},{12,0},{1,13},{5,9},{9,5},{13,1},{2,14},{6,10},... | collective-permute-start | bytes 221192 | tf_op jit(solution)/shard_map/ppermute | solution.py:462
  36.1 3.7 %collective-permute-start.7 = (f32[1,8,256]{2,1,0:T(8,128)S(1)}, f32[1,8,256]{2,1,0:T(8,128)S(1)}, u32[]{:S(2)}, u32[]{:S(2)}) collective-permute-start(f32[1,8,256]{2,1,0:T(8,128)S(1)} %get-tuple-element.32.own_small_ref), channel_id=1, source_target_pairs={{0,16},{16,0},{1,17},{17,1},{2,18},{18,2},{3,19},{19,3},{4,20},{20... | collective-permute-start | bytes 24584 | tf_op jit(solution)/shard_map/ppermute | solution.py:555

commit v10 on v9

--- a/solution.py
+++ b/solution.py
@@ -207,7 +207,7 @@
         for which in range(2):
             fetch(which, g).start()
 
-    ahead = 3
+    ahead = 2
     tables = pltpu.make_async_copy(tables_hbm, tables_ref, sems.at[0, groups])
     tables.start()
     for g in range(min(ahead, groups)):
@@ -280,17 +280,16 @@
         arrive(g + 1)
         upward_part(g + 1, odd_ref)
         north_part(g, even_ref)
-        later = jnp.minimum(g + 2, groups - 1)
-
-        @pl.when(g + 2 < groups)
-        def _():
-            arrive(g + 2)
-
-        upward_part(later, even_ref)
+        arrive(g + 2)
+        upward_part(g + 2, even_ref)
         north_part(g + 1, odd_ref)
         return 0
 
-    lax.fori_loop(0, groups // 2, body, 0)
+    lax.fori_loop(0, groups // 2 - 1, body, 0)
+    arrive(groups - 1)
+    upward_part(groups - 1, odd_ref)
+    north_part(groups - 2, even_ref)
+    north_part(groups - 1, odd_ref)
 
     ends = end_places(count, east)
     planes = [warmth_ref[place(i) + 1] for i, _ in ends]
@@ -500,7 +499,7 @@
     def kept(*sizes):
         return jax.ShapeDtypeStruct(sizes, F32)
 
-    group = 4
+    group = 8
     folded = kept(north // 2 + 8, 2 * east)
     swept, warmth, upward_ends, north_ends, own, *messages = pl.pallas_call(
         functools.partial(local_kernel, pair, group, factors, exchanges[2][0]),

time: 45.9 us -> 44.5 us (0.969)
  Pallas kernels: 22.8 us -> 21.4 us
    pallas_call x1, Pallas kernels: 15.9 us -> 14.5 us  [local(): pl.pallas_call(functools.partial(local_kernel, pair, group, factors, exch...]
where the time goes in v10:
time: 44.5 us; the launch traced here: 44.4 us
  Pallas kernels  21.4 us (48%)
  waiting for transfers between devices  12.9 us (29%)
  starting transfers between devices  9.96 us (22%)
    pallas_call x1, Pallas kernels, local(): pl.pallas_call(functools.partial(local_kernel, pair, group, factors, exch...  14.5 us
    ppermute x6, waiting for transfers between devices, spread_out(): lax.ppermute(messages[d], axis, [(k, peers(k, members, d + 1)[0]) for k i...  9.73 us
    ppermute x6, starting transfers between devices, spread_out(): lax.ppermute(messages[d], axis, [(k, peers(k, members, d + 1)[0]) for k i...  6.32 us
    pallas_call x1, Pallas kernels, local(): pl.pallas_call(functools.partial(final_kernel, pair, table, tile), in_spe...  5.9 us
    ppermute x1, waiting for transfers between devices, local(): other_small = lax.ppermute(own_small, 'gx', [(0, 1), (1, 0)])  3.14 us
    ppermute x1, starting transfers between devices, local(): other = lax.ppermute(own, 'gx', [(0, 1), (1, 0)])  3.07 us
  transfers between devices with their start and end apart: 8, of which 5 were waited for; matrix products, arithmetic and copies ran while one was open for 0% of the time, Pallas kernels for 2%

profile of v10, /device:TPU:0, one launch (start us, length us, event | category | flops | bytes accessed | tf_op | source)
XLA Modules:
  0.0 44.4 jit_solution(784966712127432671)
XLA Ops:
  0.0 0.0 copy-start.1
  0.0 0.0 copy-start.2
  0.0 0.0 copy-start.3
  0.0 0.0 copy-start.4
  0.0 0.0 copy-start
  0.0 0.0 copy-start.5
  0.0 0.0 copy-start.6
  0.0 14.5 %shard_map.100 = (f32[64,128,256]{2,1,0:T(8,128)S(1)}, f32[66,128,256]{2,1,0:T(8,128)S(1)}, f32[2,72,128]{2,1,0:T(8,128)S(1)}, f32[2,72,256]{2,1,0:T(8,128)S(1)}...) custom-call(f32[904,256]{1,0:T(8,128)} %constant.16.clone.tables_hbm, ...), custom_call_target="tpu_custom_call" | custom-call | tf_op jit(solution)/shard_map/pallas_call | solution.py:504
  14.6 3.1 %collective-permute-start = (f32[1,128,256]{2,1,0:T(8,128)S(1)}, f32[1,128,256]{2,1,0:T(8,128)S(1)}, u32[]{:S(2)}, u32[]{:S(2)}) collective-permute-start(f32[1,128,256]{2,1,0:T(8,128)S(1)} %get-tuple-element.21.own_ref), channel_id=1, source_target_pairs={{0,16},{16,0},{1,17},{17,1},{2,18},{18,2},{3,19},{19,3},{4,20},{20... | collective-permute-start | bytes 393224 | tf_op jit(solution)/shard_map/ppermute | solution.py:532
  17.6 1.6 %collective-permute-start.1 = (f32[72,128]{1,0:T(8,128)S(1)}, f32[72,128]{1,0:T(8,128)S(1)}, u32[]{:S(2)}, u32[]{:S(2)}) collective-permute-start(f32[72,128]{1,0:T(8,128)S(1)} %get-tuple-element.24), channel_id=1, source_target_pairs={{0,1},{1,0},{2,3},{3,2},{4,5},{5,4},{6,7},{7,6},{8,9},{9,8},{10,11... | collective-permute-start | bytes 110600 | tf_op jit(solution)/shard_map/ppermute | solution.py:461
  19.2 2.6 %collective-permute-start.2 = (f32[72,128]{1,0:T(8,128)S(1)}, f32[72,128]{1,0:T(8,128)S(1)}, u32[]{:S(2)}, u32[]{:S(2)}) collective-permute-start(f32[72,128]{1,0:T(8,128)S(1)} %get-tuple-element.25), channel_id=1, source_target_pairs={{0,2},{1,3},{2,0},{3,1},{4,6},{5,7},{6,4},{7,5},{8,10},{9,11},{10,... | collective-permute-start | bytes 110600 | tf_op jit(solution)/shard_map/ppermute | solution.py:461
  21.8 0.2 collective-permute-start.3
  22.0 0.0 collective-permute-done.1.rest_0_
  22.0 2.4 %collective-permute-done.2.rest_1_ = f32[72,128]{1,0:T(8,128)S(1)} collective-permute-done((f32[72,128]{1,0:T(8,128)S(1)}, f32[72,128]{1,0:T(8,128)S(1)}, u32[]{:S(2)}, u32[]{:S(2)}) %collective-permute-start.2) | collective-permute-done | bytes 36896 | tf_op jit(solution)/shard_map/ppermute | solution.py:461
  24.5 3.1 %collective-permute-done.3.rest_2_ = f32[72,128]{1,0:T(8,128)S(1)} collective-permute-done((f32[72,128]{1,0:T(8,128)S(1)}, f32[72,128]{1,0:T(8,128)S(1)}, u32[]{:S(2)}, u32[]{:S(2)}) %collective-permute-start.3) | collective-permute-done | bytes 36896 | tf_op jit(solution)/shard_map/ppermute | solution.py:461
  27.6 0.0 copy-done.1
  27.6 0.0 copy-done.2
  27.6 0.0 copy-done.3
  27.6 0.7 %shard_map.101 = (f32[128,128]{1,0:T(8,128)S(1)}, f32[2,72,256]{2,1,0:T(8,128)S(1)}, f32[1,8,128]{2,1,0:T(8,128)S(1)}, f32[72,256]{1,0:T(8,128)S(1)}, f32[72,256]{1,0:T(8,128)S(1)}, /*index=5*/f32[72,256]{1,0:T(8,128)S(1)}) custom-call(f32[2,72,128]{2,1,0:T(8,128)S(1)} %get-tuple-element.22.ends_ref, f32[2,72,256]{2,1,0:T(8,128)S(1)} %get-tuple-element.23.north_ends_ref, ...), custom_call_target="tpu_custom_call" | custom-call | tf_op jit(solution)/shard_map/pallas_call | solution.py:535
  28.3 0.1 collective-permute-start.4
  28.3 1.6 %collective-permute-start.5 = (f32[72,256]{1,0:T(8,128)S(1)}, f32[72,256]{1,0:T(8,128)S(1)}, u32[]{:S(2)}, u32[]{:S(2)}) collective-permute-start(f32[72,256]{1,0:T(8,128)S(1)} %get-tuple-element.30), channel_id=1, source_target_pairs={{0,8},{4,12},{8,0},{12,4},{1,9},{5,13},{9,1},{13,5},{2,10},{6,14},... | collective-permute-start | bytes 221192 | tf_op jit(solution)/shard_map/ppermute | solution.py:461
  29.9 0.3 collective-permute-start.6
  30.2 0.0 collective-permute-done.4.rest_0_
  30.2 3.0 %collective-permute-done.5.rest_1_ = f32[72,256]{1,0:T(8,128)S(1)} collective-permute-done((f32[72,256]{1,0:T(8,128)S(1)}, f32[72,256]{1,0:T(8,128)S(1)}, u32[]{:S(2)}, u32[]{:S(2)}) %collective-permute-start.5) | collective-permute-done | bytes 73760 | tf_op jit(solution)/shard_map/ppermute | solution.py:461
  33.2 1.2 %collective-permute-done.6.rest_2_ = f32[72,256]{1,0:T(8,128)S(1)} collective-permute-done((f32[72,256]{1,0:T(8,128)S(1)}, f32[72,256]{1,0:T(8,128)S(1)}, u32[]{:S(2)}, u32[]{:S(2)}) %collective-permute-start.6) | collective-permute-done | bytes 73760 | tf_op jit(solution)/shard_map/ppermute | solution.py:461
  34.4 0.0 copy-done.4
  34.4 0.3 shard_map.102
  34.7 0.6 %collective-permute-start.7 = (f32[1,8,256]{2,1,0:T(8,128)S(1)}, f32[1,8,256]{2,1,0:T(8,128)S(1)}, u32[]{:S(2)}, u32[]{:S(2)}) collective-permute-start(f32[1,8,256]{2,1,0:T(8,128)S(1)} %get-tuple-element.32.own_small_ref), channel_id=1, source_target_pairs={{0,16},{16,0},{1,17},{17,1},{2,18},{18,2},{3,19},{19,3},{4,20},{20... | collective-permute-start | bytes 24584 | tf_op jit(solution)/shard_map/ppermute | solution.py:554
  35.3 3.1 %collective-permute-done.7.other_small_ref = f32[1,8,256]{2,1,0:T(8,128)S(1)} collective-permute-done((f32[1,8,256]{2,1,0:T(8,128)S(1)}, f32[1,8,256]{2,1,0:T(8,128)S(1)}, u32[]{:S(2)}, u32[]{:S(2)}) %collective-permute-start.7) | collective-permute-done | bytes 8224 | tf_op jit(solution)/shard_map/ppermute | solution.py:554
  38.4 0.0 collective-permute-done.other_ref
  38.4 0.0 copy-done
  38.5 0.0 copy-done.5
  38.5 0.0 copy-done.6
  38.5 5.9 %shard_map.103 = f32[64,128,256]{2,1,0:T(8,128)} custom-call(f32[3,64]{1,0:T(4,128)S(1)} %copy-done.6, f32[1,128,256]{2,1,0:T(8,128)S(1)} %get-tuple-element.21.own_ref, f32[1,128,256]{2,1,0:T(8,128)S(1)} %collective-permute-done.other_ref, f32[1,8,256]{2,1,0:T(8,128)S(1)} %get-tuple-element.32.own_small_ref, ...), custom_call_target="tpu_custom_call" | custom-call | tf_op jit(solution)/shard_map/pallas_call | solution.py:563
Async XLA Ops:
  0.0 27.6 %copy-start.1 = (f32[128,256]{1,0:T(8,128)S(1)}, f32[128,256]{1,0:T(8,128)}, u32[]{:S(2)}) copy-start(f32[128,256]{1,0:T(8,128)} %constant.19.clone.spread_ref) | copy-start | bytes 393220
  0.0 27.6 %copy-start.2 = (f32[128,128]{1,0:T(8,128)S(1)}, f32[128,128]{1,0:T(8,128)}, u32[]{:S(2)}) copy-start(f32[128,128]{1,0:T(8,128)} %constant.18.clone.east_twice_ref) | copy-start | bytes 196612
  0.0 27.6 %copy-start.3 = (f32[128,128]{1,0:T(8,128)S(1)}, f32[128,128]{1,0:T(8,128)}, u32[]{:S(2)}) copy-start(f32[128,128]{1,0:T(8,128)} %constant.17.clone.north_inverse_ref) | copy-start | bytes 196612
  0.0 34.4 %copy-start.4 = (f32[64,64]{1,0:T(8,128)S(1)}, f32[64,64]{1,0:T(8,128)}, u32[]{:S(2)}) copy-start(f32[64,64]{1,0:T(8,128)} %constant.20.clone.east_inverse_ref) | copy-start | bytes 49156
  0.0 38.4 %copy-start = (f32[2,128,256]{2,1,0:T(8,128)S(1)}, f32[2,128,256]{2,1,0:T(8,128)}, u32[]{:S(2)}) copy-start(f32[2,128,256]{2,1,0:T(8,128)} %constant.23.clone.north_spikes_ref) | copy-start | bytes 786436
  0.0 38.4 %copy-start.5 = (f32[2,256]{1,0:T(2,128)S(1)}, f32[2,256]{1,0:T(2,128)}, u32[]{:S(2)}) copy-start(f32[2,256]{1,0:T(2,128)} %constant.22.clone.upward_spikes_ref) | copy-start | bytes 6148
  0.0 38.4 %copy-start.6 = (f32[3,64]{1,0:T(4,128)S(1)}, f32[3,64]{1,0:T(4,128)}, u32[]{:S(2)}) copy-start(f32[3,64]{1,0:T(4,128)} %constant.21.clone.sweep_ref) | copy-start | bytes 2308
  14.6 23.9 %collective-permute-start = (f32[1,128,256]{2,1,0:T(8,128)S(1)}, f32[1,128,256]{2,1,0:T(8,128)S(1)}, u32[]{:S(2)}, u32[]{:S(2)}) collective-permute-start(f32[1,128,256]{2,1,0:T(8,128)S(1)} %get-tuple-element.21.own_ref), channel_id=1, source_target_pairs={{0,16},{16,0},{1,17},{17,1},{2,18},{18,2},{3,19},{19,3},{4,20},{20... | collective-permute-start | bytes 393224 | tf_op jit(solution)/shard_map/ppermute | solution.py:532
  17.6 4.4 %collective-permute-start.1 = (f32[72,128]{1,0:T(8,128)S(1)}, f32[72,128]{1,0:T(8,128)S(1)}, u32[]{:S(2)}, u32[]{:S(2)}) collective-permute-start(f32[72,128]{1,0:T(8,128)S(1)} %get-tuple-element.24), channel_id=1, source_target_pairs={{0,1},{1,0},{2,3},{3,2},{4,5},{5,4},{6,7},{7,6},{8,9},{9,8},{10,11... | collective-permute-start | bytes 110600 | tf_op jit(solution)/shard_map/ppermute | solution.py:461
  19.2 5.3 %collective-permute-start.2 = (f32[72,128]{1,0:T(8,128)S(1)}, f32[72,128]{1,0:T(8,128)S(1)}, u32[]{:S(2)}, u32[]{:S(2)}) collective-permute-start(f32[72,128]{1,0:T(8,128)S(1)} %get-tuple-element.25), channel_id=1, source_target_pairs={{0,2},{1,3},{2,0},{3,1},{4,6},{5,7},{6,4},{7,5},{8,10},{9,11},{10,... | collective-permute-start | bytes 110600 | tf_op jit(solution)/shard_map/ppermute | solution.py:461
  21.8 5.8 %collective-permute-start.3 = (f32[72,128]{1,0:T(8,128)S(1)}, f32[72,128]{1,0:T(8,128)S(1)}, u32[]{:S(2)}, u32[]{:S(2)}) collective-permute-start(f32[72,128]{1,0:T(8,128)S(1)} %get-tuple-element.26), channel_id=1, source_target_pairs={{0,3},{1,2},{2,1},{3,0},{4,7},{5,6},{6,5},{7,4},{8,11},{9,10},{10,... | collective-permute-start | bytes 110600 | tf_op jit(solution)/shard_map/ppermute | solution.py:461
  28.3 1.9 %collective-permute-start.4 = (f32[72,256]{1,0:T(8,128)S(1)}, f32[72,256]{1,0:T(8,128)S(1)}, u32[]{:S(2)}, u32[]{:S(2)}) collective-permute-start(f32[72,256]{1,0:T(8,128)S(1)} %get-tuple-element.29), channel_id=1, source_target_pairs={{0,4},{4,0},{8,12},{12,8},{1,5},{5,1},{9,13},{13,9},{2,6},{6,2},{1... | collective-permute-start | bytes 221192 | tf_op jit(solution)/shard_map/ppermute | solution.py:461
  28.3 4.8 %collective-permute-start.5 = (f32[72,256]{1,0:T(8,128)S(1)}, f32[72,256]{1,0:T(8,128)S(1)}, u32[]{:S(2)}, u32[]{:S(2)}) collective-permute-start(f32[72,256]{1,0:T(8,128)S(1)} %get-tuple-element.30), channel_id=1, source_target_pairs={{0,8},{4,12},{8,0},{12,4},{1,9},{5,13},{9,1},{13,5},{2,10},{6,14},... | collective-permute-start | bytes 221192 | tf_op jit(solution)/shard_map/ppermute | solution.py:461
  29.9 4.5 %collective-permute-start.6 = (f32[72,256]{1,0:T(8,128)S(1)}, f32[72,256]{1,0:T(8,128)S(1)}, u32[]{:S(2)}, u32[]{:S(2)}) collective-permute-start(f32[72,256]{1,0:T(8,128)S(1)} %get-tuple-element.31), channel_id=1, source_target_pairs={{0,12},{4,8},{8,4},{12,0},{1,13},{5,9},{9,5},{13,1},{2,14},{6,10},... | collective-permute-start | bytes 221192 | tf_op jit(solution)/shard_map/ppermute | solution.py:461
  34.7 3.7 %collective-permute-start.7 = (f32[1,8,256]{2,1,0:T(8,128)S(1)}, f32[1,8,256]{2,1,0:T(8,128)S(1)}, u32[]{:S(2)}, u32[]{:S(2)}) collective-permute-start(f32[1,8,256]{2,1,0:T(8,128)S(1)} %get-tuple-element.32.own_small_ref), channel_id=1, source_target_pairs={{0,16},{16,0},{1,17},{17,1},{2,18},{18,2},{3,19},{19,3},{4,20},{20... | collective-permute-start | bytes 24584 | tf_op jit(solution)/shard_map/ppermute | solution.py:554

commit v11 on v10

--- a/solution.py
+++ b/solution.py
@@ -184,7 +184,7 @@
 
 
 def local_kernel(
-    pair, group, factors, sending,
+    pair, group, piece, factors, sending,
     tables_hbm, warmth_hbm, supply_hbm,
     swept_ref, warmth_ref, upward_ends_ref, north_ends_ref, east_ends_ref, *rest,
 ):
@@ -196,22 +196,20 @@
     count = east_ends_ref.shape[0]
     place = ordered(pair, east)
 
-    def fetch(which, g):
-        start = jnp.minimum(place(g * group), place(g * group + group - 1))
-        block = pl.ds(start, group)
+    def fetch(which, b):
+        start = jnp.minimum(place(b * piece), place(b * piece + piece - 1))
+        block = pl.ds(start, piece)
         if which == 0:
-            return pltpu.make_async_copy(warmth_hbm.at[block], warmth_ref.at[pl.ds(start + 1, group)], sems.at[0, g])
-        return pltpu.make_async_copy(supply_hbm.at[block], supply_ref.at[block], sems.at[1, g])
-
-    def begin(g):
+            return pltpu.make_async_copy(warmth_hbm.at[block], warmth_ref.at[pl.ds(start + 1, piece)], sems.at[0, b])
+        return pltpu.make_async_copy(supply_hbm.at[block], supply_ref.at[block], sems.at[1, b])
+
+    blocks = east // piece
+    tables = pltpu.make_async_copy(tables_hbm, tables_ref, sems.at[0, blocks])
+    for b in range(blocks):
         for which in range(2):
-            fetch(which, g).start()
-
-    ahead = 2
-    tables = pltpu.make_async_copy(tables_hbm, tables_ref, sems.at[0, groups])
-    tables.start()
-    for g in range(min(ahead, groups)):
-        begin(g)
+            fetch(which, b).start()
+        if b == 1:
+            tables.start()
     warmth_ref[0] = jnp.zeros((north, upward), F32)
     warmth_ref[east + 1] = jnp.zeros((north, upward), F32)
     both_ref[...] = jnp.zeros_like(both_ref)
@@ -219,22 +217,23 @@
     lane = lax.broadcasted_iota(jnp.int32, (1, 2 * east), 1)
     line = lax.broadcasted_iota(jnp.int32, (8, 1), 0)
     half_factor = 0.5 * factors[0]
-    tables.wait()
-    up_ref[...] = tables_ref[: 2 * upward].astype(BF16)
-    north_ref[...] = tables_ref[2 * upward : 2 * upward + 2 * north, : 2 * north].astype(BF16)
+    def settle_tables():
+        tables.wait()
+        up_ref[...] = tables_ref[: 2 * upward].astype(BF16)
+        north_ref[...] = tables_ref[2 * upward : 2 * upward + 2 * north, : 2 * north].astype(BF16)
     sweep = 2 * upward + 2 * north
     fetch(0, 0).wait()
 
+    def arrive_block(b):
+        fetch(1, b).wait()
+
+        @pl.when(b + 1 < blocks)
+        def _():
+            fetch(0, b + 1).wait()
+
     def arrive(g):
-        fetch(1, g).wait()
-
-        @pl.when(g + 1 < groups)
-        def _():
-            fetch(0, g + 1).wait()
-
-        @pl.when(g + ahead < groups)
-        def _():
-            begin(g + ahead)
+        for c in range(group // piece):
+            arrive_block(g * (group // piece) + c)
 
     def shifted(values, step):
         turned = pltpu.roll(values, step % north, 0)
@@ -242,9 +241,11 @@
             return jnp.concatenate([jnp.where(line == 0, 0.0, turned[:8]), turned[8:]], axis=0)
         return jnp.concatenate([turned[:-8], jnp.where(line == 7, 0.0, turned[-8:])], axis=0)
 
-    def upward_part(g, slot_ref):
+    def upward_part(g, slot_ref, first=False):
         heat_list = []
         for k in range(group):
+            if first and k % piece == 0:
+                arrive_block(k // piece)
             i = g * group + k
             x = place(i)
             warm = warmth_ref[x + 1]
@@ -253,6 +254,8 @@
             heat_list.append((supply_ref[x] + 2.0 * warm) + (factors[0] * bent + factors[1] * across))
             edges_ref[pl.ds(i, 1)] = warm[:1]
             edges_ref[pl.ds(east + i, 1)] = warm[north - 1 :]
+        if first:
+            settle_tables()
         slot_ref[...] = upward_dot(jnp.concatenate(heat_list, axis=0), up_ref)
 
     def north_part(g, slot_ref):
@@ -272,8 +275,7 @@
             if not pair:
                 east_ends_ref[0] += tables_ref[pl.ds(sweep + east + i, 1), :] * swept
 
-    arrive(0)
-    upward_part(0, even_ref)
+    upward_part(0, even_ref, first=True)
 
     def body(j, _):
         g = 2 * j
@@ -499,10 +501,10 @@
     def kept(*sizes):
         return jax.ShapeDtypeStruct(sizes, F32)
 
-    group = 8
+    group, piece = 8, 4
     folded = kept(north // 2 + 8, 2 * east)
     swept, warmth, upward_ends, north_ends, own, *messages = pl.pallas_call(
-        functools.partial(local_kernel, pair, group, factors, exchanges[2][0]),
+        functools.partial(local_kernel, pair, group, piece, factors, exchanges[2][0]),
         in_specs=[hbm] * 3,
         out_specs=[vmem] * (5 + to_up),
         out_shape=[
@@ -522,7 +524,7 @@
             pltpu.VMEM((2 * north, 2 * north), BF16),
             pltpu.VMEM((group * north, upward), F32),
             pltpu.VMEM((group * north, upward), F32),
-            pltpu.SemaphoreType.DMA((2, east // group + 1)),
+            pltpu.SemaphoreType.DMA((2, east // piece + 1)),
         ],
         compiler_params=pltpu.CompilerParams(vmem_limit_bytes=32 * MIB),
     )(pltpu.with_memory_space_constraint(jnp.asarray(tables), pltpu.HBM), initial_warmth, heat_supply)

time: 44.5 us -> 44.1 us (level)
  no operation moved by 1% of the time
where the time goes in v11:
time: 44.1 us; the launch traced here: 43.9 us
  Pallas kernels  21 us (48%)
  waiting for transfers between devices  12.9 us (29%)
  starting transfers between devices  9.92 us (22%)
    pallas_call x1, Pallas kernels, local(): pl.pallas_call(functools.partial(local_kernel, pair, group, piece, factor...  14.1 us
    ppermute x6, waiting for transfers between devices, spread_out(): lax.ppermute(messages[d], axis, [(k, peers(k, members, d + 1)[0]) for k i...  9.75 us
    ppermute x6, starting transfers between devices, spread_out(): lax.ppermute(messages[d], axis, [(k, peers(k, members, d + 1)[0]) for k i...  6.32 us
    pallas_call x1, Pallas kernels, local(): pl.pallas_call(functools.partial(final_kernel, pair, table, tile), in_spe...  5.9 us
    ppermute x1, waiting for transfers between devices, local(): other_small = lax.ppermute(own_small, 'gx', [(0, 1), (1, 0)])  3.17 us
    ppermute x1, starting transfers between devices, local(): other = lax.ppermute(own, 'gx', [(0, 1), (1, 0)])  3.06 us
  transfers between devices with their start and end apart: 8, of which 5 were waited for; matrix products, arithmetic and copies ran while one was open for 0% of the time, Pallas kernels for 2%

profile of v11, /device:TPU:0, one launch (start us, length us, event | category | flops | bytes accessed | tf_op | source)
XLA Modules:
  0.0 43.9 jit_solution(7904603999810778621)
XLA Ops:
  0.0 0.0 copy-start.1
  0.0 0.0 copy-start.2
  0.0 0.0 copy-start.3
  0.0 0.0 copy-start.4
  0.0 0.0 copy-start
  0.0 0.0 copy-start.5
  0.0 0.0 copy-start.6
  0.0 14.1 %shard_map.100 = (f32[64,128,256]{2,1,0:T(8,128)S(1)}, f32[66,128,256]{2,1,0:T(8,128)S(1)}, f32[2,72,128]{2,1,0:T(8,128)S(1)}, f32[2,72,256]{2,1,0:T(8,128)S(1)}...) custom-call(f32[904,256]{1,0:T(8,128)} %constant.16.clone.tables_hbm, ...), custom_call_target="tpu_custom_call" | custom-call | tf_op jit(solution)/shard_map/pallas_call | solution.py:506
  14.1 3.1 %collective-permute-start = (f32[1,128,256]{2,1,0:T(8,128)S(1)}, f32[1,128,256]{2,1,0:T(8,128)S(1)}, u32[]{:S(2)}, u32[]{:S(2)}) collective-permute-start(f32[1,128,256]{2,1,0:T(8,128)S(1)} %get-tuple-element.21.own_ref), channel_id=1, source_target_pairs={{0,16},{16,0},{1,17},{17,1},{2,18},{18,2},{3,19},{19,3},{4,20},{20... | collective-permute-start | bytes 393224 | tf_op jit(solution)/shard_map/ppermute | solution.py:534
  17.2 1.6 %collective-permute-start.1 = (f32[72,128]{1,0:T(8,128)S(1)}, f32[72,128]{1,0:T(8,128)S(1)}, u32[]{:S(2)}, u32[]{:S(2)}) collective-permute-start(f32[72,128]{1,0:T(8,128)S(1)} %get-tuple-element.24), channel_id=1, source_target_pairs={{0,1},{1,0},{2,3},{3,2},{4,5},{5,4},{6,7},{7,6},{8,9},{9,8},{10,11... | collective-permute-start | bytes 110600 | tf_op jit(solution)/shard_map/ppermute | solution.py:463
  18.8 2.6 %collective-permute-start.2 = (f32[72,128]{1,0:T(8,128)S(1)}, f32[72,128]{1,0:T(8,128)S(1)}, u32[]{:S(2)}, u32[]{:S(2)}) collective-permute-start(f32[72,128]{1,0:T(8,128)S(1)} %get-tuple-element.25), channel_id=1, source_target_pairs={{0,2},{1,3},{2,0},{3,1},{4,6},{5,7},{6,4},{7,5},{8,10},{9,11},{10,... | collective-permute-start | bytes 110600 | tf_op jit(solution)/shard_map/ppermute | solution.py:463
  21.4 0.2 collective-permute-start.3
  21.6 0.0 collective-permute-done.1.rest_0_
  21.6 2.4 %collective-permute-done.2.rest_1_ = f32[72,128]{1,0:T(8,128)S(1)} collective-permute-done((f32[72,128]{1,0:T(8,128)S(1)}, f32[72,128]{1,0:T(8,128)S(1)}, u32[]{:S(2)}, u32[]{:S(2)}) %collective-permute-start.2) | collective-permute-done | bytes 36896 | tf_op jit(solution)/shard_map/ppermute | solution.py:463
  24.0 3.1 %collective-permute-done.3.rest_2_ = f32[72,128]{1,0:T(8,128)S(1)} collective-permute-done((f32[72,128]{1,0:T(8,128)S(1)}, f32[72,128]{1,0:T(8,128)S(1)}, u32[]{:S(2)}, u32[]{:S(2)}) %collective-permute-start.3) | collective-permute-done | bytes 36896 | tf_op jit(solution)/shard_map/ppermute | solution.py:463
  27.1 0.0 copy-done.1
  27.1 0.0 copy-done.2
  27.1 0.0 copy-done.3
  27.1 0.7 %shard_map.101 = (f32[128,128]{1,0:T(8,128)S(1)}, f32[2,72,256]{2,1,0:T(8,128)S(1)}, f32[1,8,128]{2,1,0:T(8,128)S(1)}, f32[72,256]{1,0:T(8,128)S(1)}, f32[72,256]{1,0:T(8,128)S(1)}, /*index=5*/f32[72,256]{1,0:T(8,128)S(1)}) custom-call(f32[2,72,128]{2,1,0:T(8,128)S(1)} %get-tuple-element.22.ends_ref, f32[2,72,256]{2,1,0:T(8,128)S(1)} %get-tuple-element.23.north_ends_ref, ...), custom_call_target="tpu_custom_call" | custom-call | tf_op jit(solution)/shard_map/pallas_call | solution.py:537
  27.8 0.1 collective-permute-start.4
  27.9 1.5 %collective-permute-start.5 = (f32[72,256]{1,0:T(8,128)S(1)}, f32[72,256]{1,0:T(8,128)S(1)}, u32[]{:S(2)}, u32[]{:S(2)}) collective-permute-start(f32[72,256]{1,0:T(8,128)S(1)} %get-tuple-element.30), channel_id=1, source_target_pairs={{0,8},{4,12},{8,0},{12,4},{1,9},{5,13},{9,1},{13,5},{2,10},{6,14},... | collective-permute-start | bytes 221192 | tf_op jit(solution)/shard_map/ppermute | solution.py:463
  29.5 0.3 collective-permute-start.6
  29.8 0.0 collective-permute-done.4.rest_0_
  29.8 3.0 %collective-permute-done.5.rest_1_ = f32[72,256]{1,0:T(8,128)S(1)} collective-permute-done((f32[72,256]{1,0:T(8,128)S(1)}, f32[72,256]{1,0:T(8,128)S(1)}, u32[]{:S(2)}, u32[]{:S(2)}) %collective-permute-start.5) | collective-permute-done | bytes 73760 | tf_op jit(solution)/shard_map/ppermute | solution.py:463
  32.8 1.2 %collective-permute-done.6.rest_2_ = f32[72,256]{1,0:T(8,128)S(1)} collective-permute-done((f32[72,256]{1,0:T(8,128)S(1)}, f32[72,256]{1,0:T(8,128)S(1)}, u32[]{:S(2)}, u32[]{:S(2)}) %collective-permute-start.6) | collective-permute-done | bytes 73760 | tf_op jit(solution)/shard_map/ppermute | solution.py:463
  34.0 0.0 copy-done.4
  34.0 0.3 shard_map.102
  34.3 0.5 %collective-permute-start.7 = (f32[1,8,256]{2,1,0:T(8,128)S(1)}, f32[1,8,256]{2,1,0:T(8,128)S(1)}, u32[]{:S(2)}, u32[]{:S(2)}) collective-permute-start(f32[1,8,256]{2,1,0:T(8,128)S(1)} %get-tuple-element.32.own_small_ref), channel_id=1, source_target_pairs={{0,16},{16,0},{1,17},{17,1},{2,18},{18,2},{3,19},{19,3},{4,20},{20... | collective-permute-start | bytes 24584 | tf_op jit(solution)/shard_map/ppermute | solution.py:556
  34.9 3.2 %collective-permute-done.7.other_small_ref = f32[1,8,256]{2,1,0:T(8,128)S(1)} collective-permute-done((f32[1,8,256]{2,1,0:T(8,128)S(1)}, f32[1,8,256]{2,1,0:T(8,128)S(1)}, u32[]{:S(2)}, u32[]{:S(2)}) %collective-permute-start.7) | collective-permute-done | bytes 8224 | tf_op jit(solution)/shard_map/ppermute | solution.py:556
  38.0 0.0 collective-permute-done.other_ref
  38.0 0.0 copy-done
  38.0 0.0 copy-done.5
  38.0 0.0 copy-done.6
  38.0 5.9 %shard_map.103 = f32[64,128,256]{2,1,0:T(8,128)} custom-call(f32[3,64]{1,0:T(4,128)S(1)} %copy-done.6, f32[1,128,256]{2,1,0:T(8,128)S(1)} %get-tuple-element.21.own_ref, f32[1,128,256]{2,1,0:T(8,128)S(1)} %collective-permute-done.other_ref, f32[1,8,256]{2,1,0:T(8,128)S(1)} %get-tuple-element.32.own_small_ref, ...), custom_call_target="tpu_custom_call" | custom-call | tf_op jit(solution)/shard_map/pallas_call | solution.py:565
Async XLA Ops:
  0.0 27.1 %copy-start.1 = (f32[128,256]{1,0:T(8,128)S(1)}, f32[128,256]{1,0:T(8,128)}, u32[]{:S(2)}) copy-start(f32[128,256]{1,0:T(8,128)} %constant.19.clone.spread_ref) | copy-start | bytes 393220
  0.0 27.1 %copy-start.2 = (f32[128,128]{1,0:T(8,128)S(1)}, f32[128,128]{1,0:T(8,128)}, u32[]{:S(2)}) copy-start(f32[128,128]{1,0:T(8,128)} %constant.18.clone.east_twice_ref) | copy-start | bytes 196612
  0.0 27.1 %copy-start.3 = (f32[128,128]{1,0:T(8,128)S(1)}, f32[128,128]{1,0:T(8,128)}, u32[]{:S(2)}) copy-start(f32[128,128]{1,0:T(8,128)} %constant.17.clone.north_inverse_ref) | copy-start | bytes 196612
  0.0 34.0 %copy-start.4 = (f32[64,64]{1,0:T(8,128)S(1)}, f32[64,64]{1,0:T(8,128)}, u32[]{:S(2)}) copy-start(f32[64,64]{1,0:T(8,128)} %constant.20.clone.east_inverse_ref) | copy-start | bytes 49156
  0.0 38.0 %copy-start = (f32[2,128,256]{2,1,0:T(8,128)S(1)}, f32[2,128,256]{2,1,0:T(8,128)}, u32[]{:S(2)}) copy-start(f32[2,128,256]{2,1,0:T(8,128)} %constant.23.clone.north_spikes_ref) | copy-start | bytes 786436
  0.0 38.0 %copy-start.5 = (f32[2,256]{1,0:T(2,128)S(1)}, f32[2,256]{1,0:T(2,128)}, u32[]{:S(2)}) copy-start(f32[2,256]{1,0:T(2,128)} %constant.22.clone.upward_spikes_ref) | copy-start | bytes 6148
  0.0 38.0 %copy-start.6 = (f32[3,64]{1,0:T(4,128)S(1)}, f32[3,64]{1,0:T(4,128)}, u32[]{:S(2)}) copy-start(f32[3,64]{1,0:T(4,128)} %constant.21.clone.sweep_ref) | copy-start | bytes 2308
  14.1 23.9 %collective-permute-start = (f32[1,128,256]{2,1,0:T(8,128)S(1)}, f32[1,128,256]{2,1,0:T(8,128)S(1)}, u32[]{:S(2)}, u32[]{:S(2)}) collective-permute-start(f32[1,128,256]{2,1,0:T(8,128)S(1)} %get-tuple-element.21.own_ref), channel_id=1, source_target_pairs={{0,16},{16,0},{1,17},{17,1},{2,18},{18,2},{3,19},{19,3},{4,20},{20... | collective-permute-start | bytes 393224 | tf_op jit(solution)/shard_map/ppermute | solution.py:534
  17.2 4.4 %collective-permute-start.1 = (f32[72,128]{1,0:T(8,128)S(1)}, f32[72,128]{1,0:T(8,128)S(1)}, u32[]{:S(2)}, u32[]{:S(2)}) collective-permute-start(f32[72,128]{1,0:T(8,128)S(1)} %get-tuple-element.24), channel_id=1, source_target_pairs={{0,1},{1,0},{2,3},{3,2},{4,5},{5,4},{6,7},{7,6},{8,9},{9,8},{10,11... | collective-permute-start | bytes 110600 | tf_op jit(solution)/shard_map/ppermute | solution.py:463
  18.8 5.3 %collective-permute-start.2 = (f32[72,128]{1,0:T(8,128)S(1)}, f32[72,128]{1,0:T(8,128)S(1)}, u32[]{:S(2)}, u32[]{:S(2)}) collective-permute-start(f32[72,128]{1,0:T(8,128)S(1)} %get-tuple-element.25), channel_id=1, source_target_pairs={{0,2},{1,3},{2,0},{3,1},{4,6},{5,7},{6,4},{7,5},{8,10},{9,11},{10,... | collective-permute-start | bytes 110600 | tf_op jit(solution)/shard_map/ppermute | solution.py:463
  21.4 5.8 %collective-permute-start.3 = (f32[72,128]{1,0:T(8,128)S(1)}, f32[72,128]{1,0:T(8,128)S(1)}, u32[]{:S(2)}, u32[]{:S(2)}) collective-permute-start(f32[72,128]{1,0:T(8,128)S(1)} %get-tuple-element.26), channel_id=1, source_target_pairs={{0,3},{1,2},{2,1},{3,0},{4,7},{5,6},{6,5},{7,4},{8,11},{9,10},{10,... | collective-permute-start | bytes 110600 | tf_op jit(solution)/shard_map/ppermute | solution.py:463
  27.8 1.9 %collective-permute-start.4 = (f32[72,256]{1,0:T(8,128)S(1)}, f32[72,256]{1,0:T(8,128)S(1)}, u32[]{:S(2)}, u32[]{:S(2)}) collective-permute-start(f32[72,256]{1,0:T(8,128)S(1)} %get-tuple-element.29), channel_id=1, source_target_pairs={{0,4},{4,0},{8,12},{12,8},{1,5},{5,1},{9,13},{13,9},{2,6},{6,2},{1... | collective-permute-start | bytes 221192 | tf_op jit(solution)/shard_map/ppermute | solution.py:463
  27.9 4.8 %collective-permute-start.5 = (f32[72,256]{1,0:T(8,128)S(1)}, f32[72,256]{1,0:T(8,128)S(1)}, u32[]{:S(2)}, u32[]{:S(2)}) collective-permute-start(f32[72,256]{1,0:T(8,128)S(1)} %get-tuple-element.30), channel_id=1, source_target_pairs={{0,8},{4,12},{8,0},{12,4},{1,9},{5,13},{9,1},{13,5},{2,10},{6,14},... | collective-permute-start | bytes 221192 | tf_op jit(solution)/shard_map/ppermute | solution.py:463
  29.5 4.5 %collective-permute-start.6 = (f32[72,256]{1,0:T(8,128)S(1)}, f32[72,256]{1,0:T(8,128)S(1)}, u32[]{:S(2)}, u32[]{:S(2)}) collective-permute-start(f32[72,256]{1,0:T(8,128)S(1)} %get-tuple-element.31), channel_id=1, source_target_pairs={{0,12},{4,8},{8,4},{12,0},{1,13},{5,9},{9,5},{13,1},{2,14},{6,10},... | collective-permute-start | bytes 221192 | tf_op jit(solution)/shard_map/ppermute | solution.py:463
  34.3 3.7 %collective-permute-start.7 = (f32[1,8,256]{2,1,0:T(8,128)S(1)}, f32[1,8,256]{2,1,0:T(8,128)S(1)}, u32[]{:S(2)}, u32[]{:S(2)}) collective-permute-start(f32[1,8,256]{2,1,0:T(8,128)S(1)} %get-tuple-element.32.own_small_ref), channel_id=1, source_target_pairs={{0,16},{16,0},{1,17},{17,1},{2,18},{18,2},{3,19},{19,3},{4,20},{20... | collective-permute-start | bytes 24584 | tf_op jit(solution)/shard_map/ppermute | solution.py:556
